TPU v7x, 512 devices: a whole 4x4x16 slice. The times are simulated.
512 devices in a mesh: sess: 128 (over x, y, z_lo, core), blk: 4 (over z_hi).
Axes of the slice: x: 4, y: 4, z: 16 (z_hi: 4, z_lo: 4; z = z_hi * 4 + z_lo), core: 2. Of those that a mesh axis runs over, the one named last changes fastest.
Arguments:
- queries: bfloat16 [128, 64, 8192], P('sess', 'blk'), may hold values from -132 to 132
- res_cache: bfloat16 [2, 128, 1024, 1024], P(None, 'sess', 'blk'), may hold values from -6 to 6
- mig_cache: bfloat16 [2, 128, 1024, 1024], P(None, 'sess', 'blk'), may hold values from -6 to 6
- res_ids: int32 [128, 4], P('sess', 'blk'), may hold values from 0 to 3, as said below
- recv_ids: int32 [128, 4], P('sess', 'blk'), may hold values from 4 to 7, as said below
- lengths: int32 [128], P('sess'), may hold values from 320 to 2048
Outputs:
- attended: bfloat16 [128, 64, 8192], P('sess', 'blk')
Inputs may be any that keep to these rules, and one draw needn't show every extreme that they name: In each session the ids of res_ids and recv_ids together are 0 to 7, each once; the first resident slots of the 4 loop members hold blocks 0 to 3 in some order. `recv_ids`: see res_ids.
All inputs are finite; a program needn't handle non-finite values.
Results may differ from a plain program's by a relative error of at most 0.01.
Values may be sent and summed in bfloat16 or wider, within the bound.
No kernel may reach another device: no remote copies, remote signals or barrier semaphores. Data moves between devices by JAX's collectives and lax.ppermute only.
A program may use at most 64 MiB of HBM per device.

v0:
```python
import math

import jax
import jax.numpy as jnp
from jax import lax
from jax.sharding import PartitionSpec as P

HEADS = 64
KV_HEADS = 8
HEAD = 128
BLOCK = 256
QROWS = 64


def from_behind(value, axis, steps):
    count = lax.axis_size(axis)
    pairs = [(source, (source + steps) % count) for source in range(count)]
    return lax.ppermute(value, axis, pairs)


def attend_part(queries, row_pos, key_rows, value_rows, key_pos):
    group_size = HEADS // KV_HEADS
    row_count = queries.shape[0]
    scaling = 1.0 / math.sqrt(HEAD)
    query_four = queries.reshape(row_count, KV_HEADS, group_size, HEAD)
    key_three = key_rows.reshape(-1, KV_HEADS, HEAD)
    value_three = value_rows.reshape(-1, KV_HEADS, HEAD)
    scores = (
        jnp.einsum("rgjd,kgd->rgjk", query_four, key_three, preferred_element_type=jnp.float32)
        * scaling
    )
    allowed = (key_pos[None, :] <= row_pos[:, None])[:, None, None, :]
    row_max = jnp.max(jnp.where(allowed, scores, -1e30), axis=-1)
    weights = jnp.where(allowed, jnp.exp(scores - row_max[..., None]), 0.0).astype(jnp.bfloat16)
    totals = jnp.sum(weights, axis=-1, dtype=jnp.float32)
    mixed_sum = jnp.einsum(
        "rgjk,kgd->rgjd", weights, value_three, preferred_element_type=jnp.float32
    )
    return (
        mixed_sum.reshape(row_count, HEADS * HEAD),
        row_max.reshape(row_count, HEADS),
        totals.reshape(row_count, HEADS),
    )


def combine(earlier, later):
    row_count = earlier[0].shape[0]
    joined_max = jnp.maximum(earlier[1], later[1])
    scale_one = jnp.exp(earlier[1] - joined_max)
    scale_two = jnp.exp(later[1] - joined_max)
    joined = (
        earlier[0].reshape(row_count, HEADS, HEAD) * scale_one[..., None]
        + later[0].reshape(row_count, HEADS, HEAD) * scale_two[..., None]
    )
    return (
        joined.reshape(row_count, HEADS * HEAD),
        joined_max,
        earlier[2] * scale_one + later[2] * scale_two,
    )


def attend_groups(queries, row_pos, groups):
    result = attend_part(queries, row_pos, groups[0][0], groups[0][1], groups[0][2])
    for key_group in groups[1:]:
        result = combine(
            result, attend_part(queries, row_pos, key_group[0], key_group[1], key_group[2])
        )
    return result


def positions(block_ids):
    offsets = jnp.arange(BLOCK, dtype=jnp.int32)
    return (block_ids[:, None] * BLOCK + offsets[None, :]).reshape(-1)


def finish(merged):
    row_count = merged[0].shape[0]
    scaled = merged[0].reshape(row_count, HEADS, HEAD) / merged[2][..., None]
    return scaled.reshape(row_count, HEADS * HEAD).astype(jnp.bfloat16)


def per_device(queries, res_cache, mig_cache, res_ids, recv_ids, lengths):
    loop_size = lax.axis_size("blk")
    member = lax.axis_index("blk")
    half_way = lax.axis_size("sess") // 2
    home_rows = queries[0]
    row_count = home_rows.shape[0]
    home_groups = [(res_cache[0, 0], res_cache[1, 0], positions(res_ids[0]))]
    arrived_blocks = from_behind(mig_cache, "sess", half_way)
    home_groups.append((arrived_blocks[0, 0], arrived_blocks[1, 0], positions(recv_ids[0])))
    query_sets = (home_rows,)
    length_sets = lengths[0]
    moving = query_sets
    flat_states = ()
    for hop_index in range(loop_size):
        if hop_index > 0:
            moving = from_behind((moving[0],), "blk", 1)
        anchor = (member - hop_index) % loop_size
        updated = ()
        row_pos = length_sets - QROWS + anchor * row_count + jnp.arange(row_count, dtype=jnp.int32)
        partial_out = attend_groups(moving[0], row_pos, home_groups)
        if hop_index > 0:
            partial_out = combine(flat_states[0:3], partial_out)
        updated = updated + partial_out
        flat_states = from_behind(updated, "blk", 1)
    states = flat_states[0:3]
    return finish(states)[None]


def solution(mesh):
    placed = (
        P("sess", "blk", None),
        P(None, "sess", "blk", None),
        P(None, "sess", "blk", None),
        P("sess", "blk"),
        P("sess", "blk"),
        P("sess"),
    )
    return jax.shard_map(
        per_device, mesh=mesh, in_specs=placed, out_specs=P("sess", "blk", None), check_vma=False
    )
```

profile of v0, /device:TPU:24, one launch (start us, length us, event | category | flops | bytes accessed | tf_op | source)
XLA Modules:
  0.0 317.5 jit_solution(7446523244855811521)
XLA Ops:
  0.0 2.4 copy.148
  2.4 4.9 %collective-permute-start = (bf16[2,1,256,1024]{2,3,1,0:T(8,128)(2,1)}, bf16[2,1,256,1024]{2,3,1,0:T(8,128)(2,1)}, u32[]{:S(2)}, u32[]{:S(2)}) collective-permute-start(bf16[2,1,256,1024]{2,3,1,0:T(8,128)(2,1)} %copy.148), channel_id=1, source_target_pairs={{0,256},{4,260},{8,264},{12,268},{16,272},{20,276},{24,280},{28,28... | collective-permute-start | bytes 3145736 | tf_op jit(solution)/shard_map/ppermute | solution.py:18
  7.3 9.1 %collective-permute-start.3 = (bf16[16,8192]{1,0:T(8,128)(2,1)S(1)}, bf16[16,8192]{1,0:T(8,128)(2,1)S(1)}, u32[]{:S(2)}, u32[]{:S(2)}) collective-permute-start(bf16[16,8192]{1,0:T(8,128)(2,1)S(1)} %bitcast.269), channel_id=1, source_target_pairs={{0,1},{1,2},{2,3},{3,0},{4,5},{5,6},{6,7},{7,4},{8,9},{9,10},{10,1... | collective-permute-start | bytes 786440 | tf_op jit(solution)/shard_map/ppermute | solution.py:18
  21.8 7.5 %collective-permute-done.3 = bf16[16,8192]{1,0:T(8,128)(2,1)S(1)} collective-permute-done((bf16[16,8192]{1,0:T(8,128)(2,1)S(1)}, bf16[16,8192]{1,0:T(8,128)(2,1)S(1)}, u32[]{:S(2)}, u32[]{:S(2)}) %collective-permute-start.3) | collective-permute-done | bytes 262176 | tf_op jit(solution)/shard_map/ppermute | solution.py:18
  29.4 18.2 %collective-permute-start.6 = (bf16[16,8192]{1,0:T(8,128)(2,1)S(1)}, bf16[16,8192]{1,0:T(8,128)(2,1)S(1)}, u32[]{:S(2)}, u32[]{:S(2)}) collective-permute-start(bf16[16,8192]{1,0:T(8,128)(2,1)S(1)} %collective-permute-done.3), channel_id=1, source_target_pairs={{0,1},{1,2},{2,3},{3,0},{4,5},{5,6},{6,7},{7,4},{8,9},{9,10},{10,1... | collective-permute-start | bytes 786440 | tf_op jit(solution)/shard_map/ppermute | solution.py:18
  48.1 39.1 %collective-permute-done.6 = bf16[16,8192]{1,0:T(8,128)(2,1)S(1)} collective-permute-done((bf16[16,8192]{1,0:T(8,128)(2,1)S(1)}, bf16[16,8192]{1,0:T(8,128)(2,1)S(1)}, u32[]{:S(2)}, u32[]{:S(2)}) %collective-permute-start.6) | collective-permute-done | bytes 262176 | tf_op jit(solution)/shard_map/ppermute | solution.py:18
  87.2 8.3 %collective-permute-start.9 = (bf16[16,8192]{1,0:T(8,128)(2,1)S(1)}, bf16[16,8192]{1,0:T(8,128)(2,1)S(1)}, u32[]{:S(2)}, u32[]{:S(2)}) collective-permute-start(bf16[16,8192]{1,0:T(8,128)(2,1)S(1)} %collective-permute-done.6), channel_id=1, source_target_pairs={{0,1},{1,2},{2,3},{3,0},{4,5},{5,6},{6,7},{7,4},{8,9},{9,10},{10,1... | collective-permute-start | bytes 786440 | tf_op jit(solution)/shard_map/ppermute | solution.py:18
  96.9 38.3 %collective-permute-done.9 = bf16[16,8192]{1,0:T(8,128)(2,1)S(1)} collective-permute-done((bf16[16,8192]{1,0:T(8,128)(2,1)S(1)}, bf16[16,8192]{1,0:T(8,128)(2,1)S(1)}, u32[]{:S(2)}, u32[]{:S(2)}) %collective-permute-start.9) | collective-permute-done | bytes 262176 | tf_op jit(solution)/shard_map/ppermute | solution.py:18
  148.1 1.9 fusion.15
  150.1 8.5 %collective-permute-start.1 = (f32[16,8192]{1,0:T(8,128)}, f32[16,8192]{1,0:T(8,128)}, u32[]{:S(2)}, u32[]{:S(2)}) collective-permute-start(f32[16,8192]{1,0:T(8,128)} %fusion.15), channel_id=1, source_target_pairs={{0,1},{1,2},{2,3},{3,0},{4,5},{5,6},{6,7},{7,4},{8,9},{9,10},{10,1... | collective-permute-start | bytes 1572872 | tf_op jit(solution)/shard_map/ppermute | solution.py:18
  158.5 1.9 collective-permute-start.11
  160.4 2.1 collective-permute-start.2
  173.6 56.3 %collective-permute-done.11 = f32[16,64]{1,0:T(8,128)} collective-permute-done((f32[16,64]{1,0:T(8,128)}, f32[16,64]{1,0:T(8,128)}, u32[]{:S(2)}, u32[]{:S(2)}) %collective-permute-start.11) | collective-permute-done | bytes 4128 | tf_op jit(solution)/shard_map/ppermute | solution.py:18
  231.5 4.0 %fusion.13 = f32[16,8192]{1,0:T(8,128)} fusion(f32[2,8,64,128]{3,2,1,0:T(8,128)S(1)} %bitcast.258, f32[2,8,64,128]{3,2,1,0:T(8,128)S(1)} %bitcast.255, f32[2,8,64,128]{3,2,1,0:T(8,128)S(1)} %bitcast.243, f32[2,8,64,128]{3,2,1,0:T(8,128)S(1)} %bitcast.252, f32[2,8,64,128]{3,2,1,0:T(8,128)S(1)} %bitcast.245, f32[16,8192]{1,0:T(8,128)} %collective-permute-done.1, ...), kind=kLoop, calls=%fused_computation.63 | loop fusion | flops 786432 | bytes 4194304 | tf_op jit(solution)/shard_map/add | solution.py:52
  235.6 2.2 collective-permute-start.4
  240.8 7.0 %collective-permute-start.5 = (f32[16,64]{1,0:T(8,128)S(1)}, f32[16,64]{1,0:T(8,128)S(1)}, u32[]{:S(2)}, u32[]{:S(2)}) collective-permute-start(f32[16,64]{1,0:T(8,128)S(1)} %get-tuple-element.21), channel_id=1, source_target_pairs={{0,1},{1,2},{2,3},{3,0},{4,5},{5,6},{6,7},{7,4},{8,9},{9,10},{10,1... | collective-permute-start | bytes 12296 | tf_op jit(solution)/shard_map/ppermute | solution.py:18
  250.3 27.2 %collective-permute-done.12 = f32[16,64]{1,0:T(8,128)S(1)} collective-permute-done((f32[16,64]{1,0:T(8,128)S(1)}, f32[16,64]{1,0:T(8,128)S(1)}, u32[]{:S(2)}, u32[]{:S(2)}) %collective-permute-start.12) | collective-permute-done | bytes 4128 | tf_op jit(solution)/shard_map/ppermute | solution.py:18
  278.4 4.0 %fusion.11 = f32[16,8192]{1,0:T(8,128)} fusion(f32[2,8,64,128]{3,2,1,0:T(8,128)S(1)} %bitcast.259, f32[2,8,64,128]{3,2,1,0:T(8,128)S(1)} %bitcast.256, f32[2,8,64,128]{3,2,1,0:T(8,128)S(1)} %bitcast.244, f32[2,8,64,128]{3,2,1,0:T(8,128)S(1)} %bitcast.253, f32[2,8,64,128]{3,2,1,0:T(8,128)S(1)} %bitcast.246, f32[16,8192]{1,0:T(8,128)} %collective-permute-done.4, ...), kind=kLoop, calls=%fused_computation.57 | loop fusion | flops 786432 | bytes 4194304 | tf_op jit(solution)/shard_map/add | solution.py:52
  284.7 1.9 collective-permute-start.13
  286.6 7.6 %collective-permute-start.8 = (f32[16,64]{1,0:T(8,128)S(1)}, f32[16,64]{1,0:T(8,128)S(1)}, u32[]{:S(2)}, u32[]{:S(2)}) collective-permute-start(f32[16,64]{1,0:T(8,128)S(1)} %get-tuple-element.15), channel_id=1, source_target_pairs={{0,1},{1,2},{2,3},{3,0},{4,5},{5,6},{6,7},{7,4},{8,9},{9,10},{10,1... | collective-permute-start | bytes 12296 | tf_op jit(solution)/shard_map/ppermute | solution.py:18
  294.9 2.9 collective-permute-done.13
  298.6 2.2 fusion.9
  300.8 6.0 %collective-permute-start.10 = (f32[16,8192]{1,0:T(8,128)S(1)}, f32[16,8192]{1,0:T(8,128)S(1)}, u32[]{:S(2)}, u32[]{:S(2)}) collective-permute-start(f32[16,8192]{1,0:T(8,128)S(1)} %fusion.9), channel_id=1, source_target_pairs={{0,1},{1,2},{2,3},{3,0},{4,5},{5,6},{6,7},{7,4},{8,9},{9,10},{10,1... | collective-permute-start | bytes 1572872 | tf_op jit(solution)/shard_map/ppermute | solution.py:18
  306.8 8.1 %collective-permute-start.14 = (f32[16,64]{1,0:T(8,128)S(1)}, f32[16,64]{1,0:T(8,128)S(1)}, u32[]{:S(2)}, u32[]{:S(2)}) collective-permute-start(f32[16,64]{1,0:T(8,128)S(1)} %get-tuple-element.5), channel_id=1, source_target_pairs={{0,1},{1,2},{2,3},{3,0},{4,5},{5,6},{6,7},{7,4},{8,9},{9,10},{10,1... | collective-permute-start | bytes 12296 | tf_op jit(solution)/shard_map/ppermute | solution.py:18
  (166 shorter events, 43.1 us)
Async XLA Ops:
  0.0 7.3 %copy-start.9 = (bf16[1,16,8192]{2,1,0:T(8,128)(2,1)S(1)}, bf16[1,16,8192]{2,1,0:T(8,128)(2,1)}, u32[]{:S(2)}) copy-start(bf16[1,16,8192]{2,1,0:T(8,128)(2,1)} %param.6) | copy-start | bytes 786436
  0.0 18.6 %copy-start.6 = (bf16[2,1,256,1024]{3,2,1,0:T(8,128)(2,1)S(1)}, bf16[2,1,256,1024]{3,2,1,0:T(8,128)(2,1)}, u32[]{:S(2)}) copy-start(bf16[2,1,256,1024]{3,2,1,0:T(8,128)(2,1)} %param.7) | copy-start | bytes 3145732
  2.4 135.5 %collective-permute-start = (bf16[2,1,256,1024]{2,3,1,0:T(8,128)(2,1)}, bf16[2,1,256,1024]{2,3,1,0:T(8,128)(2,1)}, u32[]{:S(2)}, u32[]{:S(2)}) collective-permute-start(bf16[2,1,256,1024]{2,3,1,0:T(8,128)(2,1)} %copy.148), channel_id=1, source_target_pairs={{0,256},{4,260},{8,264},{12,268},{16,272},{20,276},{24,280},{28,28... | collective-permute-start | bytes 3145736 | tf_op jit(solution)/shard_map/ppermute | solution.py:18
  7.3 22.0 %collective-permute-start.3 = (bf16[16,8192]{1,0:T(8,128)(2,1)S(1)}, bf16[16,8192]{1,0:T(8,128)(2,1)S(1)}, u32[]{:S(2)}, u32[]{:S(2)}) collective-permute-start(bf16[16,8192]{1,0:T(8,128)(2,1)S(1)} %bitcast.269), channel_id=1, source_target_pairs={{0,1},{1,2},{2,3},{3,0},{4,5},{5,6},{6,7},{7,4},{8,9},{9,10},{10,1... | collective-permute-start | bytes 786440 | tf_op jit(solution)/shard_map/ppermute | solution.py:18
  19.6 28.0 %copy-start.33 = (pred[16,256]{1,0:T(8,128)(4,1)}, pred[16,256]{1,0:T(8,128)(4,1)S(1)}, u32[]{:S(2)}) copy-start(pred[16,256]{1,0:T(8,128)(4,1)S(1)} %get-tuple-element.54) | copy-start | bytes 12292
  19.6 76.0 %copy-start.29 = (pred[16,256]{1,0:T(8,128)(4,1)}, pred[16,256]{1,0:T(8,128)(4,1)S(1)}, u32[]{:S(2)}) copy-start(pred[16,256]{1,0:T(8,128)(4,1)S(1)} %get-tuple-element.53) | copy-start | bytes 12292
  29.4 18.6 %copy-start.10 = (bf16[2,8,64,128]{3,2,1,0:T(8,128)(2,1)}, bf16[2,8,64,128]{3,2,1,0:T(8,128)(2,1)S(1)}, u32[]{:S(2)}) copy-start(bf16[2,8,64,128]{3,2,1,0:T(8,128)(2,1)S(1)} %copy.263) | copy-start | bytes 786436
  29.4 57.8 %collective-permute-start.6 = (bf16[16,8192]{1,0:T(8,128)(2,1)S(1)}, bf16[16,8192]{1,0:T(8,128)(2,1)S(1)}, u32[]{:S(2)}, u32[]{:S(2)}) collective-permute-start(bf16[16,8192]{1,0:T(8,128)(2,1)S(1)} %collective-permute-done.3), channel_id=1, source_target_pairs={{0,1},{1,2},{2,3},{3,0},{4,5},{5,6},{6,7},{7,4},{8,9},{9,10},{10,1... | collective-permute-start | bytes 786440 | tf_op jit(solution)/shard_map/ppermute | solution.py:18
  87.2 47.9 %collective-permute-start.9 = (bf16[16,8192]{1,0:T(8,128)(2,1)S(1)}, bf16[16,8192]{1,0:T(8,128)(2,1)S(1)}, u32[]{:S(2)}, u32[]{:S(2)}) collective-permute-start(bf16[16,8192]{1,0:T(8,128)(2,1)S(1)} %collective-permute-done.6), channel_id=1, source_target_pairs={{0,1},{1,2},{2,3},{3,0},{4,5},{5,6},{6,7},{7,4},{8,9},{9,10},{10,1... | collective-permute-start | bytes 786440 | tf_op jit(solution)/shard_map/ppermute | solution.py:18
  148.1 14.5 %copy-start.8 = (bf16[1,1,256,1024]{2,3,1,0:T(8,128)(2,1)S(1)}, bf16[1,1,256,1024]{2,3,1,0:T(8,128)(2,1)}, u32[]{:S(2)}) copy-start(bf16[1,1,256,1024]{2,3,1,0:T(8,128)(2,1)} %copy-done.7) | copy-start | bytes 1572868
  148.1 14.5 %copy-start.11 = (bf16[2,8,64,128]{3,2,1,0:T(8,128)(2,1)S(1)}, bf16[2,8,64,128]{3,2,1,0:T(8,128)(2,1)}, u32[]{:S(2)}) copy-start(bf16[2,8,64,128]{3,2,1,0:T(8,128)(2,1)} %copy-done.10) | copy-start | bytes 786436
  150.0 12.5 %copy-start.32 = (pred[16,256]{1,0:T(8,128)(4,1)S(1)}, pred[16,256]{1,0:T(8,128)(4,1)}, u32[]{:S(2)}) copy-start(pred[16,256]{1,0:T(8,128)(4,1)} %get-tuple-element.51) | copy-start | bytes 12292
  150.1 80.7 %collective-permute-start.1 = (f32[16,8192]{1,0:T(8,128)}, f32[16,8192]{1,0:T(8,128)}, u32[]{:S(2)}, u32[]{:S(2)}) collective-permute-start(f32[16,8192]{1,0:T(8,128)} %fusion.15), channel_id=1, source_target_pairs={{0,1},{1,2},{2,3},{3,0},{4,5},{5,6},{6,7},{7,4},{8,9},{9,10},{10,1... | collective-permute-start | bytes 1572872 | tf_op jit(solution)/shard_map/ppermute | solution.py:18
  158.5 71.3 %collective-permute-start.11 = (f32[16,64]{1,0:T(8,128)}, f32[16,64]{1,0:T(8,128)}, u32[]{:S(2)}, u32[]{:S(2)}) collective-permute-start(f32[16,64]{1,0:T(8,128)} %get-tuple-element.22), channel_id=1, source_target_pairs={{0,1},{1,2},{2,3},{3,0},{4,5},{5,6},{6,7},{7,4},{8,9},{9,10},{10,1... | collective-permute-start | bytes 12296 | tf_op jit(solution)/shard_map/ppermute | solution.py:18
  160.4 69.5 %collective-permute-start.2 = (f32[16,64]{1,0:T(8,128)}, f32[16,64]{1,0:T(8,128)}, u32[]{:S(2)}, u32[]{:S(2)}) collective-permute-start(f32[16,64]{1,0:T(8,128)} %get-tuple-element.25), channel_id=1, source_target_pairs={{0,1},{1,2},{2,3},{3,0},{4,5},{5,6},{6,7},{7,4},{8,9},{9,10},{10,1... | collective-permute-start | bytes 12296 | tf_op jit(solution)/shard_map/ppermute | solution.py:18
  235.6 42.0 %collective-permute-start.4 = (f32[16,8192]{1,0:T(8,128)}, f32[16,8192]{1,0:T(8,128)}, u32[]{:S(2)}, u32[]{:S(2)}) collective-permute-start(f32[16,8192]{1,0:T(8,128)} %fusion.13), channel_id=1, source_target_pairs={{0,1},{1,2},{2,3},{3,0},{4,5},{5,6},{6,7},{7,4},{8,9},{9,10},{10,1... | collective-permute-start | bytes 1572872 | tf_op jit(solution)/shard_map/ppermute | solution.py:18
  238.9 38.6 %collective-permute-start.12 = (f32[16,64]{1,0:T(8,128)S(1)}, f32[16,64]{1,0:T(8,128)S(1)}, u32[]{:S(2)}, u32[]{:S(2)}) collective-permute-start(f32[16,64]{1,0:T(8,128)S(1)} %get-tuple-element.16), channel_id=1, source_target_pairs={{0,1},{1,2},{2,3},{3,0},{4,5},{5,6},{6,7},{7,4},{8,9},{9,10},{10,1... | collective-permute-start | bytes 12296 | tf_op jit(solution)/shard_map/ppermute | solution.py:18
  240.8 36.7 %collective-permute-start.5 = (f32[16,64]{1,0:T(8,128)S(1)}, f32[16,64]{1,0:T(8,128)S(1)}, u32[]{:S(2)}, u32[]{:S(2)}) collective-permute-start(f32[16,64]{1,0:T(8,128)S(1)} %get-tuple-element.21), channel_id=1, source_target_pairs={{0,1},{1,2},{2,3},{3,0},{4,5},{5,6},{6,7},{7,4},{8,9},{9,10},{10,1... | collective-permute-start | bytes 12296 | tf_op jit(solution)/shard_map/ppermute | solution.py:18
  282.4 15.4 %collective-permute-start.7 = (f32[16,8192]{1,0:T(8,128)}, f32[16,8192]{1,0:T(8,128)S(1)}, u32[]{:S(2)}, u32[]{:S(2)}) collective-permute-start(f32[16,8192]{1,0:T(8,128)} %fusion.11), channel_id=1, source_target_pairs={{0,1},{1,2},{2,3},{3,0},{4,5},{5,6},{6,7},{7,4},{8,9},{9,10},{10,1... | collective-permute-start | bytes 1572872 | tf_op jit(solution)/shard_map/ppermute | solution.py:18
  284.7 13.0 %collective-permute-start.13 = (f32[16,64]{1,0:T(8,128)S(1)}, f32[16,64]{1,0:T(8,128)S(1)}, u32[]{:S(2)}, u32[]{:S(2)}) collective-permute-start(f32[16,64]{1,0:T(8,128)S(1)} %get-tuple-element.10), channel_id=1, source_target_pairs={{0,1},{1,2},{2,3},{3,0},{4,5},{5,6},{6,7},{7,4},{8,9},{9,10},{10,1... | collective-permute-start | bytes 12296 | tf_op jit(solution)/shard_map/ppermute | solution.py:18
  286.6 11.2 %collective-permute-start.8 = (f32[16,64]{1,0:T(8,128)S(1)}, f32[16,64]{1,0:T(8,128)S(1)}, u32[]{:S(2)}, u32[]{:S(2)}) collective-permute-start(f32[16,64]{1,0:T(8,128)S(1)} %get-tuple-element.15), channel_id=1, source_target_pairs={{0,1},{1,2},{2,3},{3,0},{4,5},{5,6},{6,7},{7,4},{8,9},{9,10},{10,1... | collective-permute-start | bytes 12296 | tf_op jit(solution)/shard_map/ppermute | solution.py:18
  294.8 3.0 copy-start.21
  300.8 15.5 %collective-permute-start.10 = (f32[16,8192]{1,0:T(8,128)S(1)}, f32[16,8192]{1,0:T(8,128)S(1)}, u32[]{:S(2)}, u32[]{:S(2)}) collective-permute-start(f32[16,8192]{1,0:T(8,128)S(1)} %fusion.9), channel_id=1, source_target_pairs={{0,1},{1,2},{2,3},{3,0},{4,5},{5,6},{6,7},{7,4},{8,9},{9,10},{10,1... | collective-permute-start | bytes 1572872 | tf_op jit(solution)/shard_map/ppermute | solution.py:18
  306.8 9.5 %collective-permute-start.14 = (f32[16,64]{1,0:T(8,128)S(1)}, f32[16,64]{1,0:T(8,128)S(1)}, u32[]{:S(2)}, u32[]{:S(2)}) collective-permute-start(f32[16,64]{1,0:T(8,128)S(1)} %get-tuple-element.5), channel_id=1, source_target_pairs={{0,1},{1,2},{2,3},{3,0},{4,5},{5,6},{6,7},{7,4},{8,9},{9,10},{10,1... | collective-permute-start | bytes 12296 | tf_op jit(solution)/shard_map/ppermute | solution.py:18
  (29 other events, 31.1 us)
where the time goes:
time: 319 us; the launch traced here: 318 us
  waiting for transfers between devices  173 us (54%)
  starting transfers between devices  89.6 us (28%)
  local copies, waits for them, and re-layouts  21.4 us (7%)
  other arithmetic  19.1 us (6%)
  matrix products  11.7 us (4%)
    ppermute x15, waiting for transfers between devices, from_behind(): return lax.ppermute(value, axis, pairs)  173 us
    ppermute x15, starting transfers between devices, from_behind(): return lax.ppermute(value, axis, pairs)  89.6 us
    add x4, other arithmetic, combine(): earlier[0].reshape(row_count, HEADS, HEAD) * scale_one[..., None]  12.2 us
    unnamed x83, local copies, waits for them, and re-layouts  10.8 us
  transfers between devices with their start and end apart: 15, of which 10 were waited for; matrix products, arithmetic and copies ran while one was open for 6% of the time, Pallas kernels for 0%

commit v1 on v0

v1 whole, which is shorter than its diff:
```python
import functools
import math

import jax
import jax.numpy as jnp
from jax import lax
from jax.experimental import pallas as pl
from jax.experimental.pallas import tpu as pltpu
from jax.sharding import PartitionSpec as P

HEADS = 64
KV_HEADS = 8
HEAD = 128
BLOCK = 256
QROWS = 64
GROUP = HEADS // KV_HEADS
HALF_HEADS = HEADS // 2
HALF = HALF_HEADS * HEAD
PACKET = HALF + 128
FAR = -1e30
LOG2E = math.log2(math.e)

VMEM = pl.BlockSpec(memory_space=pltpu.VMEM)
SMEM = pl.BlockSpec(memory_space=pltpu.SMEM)


def shifted(value, axis, steps):
    count = lax.axis_size(axis)
    pairs = [(source, (source + steps) % count) for source in range(count)]
    return lax.ppermute(value, axis, pairs)


def split_three(value):
    high = value.astype(jnp.bfloat16)
    rest = value - high.astype(jnp.float32)
    middle = rest.astype(jnp.bfloat16)
    low = (rest - middle.astype(jnp.float32)).astype(jnp.bfloat16)
    return high, middle, low


def put_stats(out_ref, stats):
    high, middle, low = (part.astype(jnp.float32) for part in split_three(stats))
    lane = lax.broadcasted_iota(jnp.int32, stats.shape, 1)
    middle = pltpu.roll(middle, HALF_HEADS, 1)
    low = pltpu.roll(low, 2 * HALF_HEADS, 1)
    tile = jnp.where(lane < HALF_HEADS, high, jnp.where(lane < 2 * HALF_HEADS, middle, low))
    out_ref[:, HALF:] = tile.astype(jnp.bfloat16)


def get_stats(packet_ref):
    tile = packet_ref[:, HALF:].astype(jnp.float32)
    middle = pltpu.roll(tile, 128 - HALF_HEADS, 1)
    low = pltpu.roll(tile, 128 - 2 * HALF_HEADS, 1)
    return tile + middle + low


def attend_body(jobs, info_ref, res_id_ref, recv_id_ref, length_ref, res_ref, mig_ref, *refs):
    out_refs = refs[-len(jobs):]
    query_refs = refs[: -len(jobs)]
    member = info_ref[0]
    loop = info_ref[1]
    ones = jnp.ones((2 * BLOCK, HEAD), jnp.bfloat16)
    for (distance, half, operand, first), out_ref in zip(jobs, out_refs, strict=True):
        query_ref = query_refs[operand]
        row_count = query_ref.shape[0]
        anchor = lax.rem(member + distance, loop)
        start = length_ref[0] - QROWS + anchor * row_count
        row = lax.broadcasted_iota(jnp.int32, (row_count, BLOCK), 0)
        token = lax.broadcasted_iota(jnp.int32, (row_count, BLOCK), 1)
        bias = []
        for id_ref in (res_id_ref, recv_id_ref):
            limit = start - id_ref[0, 0] * BLOCK
            bias.append(jnp.where(token <= row + limit, 0.0, FAR).astype(jnp.float32))
        bias = jnp.concatenate(bias, axis=1)
        bias = jnp.concatenate([bias] * GROUP, axis=0)
        lane = lax.broadcasted_iota(jnp.int32, (row_count, 128), 1)
        stats = jnp.zeros((row_count, 128), jnp.float32)
        for local in range(KV_HEADS // 2):
            kv_head = half * (KV_HEADS // 2) + local
            columns = slice(kv_head * HEAD, (kv_head + 1) * HEAD)
            query = jnp.concatenate(
                [
                    query_ref[:, first + (local * GROUP + j) * HEAD : first + (local * GROUP + j + 1) * HEAD]
                    for j in range(GROUP)
                ],
                axis=0,
            )
            keys = jnp.concatenate([res_ref[0, 0, :, columns], mig_ref[0, 0, :, columns]], axis=0)
            values = jnp.concatenate([res_ref[1, 0, :, columns], mig_ref[1, 0, :, columns]], axis=0)
            scores = lax.dot_general(
                query, keys, (((1,), (1,)), ((), ())), preferred_element_type=jnp.float32
            )
            scores = scores * (LOG2E / math.sqrt(HEAD)) + bias
            row_max = jnp.max(scores, axis=1, keepdims=True)
            weights = jnp.exp2(scores - row_max).astype(jnp.bfloat16)
            mixed = jnp.dot(
                weights,
                jnp.concatenate([values, ones], axis=1),
                preferred_element_type=jnp.float32,
            )
            totals = mixed[:, HEAD:]
            scaled = (mixed[:, :HEAD] / totals).astype(jnp.bfloat16)
            level = row_max + jnp.log2(totals)
            for j in range(GROUP):
                head = local * GROUP + j
                rows = slice(j * row_count, (j + 1) * row_count)
                out_ref[:, head * HEAD : (head + 1) * HEAD] = scaled[rows]
                stats = jnp.where(lane == head, level[rows], stats)
        put_stats(out_ref, stats)


def attend(info, ids, res_cache, mig_cache, queries, jobs, name):
    row_count = queries[0].shape[0]
    packet = jax.ShapeDtypeStruct((row_count, PACKET), jnp.bfloat16)
    pairs = len(jobs) * row_count * HALF_HEADS * 2 * BLOCK
    return pl.pallas_call(
        functools.partial(attend_body, jobs),
        out_shape=[packet] * len(jobs),
        in_specs=[SMEM] * 4 + [VMEM] * (2 + len(queries)),
        out_specs=[VMEM] * len(jobs),
        compiler_params=pltpu.CompilerParams(vmem_limit_bytes=32 * 1024 * 1024),
        cost_estimate=pl.CostEstimate(
            flops=pairs * HEAD * 4, bytes_accessed=2 * 1024 * 1024, transcendentals=pairs
        ),
        name=name,
    )(info, *ids, res_cache, mig_cache, *queries)


def join_body(groups, width, *refs):
    in_refs = refs[: sum(groups)]
    out_refs = refs[sum(groups):]
    at = 0
    for index, size in enumerate(groups):
        packets = in_refs[at : at + size]
        at += size
        stats = [get_stats(packet) for packet in packets]
        top = functools.reduce(jnp.maximum, stats)
        shares = [jnp.exp2(stat - top) for stat in stats]
        total = functools.reduce(jnp.add, shares)
        shares = [share / total for share in shares]
        out_ref = out_refs[0] if width else out_refs[index]
        shift = index * HALF if width else 0
        for head in range(HALF_HEADS):
            columns = slice(head * HEAD, (head + 1) * HEAD)
            joined = functools.reduce(
                jnp.add,
                [
                    packet[:, columns].astype(jnp.float32) * share[:, head : head + 1]
                    for packet, share in zip(packets, shares, strict=True)
                ],
            )
            out_ref[:, shift + head * HEAD : shift + (head + 1) * HEAD] = joined.astype(jnp.bfloat16)
        if not width:
            lane = lax.broadcasted_iota(jnp.int32, top.shape, 1)
            put_stats(out_ref, jnp.where(lane < HALF_HEADS, top + jnp.log2(total), 0.0))


def join(groups, name, width=0):
    row_count = groups[0][0].shape[0]
    if width:
        shape = jax.ShapeDtypeStruct((row_count, width), jnp.bfloat16)
    else:
        shape = [jax.ShapeDtypeStruct((row_count, PACKET), jnp.bfloat16)] * len(groups)
    packets = [packet for group in groups for packet in group]
    return pl.pallas_call(
        functools.partial(join_body, tuple(len(group) for group in groups), width),
        out_shape=shape,
        in_specs=[VMEM] * len(packets),
        out_specs=VMEM if width else [VMEM] * len(groups),
        compiler_params=pltpu.CompilerParams(vmem_limit_bytes=32 * 1024 * 1024),
        cost_estimate=pl.CostEstimate(
            flops=len(packets) * row_count * HALF * 2,
            bytes_accessed=len(packets) * row_count * PACKET * 2,
            transcendentals=0,
        ),
        name=name,
    )(*packets)


def per_device(queries, res_cache, mig_cache, res_ids, recv_ids, lengths):
    loop = lax.axis_size("blk")
    info = jnp.stack([lax.axis_index("blk"), jnp.int32(loop)]).astype(jnp.int32)
    ids = (res_ids, recv_ids, lengths)
    mine = queries[0]
    mine_a, mine_b = mine[:, :HALF], mine[:, HALF:]

    arrived = shifted(mig_cache, "sess", lax.axis_size("sess") // 2)
    left_a = shifted(mine_a, "blk", 1)
    right_b = shifted(mine_b, "blk", -1)
    left_b = shifted(mine_b, "blk", 1)
    right_a = shifted(mine_a, "blk", -1)
    far_a = shifted(left_a, "blk", 1)
    far_b = shifted(right_b, "blk", -1)

    run = functools.partial(attend, info, ids, res_cache, arrived)
    to_right_b, to_left_a = run(
        (right_b, left_a), ((1, 1, 0, 0), (loop - 1, 0, 1, 0)), "near_direct"
    )
    from_left_b = shifted(to_right_b, "blk", 1)
    from_right_a = shifted(to_left_a, "blk", -1)
    to_right_a, to_left_b = run(
        (right_a, left_b), ((1, 0, 0, 0), (loop - 1, 1, 1, 0)), "near_joined"
    )
    far_out_a, far_out_b = run((far_a, far_b), ((2, 0, 0, 0), (2, 1, 1, 0)), "far")
    via_left_a = shifted(far_out_a, "blk", 1)
    via_right_b = shifted(far_out_b, "blk", -1)
    own_a, own_b = run((mine,), ((0, 0, 0, 0), (0, 1, 0, HALF)), "own")
    (sum_right_a,) = join(((to_right_a, via_left_a),), "join_right")
    from_left_a = shifted(sum_right_a, "blk", 1)
    (sum_left_b,) = join(((to_left_b, via_right_b),), "join_left")
    from_right_b = shifted(sum_left_b, "blk", -1)
    out = join(
        ((own_a, from_right_a, from_left_a), (own_b, from_left_b, from_right_b)),
        "join_home",
        2 * HALF,
    )
    return out[None]


def solution(mesh):
    placed = (
        P("sess", "blk", None),
        P(None, "sess", "blk", None),
        P(None, "sess", "blk", None),
        P("sess", "blk"),
        P("sess", "blk"),
        P("sess"),
    )
    return jax.shard_map(
        per_device, mesh=mesh, in_specs=placed, out_specs=P("sess", "blk", None), check_vma=False
    )
```

time: 319 us -> 109 us (0.34)
  waiting for transfers between devices: 173 us -> 17.9 us
  local copies, waits for them, and re-layouts: 21.4 us -> 2.23 us
  other arithmetic: 19.1 us -> 0.08 us
  starting transfers between devices: 89.6 us -> 75.7 us
  matrix products: 11.7 us -> 0 us
  Pallas kernels: 0 us -> 9.01 us
    ppermute x15 -> x13, waiting for transfers between devices: 173 us -> 17.9 us  [shifted(): return lax.ppermute(value, axis, pairs)]
    ppermute x15 -> x13, starting transfers between devices: 89.6 us -> 75.7 us  [shifted(): return lax.ppermute(value, axis, pairs)]
    add x14 -> x0, other arithmetic: 13.6 us -> none  [the longest x4 12.2 us: combine(): earlier[0].reshape(row_count, HEADS, HEAD) * scale_one[..., None]]
    dot_general x16 -> x0, matrix products: 11.7 us -> none  [the longest x8 5.96 us: attend_part(): jnp.einsum('rgjd,kgd->rgjk', query_four, key_three, preferred_element_typ...]
    unnamed x83 -> x6, local copies, waits for them, and re-layouts: 10.8 us -> 1.24 us
    pallas_call x0 -> x7, Pallas kernels: none -> 9.01 us  [the longest x4 6.78 us: attend(): pl.pallas_call(functools.partial(attend_body, jobs), out_shape=[packet] *...]
    reshape x16 -> x0, local copies, waits for them, and re-layouts: 4.76 us -> none  [the longest x8 2.47 us: attend_part(): totals.reshape(row_count, HEADS)]
    reduce_sum x4 -> x0, other arithmetic: 3.77 us -> none  [attend_part(): totals = jnp.sum(weights, axis=-1, dtype=jnp.float32)]
  transfers between devices with their start and end apart: 15 -> 13, of which waited for: 10 -> 5; matrix products, arithmetic and copies ran while one was open for 6% -> 1% of each run, Pallas kernels for 0% -> 7%
where the time goes in v1:
time: 109 us; the launch traced here: 107 us
  starting transfers between devices  75.7 us (69%)
  waiting for transfers between devices  17.9 us (16%)
  Pallas kernels  9.01 us (8%)
  local copies, waits for them, and re-layouts  2.23 us (2%)
  between operations  2.14 us (2%)
    ppermute x13, starting transfers between devices, shifted(): return lax.ppermute(value, axis, pairs)  75.7 us
    ppermute x13, waiting for transfers between devices, shifted(): return lax.ppermute(value, axis, pairs)  17.9 us
    pallas_call x4, Pallas kernels, attend(): pl.pallas_call(functools.partial(attend_body, jobs), out_shape=[packet] *...  6.78 us
    pallas_call x3, Pallas kernels, join(): pl.pallas_call(functools.partial(join_body, tuple((len(group) for group i...  2.23 us
  transfers between devices with their start and end apart: 13, of which 5 were waited for; matrix products, arithmetic and copies ran while one was open for 1% of the time, Pallas kernels for 7%

profile of v1, /device:TPU:24, one launch (start us, length us, event | category | flops | bytes accessed | tf_op | source)
XLA Modules:
  0.0 107.0 jit_solution(8270100938944286533)
XLA Ops:
  0.0 4.9 %collective-permute-start = (bf16[2,1,256,1024]{3,2,1,0:T(8,128)(2,1)}, bf16[2,1,256,1024]{3,2,1,0:T(8,128)(2,1)S(1)}, u32[]{:S(2)}, u32[]{:S(2)}) collective-permute-start(bf16[2,1,256,1024]{3,2,1,0:T(8,128)(2,1)} %param.8), channel_id=1, source_target_pairs={{0,256},{4,260},{8,264},{12,268},{16,272},{20,276},{24,280},{28,28... | collective-permute-start | bytes 3145736 | tf_op jit(solution)/shard_map/ppermute | solution.py:30
  4.9 1.0 fusion
  5.9 9.1 %collective-permute-start.2 = (bf16[16,4096]{1,0:T(8,128)(2,1)S(1)}, bf16[16,4096]{1,0:T(8,128)(2,1)S(1)}, u32[]{:S(2)}, u32[]{:S(2)}) collective-permute-start(bf16[16,4096]{1,0:T(8,128)(2,1)S(1)} %get-tuple-element.21), channel_id=1, source_target_pairs={{0,1},{1,2},{2,3},{3,0},{4,5},{5,6},{6,7},{7,4},{8,9},{9,10},{10,1... | collective-permute-start | bytes 393224 | tf_op jit(solution)/shard_map/ppermute | solution.py:30
  15.0 5.6 %collective-permute-start.1 = (bf16[16,4096]{1,0:T(8,128)(2,1)S(1)}, bf16[16,4096]{1,0:T(8,128)(2,1)S(1)}, u32[]{:S(2)}, u32[]{:S(2)}) collective-permute-start(bf16[16,4096]{1,0:T(8,128)(2,1)S(1)} %get-tuple-element.22), channel_id=1, source_target_pairs={{0,3},{1,0},{2,1},{3,2},{4,7},{5,4},{6,5},{7,6},{8,11},{9,8},{10,9... | collective-permute-start | bytes 393224 | tf_op jit(solution)/shard_map/ppermute | solution.py:30
  20.6 1.6 %collective-permute-done.2.refs_1_ = bf16[16,4096]{1,0:T(8,128)(2,1)S(1)} collective-permute-done((bf16[16,4096]{1,0:T(8,128)(2,1)S(1)}, bf16[16,4096]{1,0:T(8,128)(2,1)S(1)}, u32[]{:S(2)}, u32[]{:S(2)}) %collective-permute-start.2) | collective-permute-done | bytes 131104 | tf_op jit(solution)/shard_map/ppermute | solution.py:30
  22.2 12.6 %collective-permute-start.6 = (bf16[16,4096]{1,0:T(8,128)(2,1)S(1)}, bf16[16,4096]{1,0:T(8,128)(2,1)S(1)}, u32[]{:S(2)}, u32[]{:S(2)}) collective-permute-start(bf16[16,4096]{1,0:T(8,128)(2,1)S(1)} %collective-permute-done.2.refs_1_), channel_id=1, source_target_pairs={{0,1},{1,2},{2,3},{3,0},{4,5},{5,6},{6,7},{7,4},{8,9},{9,10},{10,1... | collective-permute-start | bytes 393224 | tf_op jit(solution)/shard_map/ppermute | solution.py:30
  35.6 4.3 %collective-permute-start.7 = (bf16[16,4096]{1,0:T(8,128)(2,1)S(1)}, bf16[16,4096]{1,0:T(8,128)(2,1)S(1)}, u32[]{:S(2)}, u32[]{:S(2)}) collective-permute-start(bf16[16,4096]{1,0:T(8,128)(2,1)S(1)} %collective-permute-done.1.refs_0_), channel_id=1, source_target_pairs={{0,3},{1,0},{2,1},{3,2},{4,7},{5,4},{6,5},{7,6},{8,11},{9,8},{10,9... | collective-permute-start | bytes 393224 | tf_op jit(solution)/shard_map/ppermute | solution.py:30
  39.9 7.3 %collective-permute-start.4 = (bf16[16,4096]{1,0:T(8,128)(2,1)S(1)}, bf16[16,4096]{1,0:T(8,128)(2,1)S(1)}, u32[]{:S(2)}, u32[]{:S(2)}) collective-permute-start(bf16[16,4096]{1,0:T(8,128)(2,1)S(1)} %get-tuple-element.21), channel_id=1, source_target_pairs={{0,3},{1,0},{2,1},{3,2},{4,7},{5,4},{6,5},{7,6},{8,11},{9,8},{10,9... | collective-permute-start | bytes 393224 | tf_op jit(solution)/shard_map/ppermute | solution.py:30
  47.2 2.5 %collective-permute-start.5 = (bf16[16,4096]{1,0:T(8,128)(2,1)S(1)}, bf16[16,4096]{1,0:T(8,128)(2,1)S(1)}, u32[]{:S(2)}, u32[]{:S(2)}) collective-permute-start(bf16[16,4096]{1,0:T(8,128)(2,1)S(1)} %get-tuple-element.22), channel_id=1, source_target_pairs={{0,1},{1,2},{2,3},{3,0},{4,5},{5,6},{6,7},{7,4},{8,9},{9,10},{10,1... | collective-permute-start | bytes 393224 | tf_op jit(solution)/shard_map/ppermute | solution.py:30
  51.7 8.3 %collective-permute-done.7.refs_1_ = bf16[16,4096]{1,0:T(8,128)(2,1)S(1)} collective-permute-done((bf16[16,4096]{1,0:T(8,128)(2,1)S(1)}, bf16[16,4096]{1,0:T(8,128)(2,1)S(1)}, u32[]{:S(2)}, u32[]{:S(2)}) %collective-permute-start.7) | collective-permute-done | bytes 131104 | tf_op jit(solution)/shard_map/ppermute | solution.py:30
  60.0 1.2 %copy-done = bf16[2,1,256,1024]{3,2,1,0:T(8,128)(2,1)S(1)} copy-done((bf16[2,1,256,1024]{3,2,1,0:T(8,128)(2,1)S(1)}, bf16[2,1,256,1024]{3,2,1,0:T(8,128)(2,1)}, u32[]{:S(2)}) %copy-start) | copy-done | bytes 1048600
  61.2 1.7 %far.1 = (bf16[16,4224]{1,0:T(8,128)(2,1)S(1)}, bf16[16,4224]{1,0:T(8,128)(2,1)S(1)}) custom-call(s32[2]{0:T(128)S(1)} %pad_add_fusion.info_ref, s32[1,1]{1,0:T(1,128)S(6)} %copy.7.res_id_ref, s32[1,1]{1,0:T(1,128)S(6)} %copy.8.recv_id_ref, s32[1]{0:T(128)S(6)} %copy.9.length_ref, bf16[2,1,256,1024]{3,2,1,0:T(8,128)(2,1)S(1)} %copy-done, ...), custom_call_target="tpu_custom_call" | custom-call | flops 268435456 | bytes 2097152 | tf_op jit(solution)/shard_map/far/pallas_call | solution.py:116
  62.9 4.5 %collective-permute-start.11 = (bf16[16,4224]{1,0:T(8,128)(2,1)S(1)}, bf16[16,4224]{1,0:T(8,128)(2,1)S(1)}, u32[]{:S(2)}, u32[]{:S(2)}) collective-permute-start(bf16[16,4224]{1,0:T(8,128)(2,1)S(1)} %get-tuple-element.20), channel_id=1, source_target_pairs={{0,3},{1,0},{2,1},{3,2},{4,7},{5,4},{6,5},{7,6},{8,11},{9,8},{10,9... | collective-permute-start | bytes 405512 | tf_op jit(solution)/shard_map/ppermute | solution.py:30
  67.4 5.2 %collective-permute-start.8 = (bf16[16,4224]{1,0:T(8,128)(2,1)S(1)}, bf16[16,4224]{1,0:T(8,128)(2,1)S(1)}, u32[]{:S(2)}, u32[]{:S(2)}) collective-permute-start(bf16[16,4224]{1,0:T(8,128)(2,1)S(1)} %get-tuple-element.16), channel_id=1, source_target_pairs={{0,1},{1,2},{2,3},{3,0},{4,5},{5,6},{6,7},{7,4},{8,9},{9,10},{10,1... | collective-permute-start | bytes 405512 | tf_op jit(solution)/shard_map/ppermute | solution.py:30
  72.6 1.7 %near_direct.1 = (bf16[16,4224]{1,0:T(8,128)(2,1)S(1)}, bf16[16,4224]{1,0:T(8,128)(2,1)S(1)}) custom-call(s32[2]{0:T(128)S(1)} %pad_add_fusion.info_ref, s32[1,1]{1,0:T(1,128)S(6)} %copy.7.res_id_ref, s32[1,1]{1,0:T(1,128)S(6)} %copy.8.recv_id_ref, s32[1]{0:T(128)S(6)} %copy.9.length_ref, bf16[2,1,256,1024]{3,2,1,0:T(8,128)(2,1)S(1)} %copy-done, ...), custom_call_target="tpu_custom_call" | custom-call | flops 268435456 | bytes 2097152 | tf_op jit(solution)/shard_map/near_direct/pallas_call | solution.py:116
  74.3 5.5 %collective-permute-start.10 = (bf16[16,4224]{1,0:T(8,128)(2,1)S(1)}, bf16[16,4224]{1,0:T(8,128)(2,1)S(1)}, u32[]{:S(2)}, u32[]{:S(2)}) collective-permute-start(bf16[16,4224]{1,0:T(8,128)(2,1)S(1)} %get-tuple-element.18), channel_id=1, source_target_pairs={{0,1},{1,2},{2,3},{3,0},{4,5},{5,6},{6,7},{7,4},{8,9},{9,10},{10,1... | collective-permute-start | bytes 405512 | tf_op jit(solution)/shard_map/ppermute | solution.py:30
  79.9 4.4 %collective-permute-start.3 = (bf16[16,4224]{1,0:T(8,128)(2,1)S(1)}, bf16[16,4224]{1,0:T(8,128)(2,1)S(1)}, u32[]{:S(2)}, u32[]{:S(2)}) collective-permute-start(bf16[16,4224]{1,0:T(8,128)(2,1)S(1)} %get-tuple-element.14), channel_id=1, source_target_pairs={{0,3},{1,0},{2,1},{3,2},{4,7},{5,4},{6,5},{7,6},{8,11},{9,8},{10,9... | collective-permute-start | bytes 405512 | tf_op jit(solution)/shard_map/ppermute | solution.py:30
  84.3 1.7 %near_joined.1 = (bf16[16,4224]{1,0:T(8,128)(2,1)S(1)}, bf16[16,4224]{1,0:T(8,128)(2,1)S(1)}) custom-call(s32[2]{0:T(128)S(1)} %pad_add_fusion.info_ref, s32[1,1]{1,0:T(1,128)S(6)} %copy.7.res_id_ref, s32[1,1]{1,0:T(1,128)S(6)} %copy.8.recv_id_ref, s32[1]{0:T(128)S(6)} %copy.9.length_ref, bf16[2,1,256,1024]{3,2,1,0:T(8,128)(2,1)S(1)} %copy-done, ...), custom_call_target="tpu_custom_call" | custom-call | flops 268435456 | bytes 2097152 | tf_op jit(solution)/shard_map/near_joined/pallas_call | solution.py:116
  86.3 4.7 %collective-permute-start.12 = (bf16[16,4224]{1,0:T(8,128)(2,1)S(1)}, bf16[16,4224]{1,0:T(8,128)(2,1)S(1)}, u32[]{:S(2)}, u32[]{:S(2)}) collective-permute-start(bf16[16,4224]{1,0:T(8,128)(2,1)S(1)} %join_left.1), channel_id=1, source_target_pairs={{0,3},{1,0},{2,1},{3,2},{4,7},{5,4},{6,5},{7,6},{8,11},{9,8},{10,9... | collective-permute-start | bytes 405512 | tf_op jit(solution)/shard_map/ppermute | solution.py:30
  91.4 5.2 %collective-permute-start.9 = (bf16[16,4224]{1,0:T(8,128)(2,1)S(1)}, bf16[16,4224]{1,0:T(8,128)(2,1)S(1)}, u32[]{:S(2)}, u32[]{:S(2)}) collective-permute-start(bf16[16,4224]{1,0:T(8,128)(2,1)S(1)} %join_right.1), channel_id=1, source_target_pairs={{0,1},{1,2},{2,3},{3,0},{4,5},{5,6},{6,7},{7,4},{8,9},{9,10},{10,1... | collective-permute-start | bytes 405512 | tf_op jit(solution)/shard_map/ppermute | solution.py:30
  96.6 1.7 %own.1 = (bf16[16,4224]{1,0:T(8,128)(2,1)S(1)}, bf16[16,4224]{1,0:T(8,128)(2,1)S(1)}) custom-call(s32[2]{0:T(128)S(1)} %pad_add_fusion.info_ref, s32[1,1]{1,0:T(1,128)S(6)} %copy.7.res_id_ref, s32[1,1]{1,0:T(1,128)S(6)} %copy.8.recv_id_ref, s32[1]{0:T(128)S(6)} %copy.9.length_ref, bf16[2,1,256,1024]{3,2,1,0:T(8,128)(2,1)S(1)} %copy-done.1, ...), custom_call_target="tpu_custom_call" | custom-call | flops 268435456 | bytes 2097152 | tf_op jit(solution)/shard_map/own/pallas_call | solution.py:116
  98.3 1.5 %collective-permute-done.12.refs_5_ = bf16[16,4224]{1,0:T(8,128)(2,1)S(1)} collective-permute-done((bf16[16,4224]{1,0:T(8,128)(2,1)S(1)}, bf16[16,4224]{1,0:T(8,128)(2,1)S(1)}, u32[]{:S(2)}, u32[]{:S(2)}) %collective-permute-start.12) | collective-permute-done | bytes 135200 | tf_op jit(solution)/shard_map/ppermute | solution.py:30
  99.8 5.7 %collective-permute-done.9.refs_2_ = bf16[16,4224]{1,0:T(8,128)(2,1)S(1)} collective-permute-done((bf16[16,4224]{1,0:T(8,128)(2,1)S(1)}, bf16[16,4224]{1,0:T(8,128)(2,1)S(1)}, u32[]{:S(2)}, u32[]{:S(2)}) %collective-permute-start.9) | collective-permute-done | bytes 135200 | tf_op jit(solution)/shard_map/ppermute | solution.py:30
  105.5 1.5 %join_home.1 = bf16[16,8192]{1,0:T(8,128)(2,1)} custom-call(bf16[16,4224]{1,0:T(8,128)(2,1)S(1)} %get-tuple-element.13.refs_0_, bf16[16,4224]{1,0:T(8,128)(2,1)S(1)} %collective-permute-done.3.refs_1_, bf16[16,4224]{1,0:T(8,128)(2,1)S(1)} %collective-permute-done.9.refs_2_, bf16[16,4224]{1,0:T(8,128)(2,1)S(1)} %get-tuple-element.17.refs_3_, ...), custom_call_target="tpu_custom_call" | custom-call | flops 786432 | bytes 811008 | tf_op jit(solution)/shard_map/join_home/pallas_call | solution.py:165
  (17 shorter events, 1.6 us)
Async XLA Ops:
  0.0 60.0 %collective-permute-start = (bf16[2,1,256,1024]{3,2,1,0:T(8,128)(2,1)}, bf16[2,1,256,1024]{3,2,1,0:T(8,128)(2,1)S(1)}, u32[]{:S(2)}, u32[]{:S(2)}) collective-permute-start(bf16[2,1,256,1024]{3,2,1,0:T(8,128)(2,1)} %param.8), channel_id=1, source_target_pairs={{0,256},{4,260},{8,264},{12,268},{16,272},{20,276},{24,280},{28,28... | collective-permute-start | bytes 3145736 | tf_op jit(solution)/shard_map/ppermute | solution.py:30
  5.9 16.2 %collective-permute-start.2 = (bf16[16,4096]{1,0:T(8,128)(2,1)S(1)}, bf16[16,4096]{1,0:T(8,128)(2,1)S(1)}, u32[]{:S(2)}, u32[]{:S(2)}) collective-permute-start(bf16[16,4096]{1,0:T(8,128)(2,1)S(1)} %get-tuple-element.21), channel_id=1, source_target_pairs={{0,1},{1,2},{2,3},{3,0},{4,5},{5,6},{6,7},{7,4},{8,9},{9,10},{10,1... | collective-permute-start | bytes 393224 | tf_op jit(solution)/shard_map/ppermute | solution.py:30
  15.0 20.5 %collective-permute-start.1 = (bf16[16,4096]{1,0:T(8,128)(2,1)S(1)}, bf16[16,4096]{1,0:T(8,128)(2,1)S(1)}, u32[]{:S(2)}, u32[]{:S(2)}) collective-permute-start(bf16[16,4096]{1,0:T(8,128)(2,1)S(1)} %get-tuple-element.22), channel_id=1, source_target_pairs={{0,3},{1,0},{2,1},{3,2},{4,7},{5,4},{6,5},{7,6},{8,11},{9,8},{10,9... | collective-permute-start | bytes 393224 | tf_op jit(solution)/shard_map/ppermute | solution.py:30
  22.2 29.5 %collective-permute-start.6 = (bf16[16,4096]{1,0:T(8,128)(2,1)S(1)}, bf16[16,4096]{1,0:T(8,128)(2,1)S(1)}, u32[]{:S(2)}, u32[]{:S(2)}) collective-permute-start(bf16[16,4096]{1,0:T(8,128)(2,1)S(1)} %collective-permute-done.2.refs_1_), channel_id=1, source_target_pairs={{0,1},{1,2},{2,3},{3,0},{4,5},{5,6},{6,7},{7,4},{8,9},{9,10},{10,1... | collective-permute-start | bytes 393224 | tf_op jit(solution)/shard_map/ppermute | solution.py:30
  35.6 24.4 %collective-permute-start.7 = (bf16[16,4096]{1,0:T(8,128)(2,1)S(1)}, bf16[16,4096]{1,0:T(8,128)(2,1)S(1)}, u32[]{:S(2)}, u32[]{:S(2)}) collective-permute-start(bf16[16,4096]{1,0:T(8,128)(2,1)S(1)} %collective-permute-done.1.refs_0_), channel_id=1, source_target_pairs={{0,3},{1,0},{2,1},{3,2},{4,7},{5,4},{6,5},{7,6},{8,11},{9,8},{10,9... | collective-permute-start | bytes 393224 | tf_op jit(solution)/shard_map/ppermute | solution.py:30
  39.9 40.0 %collective-permute-start.4 = (bf16[16,4096]{1,0:T(8,128)(2,1)S(1)}, bf16[16,4096]{1,0:T(8,128)(2,1)S(1)}, u32[]{:S(2)}, u32[]{:S(2)}) collective-permute-start(bf16[16,4096]{1,0:T(8,128)(2,1)S(1)} %get-tuple-element.21), channel_id=1, source_target_pairs={{0,3},{1,0},{2,1},{3,2},{4,7},{5,4},{6,5},{7,6},{8,11},{9,8},{10,9... | collective-permute-start | bytes 393224 | tf_op jit(solution)/shard_map/ppermute | solution.py:30
  47.2 37.1 %collective-permute-start.5 = (bf16[16,4096]{1,0:T(8,128)(2,1)S(1)}, bf16[16,4096]{1,0:T(8,128)(2,1)S(1)}, u32[]{:S(2)}, u32[]{:S(2)}) collective-permute-start(bf16[16,4096]{1,0:T(8,128)(2,1)S(1)} %get-tuple-element.22), channel_id=1, source_target_pairs={{0,1},{1,2},{2,3},{3,0},{4,5},{5,6},{6,7},{7,4},{8,9},{9,10},{10,1... | collective-permute-start | bytes 393224 | tf_op jit(solution)/shard_map/ppermute | solution.py:30
  60.0 1.2 %copy-start = (bf16[2,1,256,1024]{3,2,1,0:T(8,128)(2,1)S(1)}, bf16[2,1,256,1024]{3,2,1,0:T(8,128)(2,1)}, u32[]{:S(2)}) copy-start(bf16[2,1,256,1024]{3,2,1,0:T(8,128)(2,1)} %res_ref.7) | copy-start | bytes 3145732
  62.9 23.1 %collective-permute-start.11 = (bf16[16,4224]{1,0:T(8,128)(2,1)S(1)}, bf16[16,4224]{1,0:T(8,128)(2,1)S(1)}, u32[]{:S(2)}, u32[]{:S(2)}) collective-permute-start(bf16[16,4224]{1,0:T(8,128)(2,1)S(1)} %get-tuple-element.20), channel_id=1, source_target_pairs={{0,3},{1,0},{2,1},{3,2},{4,7},{5,4},{6,5},{7,6},{8,11},{9,8},{10,9... | collective-permute-start | bytes 405512 | tf_op jit(solution)/shard_map/ppermute | solution.py:30
  67.4 23.6 %collective-permute-start.8 = (bf16[16,4224]{1,0:T(8,128)(2,1)S(1)}, bf16[16,4224]{1,0:T(8,128)(2,1)S(1)}, u32[]{:S(2)}, u32[]{:S(2)}) collective-permute-start(bf16[16,4224]{1,0:T(8,128)(2,1)S(1)} %get-tuple-element.16), channel_id=1, source_target_pairs={{0,1},{1,2},{2,3},{3,0},{4,5},{5,6},{6,7},{7,4},{8,9},{9,10},{10,1... | collective-permute-start | bytes 405512 | tf_op jit(solution)/shard_map/ppermute | solution.py:30
  74.3 24.0 %collective-permute-start.10 = (bf16[16,4224]{1,0:T(8,128)(2,1)S(1)}, bf16[16,4224]{1,0:T(8,128)(2,1)S(1)}, u32[]{:S(2)}, u32[]{:S(2)}) collective-permute-start(bf16[16,4224]{1,0:T(8,128)(2,1)S(1)} %get-tuple-element.18), channel_id=1, source_target_pairs={{0,1},{1,2},{2,3},{3,0},{4,5},{5,6},{6,7},{7,4},{8,9},{9,10},{10,1... | collective-permute-start | bytes 405512 | tf_op jit(solution)/shard_map/ppermute | solution.py:30
  79.9 16.7 %copy-start.1 = (bf16[2,1,256,1024]{3,2,1,0:T(8,128)(2,1)S(1)}, bf16[2,1,256,1024]{3,2,1,0:T(8,128)(2,1)}, u32[]{:S(2)}) copy-start(bf16[2,1,256,1024]{3,2,1,0:T(8,128)(2,1)} %res_ref.7) | copy-start | bytes 3145732
  79.9 18.4 %collective-permute-start.3 = (bf16[16,4224]{1,0:T(8,128)(2,1)S(1)}, bf16[16,4224]{1,0:T(8,128)(2,1)S(1)}, u32[]{:S(2)}, u32[]{:S(2)}) collective-permute-start(bf16[16,4224]{1,0:T(8,128)(2,1)S(1)} %get-tuple-element.14), channel_id=1, source_target_pairs={{0,3},{1,0},{2,1},{3,2},{4,7},{5,4},{6,5},{7,6},{8,11},{9,8},{10,9... | collective-permute-start | bytes 405512 | tf_op jit(solution)/shard_map/ppermute | solution.py:30
  86.3 10.3 %copy-start.2 = (bf16[1,16,8192]{2,1,0:T(8,128)(2,1)S(1)}, bf16[1,16,8192]{2,1,0:T(8,128)(2,1)}, u32[]{:S(2)}) copy-start(bf16[1,16,8192]{2,1,0:T(8,128)(2,1)} %param.6) | copy-start | bytes 786436
  86.3 13.5 %collective-permute-start.12 = (bf16[16,4224]{1,0:T(8,128)(2,1)S(1)}, bf16[16,4224]{1,0:T(8,128)(2,1)S(1)}, u32[]{:S(2)}, u32[]{:S(2)}) collective-permute-start(bf16[16,4224]{1,0:T(8,128)(2,1)S(1)} %join_left.1), channel_id=1, source_target_pairs={{0,3},{1,0},{2,1},{3,2},{4,7},{5,4},{6,5},{7,6},{8,11},{9,8},{10,9... | collective-permute-start | bytes 405512 | tf_op jit(solution)/shard_map/ppermute | solution.py:30
  91.4 14.1 %collective-permute-start.9 = (bf16[16,4224]{1,0:T(8,128)(2,1)S(1)}, bf16[16,4224]{1,0:T(8,128)(2,1)S(1)}, u32[]{:S(2)}, u32[]{:S(2)}) collective-permute-start(bf16[16,4224]{1,0:T(8,128)(2,1)S(1)} %join_right.1), channel_id=1, source_target_pairs={{0,1},{1,2},{2,3},{3,0},{4,5},{5,6},{6,7},{7,4},{8,9},{9,10},{10,1... | collective-permute-start | bytes 405512 | tf_op jit(solution)/shard_map/ppermute | solution.py:30

commit v2 on v1

v2 whole, which is shorter than its diff:
```python
import functools
import math

import jax
import jax.numpy as jnp
from jax import lax
from jax.experimental import pallas as pl
from jax.experimental.pallas import tpu as pltpu
from jax.sharding import PartitionSpec as P

HEADS = 64
KV_HEADS = 8
HEAD = 128
BLOCK = 256
QROWS = 64
GROUP = HEADS // KV_HEADS
HALF_HEADS = HEADS // 2
HALF = HALF_HEADS * HEAD
PACKET = HALF + 128
FAR = -1e30
LOG2E = math.log2(math.e)

VMEM = pl.BlockSpec(memory_space=pltpu.VMEM)
SMEM = pl.BlockSpec(memory_space=pltpu.SMEM)


def shifted(value, axis, steps):
    count = lax.axis_size(axis)
    pairs = [(source, (source + steps) % count) for source in range(count)]
    return lax.ppermute(value, axis, pairs)


def split_three(value):
    high = value.astype(jnp.bfloat16)
    rest = value - high.astype(jnp.float32)
    middle = rest.astype(jnp.bfloat16)
    low = (rest - middle.astype(jnp.float32)).astype(jnp.bfloat16)
    return high, middle, low


def put_stats(out_ref, stats):
    high, middle, low = (part.astype(jnp.float32) for part in split_three(stats))
    lane = lax.broadcasted_iota(jnp.int32, stats.shape, 1)
    middle = pltpu.roll(middle, HALF_HEADS, 1)
    low = pltpu.roll(low, 2 * HALF_HEADS, 1)
    tile = jnp.where(lane < HALF_HEADS, high, jnp.where(lane < 2 * HALF_HEADS, middle, low))
    out_ref[:, HALF:] = tile.astype(jnp.bfloat16)


def get_stats(packet_ref):
    tile = packet_ref[:, HALF:].astype(jnp.float32)
    middle = pltpu.roll(tile, 128 - HALF_HEADS, 1)
    low = pltpu.roll(tile, 128 - 2 * HALF_HEADS, 1)
    return tile + middle + low


def attend_body(loop, distance, info_ref, res_id_ref, recv_id_ref, length_ref, query_ref, res_ref, mig_ref, *out_refs):
    row_count = query_ref.shape[0]
    anchor = lax.rem(info_ref[0] + distance * info_ref[1], loop)
    start = length_ref[0] - QROWS + anchor * row_count
    row = lax.broadcasted_iota(jnp.int32, (row_count, BLOCK), 0)
    token = lax.broadcasted_iota(jnp.int32, (row_count, BLOCK), 1)
    bias = []
    for id_ref in (res_id_ref, recv_id_ref):
        limit = start - id_ref[0, 0] * BLOCK
        bias.append(jnp.where(token <= row + limit, 0.0, FAR).astype(jnp.float32))
    bias = jnp.concatenate(bias, axis=1)
    bias = jnp.concatenate([bias] * GROUP, axis=0)
    ones = jnp.ones((2 * BLOCK, HEAD), jnp.bfloat16)
    lane = lax.broadcasted_iota(jnp.int32, (row_count, 128), 1)
    for half, out_ref in enumerate(out_refs):
        stats = jnp.zeros((row_count, 128), jnp.float32)
        for local in range(KV_HEADS // 2):
            kv_head = half * (KV_HEADS // 2) + local
            columns = slice(kv_head * HEAD, (kv_head + 1) * HEAD)
            heads = [kv_head * GROUP + j for j in range(GROUP)]
            query = jnp.concatenate([query_ref[:, h * HEAD : (h + 1) * HEAD] for h in heads], axis=0)
            keys = jnp.concatenate([res_ref[0, 0, :, columns], mig_ref[0, 0, :, columns]], axis=0)
            values = jnp.concatenate([res_ref[1, 0, :, columns], mig_ref[1, 0, :, columns]], axis=0)
            scores = lax.dot_general(
                query, keys, (((1,), (1,)), ((), ())), preferred_element_type=jnp.float32
            )
            scores = scores * (LOG2E / math.sqrt(HEAD)) + bias
            row_max = jnp.max(scores, axis=1, keepdims=True)
            weights = jnp.exp2(scores - row_max).astype(jnp.bfloat16)
            mixed = jnp.dot(
                weights,
                jnp.concatenate([values, ones], axis=1),
                preferred_element_type=jnp.float32,
            )
            totals = mixed[:, HEAD:]
            scaled = (mixed[:, :HEAD] / totals).astype(jnp.bfloat16)
            level = row_max + jnp.log2(totals)
            for j in range(GROUP):
                head = local * GROUP + j
                rows = slice(j * row_count, (j + 1) * row_count)
                out_ref[:, head * HEAD : (head + 1) * HEAD] = scaled[rows]
                stats = jnp.where(lane == head, level[rows], stats)
        put_stats(out_ref, stats)


def whole_body(loop, distance, *refs):
    out_ref = refs[-1]
    halves = [out_ref.at[:, half * PACKET : (half + 1) * PACKET] for half in range(2)]
    attend_body(loop, distance, *refs[:-1], *halves)


def attend(loop, info, ids, res_cache, mig_cache, queries, distance, name, split=False):
    row_count = queries.shape[0]
    pairs = row_count * HEADS * 2 * BLOCK
    packet = jax.ShapeDtypeStruct((row_count, PACKET), jnp.bfloat16)
    return pl.pallas_call(
        functools.partial(attend_body if split else whole_body, loop, distance),
        out_shape=[packet] * 2 if split else jax.ShapeDtypeStruct((row_count, 2 * PACKET), jnp.bfloat16),
        in_specs=[SMEM] * 4 + [VMEM] * 3,
        out_specs=[VMEM] * 2 if split else VMEM,
        compiler_params=pltpu.CompilerParams(vmem_limit_bytes=32 * 1024 * 1024),
        cost_estimate=pl.CostEstimate(
            flops=pairs * HEAD * 4, bytes_accessed=2 * 1024 * 1024, transcendentals=pairs
        ),
        name=name,
    )(info, *ids, queries, res_cache, mig_cache)


def join_packets(packets):
    stats = [get_stats(packet) for packet in packets]
    top = functools.reduce(jnp.maximum, stats)
    shares = [jnp.exp2(stat - top) for stat in stats]
    total = functools.reduce(jnp.add, shares)
    heads = []
    for head in range(HALF_HEADS):
        columns = slice(head * HEAD, (head + 1) * HEAD)
        parts = [
            packet[:, columns].astype(jnp.float32) * (share / total)[:, head : head + 1]
            for packet, share in zip(packets, shares, strict=True)
        ]
        heads.append(functools.reduce(jnp.add, parts))
    return heads, top + jnp.log2(total)


def join_body(*refs):
    out_ref = refs[-1]
    heads, stats = join_packets(refs[:-1])
    for head, joined in enumerate(heads):
        out_ref[:, head * HEAD : (head + 1) * HEAD] = joined.astype(jnp.bfloat16)
    lane = lax.broadcasted_iota(jnp.int32, stats.shape, 1)
    put_stats(out_ref, jnp.where(lane < HALF_HEADS, stats, 0.0))


def join_home_body(own_ref, direct_ref, summed_a_ref, summed_b_ref, out_ref):
    for half, summed_ref in enumerate((summed_a_ref, summed_b_ref)):
        part = slice(half * PACKET, (half + 1) * PACKET)
        heads, _ = join_packets([own_ref.at[:, part], direct_ref.at[:, part], summed_ref])
        for head, joined in enumerate(heads):
            first = half * HALF + head * HEAD
            out_ref[:, first : first + HEAD] = joined.astype(jnp.bfloat16)


def join_call(body, packets, columns, name):
    row_count = packets[0].shape[0]
    return pl.pallas_call(
        body,
        out_shape=jax.ShapeDtypeStruct((row_count, columns), jnp.bfloat16),
        in_specs=[VMEM] * len(packets),
        out_specs=VMEM,
        compiler_params=pltpu.CompilerParams(vmem_limit_bytes=32 * 1024 * 1024),
        cost_estimate=pl.CostEstimate(
            flops=len(packets) * row_count * HALF * 2,
            bytes_accessed=len(packets) * row_count * PACKET * 2,
            transcendentals=0,
        ),
        name=name,
    )(*packets)


def join(packets, name):
    return join_call(join_body, packets, PACKET, name)


def join_home(own, direct, summed):
    return join_call(join_home_body, (own, direct, *summed), 2 * HALF, "join_home")


def along(value, steps):
    sessions, loop = lax.axis_size("sess"), lax.axis_size("blk")
    pairs = [
        (s * loop + b, s * loop + (b + (steps if s % 2 == 0 else -steps)) % loop)
        for s in range(sessions)
        for b in range(loop)
    ]
    return lax.ppermute(value, ("sess", "blk"), pairs)


def per_device(queries, res_cache, mig_cache, res_ids, recv_ids, lengths):
    loop = lax.axis_size("blk")
    way = 1 - 2 * lax.rem(lax.axis_index("sess"), 2)
    info = jnp.stack([lax.axis_index("blk") + loop, way]).astype(jnp.int32)
    ids = (res_ids, recv_ids, lengths)
    mine = queries[0]

    before = along(mine, 1)
    arrived = shifted(mig_cache, "sess", lax.axis_size("sess") // 2)
    after = along(mine, -1)
    far = along(before, 1)

    run = functools.partial(attend, loop, info, ids, res_cache, arrived)
    home_1 = along(run(before, -1, "attend_before"), -1)
    after_a, after_b = run(after, 1, "attend_after", split=True)
    far, after_a, after_b = lax.optimization_barrier((far, after_a, after_b))
    far_a, far_b = run(far, 2, "attend_far", split=True)
    via_a = along(far_a, 1)
    via_b = along(far_b, 1)
    mine, home_1 = lax.optimization_barrier((mine, home_1))
    own = run(mine, 0, "attend_own")
    after_a, own = lax.optimization_barrier((after_a, own))
    home_2a = along(join((after_a, via_a), "join_a"), 1)
    home_2b = along(join((after_b, via_b), "join_b"), 1)
    return join_home(own, home_1, (home_2a, home_2b))[None]


def solution(mesh):
    placed = (
        P("sess", "blk", None),
        P(None, "sess", "blk", None),
        P(None, "sess", "blk", None),
        P("sess", "blk"),
        P("sess", "blk"),
        P("sess"),
    )
    return jax.shard_map(
        per_device, mesh=mesh, in_specs=placed, out_specs=P("sess", "blk", None), check_vma=False
    )
```

time: 109 us -> 114 us (1.046); the launches traced: 107 us -> 114 us
  waiting for transfers between devices: 17.9 us -> 32.8 us
  starting transfers between devices: 75.7 us -> 68.9 us
    ppermute x13 -> x1, starting transfers between devices: 75.7 us -> 4.92 us  [shifted(): return lax.ppermute(value, axis, pairs)]
    ppermute x0 -> x8, starting transfers between devices: none -> 64 us  [along(): return lax.ppermute(value, ('sess', 'blk'), pairs)]
    ppermute x0 -> x8, waiting for transfers between devices: none -> 32.8 us  [along(): return lax.ppermute(value, ('sess', 'blk'), pairs)]
    ppermute x13 -> x1, waiting for transfers between devices: 17.9 us -> 0.01 us  [shifted(): return lax.ppermute(value, axis, pairs)]
  transfers between devices with their start and end apart: 13 -> 9, of which waited for: 5 -> 4; matrix products, arithmetic and copies ran while one was open for 1% -> 0% of each run, Pallas kernels for 7% -> 7%
where the time goes in v2:
time: 114 us
  starting transfers between devices  68.9 us (60%)
  waiting for transfers between devices  32.8 us (29%)
  Pallas kernels  9 us (8%)
  between operations  2.07 us (2%)
  local copies, waits for them, and re-layouts  1.23 us (1%)
    ppermute x8, starting transfers between devices, along(): return lax.ppermute(value, ('sess', 'blk'), pairs)  64 us
    ppermute x8, waiting for transfers between devices, along(): return lax.ppermute(value, ('sess', 'blk'), pairs)  32.8 us
    pallas_call x4, Pallas kernels, attend(): pl.pallas_call(functools.partial(attend_body if split else whole_body, lo...  6.77 us
    ppermute x1, starting transfers between devices, shifted(): return lax.ppermute(value, axis, pairs)  4.92 us
  transfers between devices with their start and end apart: 9, of which 4 were waited for; matrix products, arithmetic and copies ran while one was open for 0% of the time, Pallas kernels for 7%

profile of v2, /device:TPU:24, one launch (start us, length us, event | category | flops | bytes accessed | tf_op | source)
XLA Modules:
  0.0 114.0 jit_solution(4760516526918907556)
XLA Ops:
  0.0 4.9 %collective-permute-start.3 = (bf16[2,1,256,1024]{3,2,1,0:T(8,128)(2,1)}, bf16[2,1,256,1024]{3,2,1,0:T(8,128)(2,1)S(1)}, u32[]{:S(2)}, u32[]{:S(2)}) collective-permute-start(bf16[2,1,256,1024]{3,2,1,0:T(8,128)(2,1)} %param.8), channel_id=1, source_target_pairs={{0,256},{4,260},{8,264},{12,268},{16,272},{20,276},{24,280},{28,28... | collective-permute-start | bytes 3145736 | tf_op jit(solution)/shard_map/ppermute | solution.py:30
  4.9 9.1 %collective-permute-start = (bf16[16,8192]{1,0:T(8,128)(2,1)}, bf16[16,8192]{1,0:T(8,128)(2,1)S(1)}, u32[]{:S(2)}, u32[]{:S(2)}) collective-permute-start(bf16[16,8192]{1,0:T(8,128)(2,1)} %bitcast.4), channel_id=1, source_target_pairs={{0,1},{1,2},{2,3},{3,0},{4,7},{5,4},{6,5},{7,6},{8,9},{9,10},{10,1... | collective-permute-start | bytes 786440 | tf_op jit(solution)/shard_map/ppermute | solution.py:191
  14.0 5.6 %collective-permute-start.2 = (bf16[16,8192]{1,0:T(8,128)(2,1)}, bf16[16,8192]{1,0:T(8,128)(2,1)S(1)}, u32[]{:S(2)}, u32[]{:S(2)}) collective-permute-start(bf16[16,8192]{1,0:T(8,128)(2,1)} %bitcast.5), channel_id=1, source_target_pairs={{0,3},{1,0},{2,1},{3,2},{4,5},{5,6},{6,7},{7,4},{8,11},{9,8},{10,9... | collective-permute-start | bytes 786440 | tf_op jit(solution)/shard_map/ppermute | solution.py:191
  19.6 2.9 %collective-permute-done.refs_4_ = bf16[16,8192]{1,0:T(8,128)(2,1)S(1)} collective-permute-done((bf16[16,8192]{1,0:T(8,128)(2,1)}, bf16[16,8192]{1,0:T(8,128)(2,1)S(1)}, u32[]{:S(2)}, u32[]{:S(2)}) %collective-permute-start) | collective-permute-done | bytes 262176 | tf_op jit(solution)/shard_map/ppermute | solution.py:191
  22.5 24.0 %collective-permute-start.1 = (bf16[16,8192]{1,0:T(8,128)(2,1)S(1)}, bf16[16,8192]{1,0:T(8,128)(2,1)S(1)}, u32[]{:S(2)}, u32[]{:S(2)}) collective-permute-start(bf16[16,8192]{1,0:T(8,128)(2,1)S(1)} %collective-permute-done.refs_4_), channel_id=1, source_target_pairs={{0,1},{1,2},{2,3},{3,0},{4,7},{5,4},{6,5},{7,6},{8,9},{9,10},{10,1... | collective-permute-start | bytes 786440 | tf_op jit(solution)/shard_map/ppermute | solution.py:191
  48.5 0.1 pad_add_fusion.info_ref.refs_0_
  48.6 0.0 collective-permute-done.3.mig_ref.refs_6_
  48.6 1.2 %copy-done = bf16[2,1,256,1024]{3,2,1,0:T(8,128)(2,1)S(1)} copy-done((bf16[2,1,256,1024]{3,2,1,0:T(8,128)(2,1)S(1)}, bf16[2,1,256,1024]{3,2,1,0:T(8,128)(2,1)}, u32[]{:S(2)}) %copy-start) | copy-done | bytes 1048600
  49.8 1.7 %attend_before.1 = bf16[16,8448]{1,0:T(8,128)(2,1)S(1)} custom-call(s32[2]{0:T(128)S(1)} %pad_add_fusion.info_ref.refs_0_, s32[1,1]{1,0:T(1,128)S(6)} %copy.7.res_id_ref.refs_1_, s32[1,1]{1,0:T(1,128)S(6)} %copy.8.recv_id_ref.refs_2_, s32[1]{0:T(128)S(6)} %copy.9.length_ref.refs_3_, bf16[16,8192]{1,0:T(8,128)(2,1)S(1)} %collective-permute-done.refs_4_, ...), custom_call_target="tpu_custom_call" | custom-call | flops 268435456 | bytes 2097152 | tf_op jit(solution)/shard_map/attend_before/pallas_call | solution.py:112
  51.5 1.9 %collective-permute-start.4 = (bf16[16,8448]{1,0:T(8,128)(2,1)S(1)}, bf16[16,8448]{1,0:T(8,128)(2,1)S(1)}, u32[]{:S(2)}, u32[]{:S(2)}) collective-permute-start(bf16[16,8448]{1,0:T(8,128)(2,1)S(1)} %attend_before.1), channel_id=1, source_target_pairs={{0,3},{1,0},{2,1},{3,2},{4,5},{5,6},{6,7},{7,4},{8,11},{9,8},{10,9... | collective-permute-start | bytes 811016 | tf_op jit(solution)/shard_map/ppermute | solution.py:191
  53.4 0.0 collective-permute-done.2.query_ref
  53.4 1.7 %attend_after.1 = (bf16[16,4224]{1,0:T(8,128)(2,1)S(1)}, bf16[16,4224]{1,0:T(8,128)(2,1)S(1)}) custom-call(s32[2]{0:T(128)S(1)} %pad_add_fusion.info_ref.refs_0_, s32[1,1]{1,0:T(1,128)S(6)} %copy.7.res_id_ref.refs_1_, s32[1,1]{1,0:T(1,128)S(6)} %copy.8.recv_id_ref.refs_2_, s32[1]{0:T(128)S(6)} %copy.9.length_ref.refs_3_, ...), custom_call_target="tpu_custom_call" | custom-call | flops 268435456 | bytes 2097152 | tf_op jit(solution)/shard_map/attend_after/pallas_call | solution.py:112
  55.1 23.0 %collective-permute-done.1.query_ref = bf16[16,8192]{1,0:T(8,128)(2,1)S(1)} collective-permute-done((bf16[16,8192]{1,0:T(8,128)(2,1)S(1)}, bf16[16,8192]{1,0:T(8,128)(2,1)S(1)}, u32[]{:S(2)}, u32[]{:S(2)}) %collective-permute-start.1) | collective-permute-done | bytes 262176 | tf_op jit(solution)/shard_map/ppermute | solution.py:191
  78.2 1.7 %attend_far.1 = (bf16[16,4224]{1,0:T(8,128)(2,1)S(1)}, bf16[16,4224]{1,0:T(8,128)(2,1)S(1)}) custom-call(s32[2]{0:T(128)S(1)} %pad_add_fusion.info_ref.refs_0_, s32[1,1]{1,0:T(1,128)S(6)} %copy.7.res_id_ref.refs_1_, s32[1,1]{1,0:T(1,128)S(6)} %copy.8.recv_id_ref.refs_2_, s32[1]{0:T(128)S(6)} %copy.9.length_ref.refs_3_, ...), custom_call_target="tpu_custom_call" | custom-call | flops 268435456 | bytes 2097152 | tf_op jit(solution)/shard_map/attend_far/pallas_call | solution.py:112
  79.8 8.5 %collective-permute-start.7 = (bf16[16,4224]{1,0:T(8,128)(2,1)S(1)}, bf16[16,4224]{1,0:T(8,128)(2,1)S(1)}, u32[]{:S(2)}, u32[]{:S(2)}) collective-permute-start(bf16[16,4224]{1,0:T(8,128)(2,1)S(1)} %get-tuple-element.26), channel_id=1, source_target_pairs={{0,1},{1,2},{2,3},{3,0},{4,7},{5,4},{6,5},{7,6},{8,9},{9,10},{10,1... | collective-permute-start | bytes 405512 | tf_op jit(solution)/shard_map/ppermute | solution.py:191
  88.3 1.9 %collective-permute-start.5 = (bf16[16,4224]{1,0:T(8,128)(2,1)S(1)}, bf16[16,4224]{1,0:T(8,128)(2,1)S(1)}, u32[]{:S(2)}, u32[]{:S(2)}) collective-permute-start(bf16[16,4224]{1,0:T(8,128)(2,1)S(1)} %get-tuple-element.24), channel_id=1, source_target_pairs={{0,1},{1,2},{2,3},{3,0},{4,7},{5,4},{6,5},{7,6},{8,9},{9,10},{10,1... | collective-permute-start | bytes 405512 | tf_op jit(solution)/shard_map/ppermute | solution.py:191
  90.3 2.2 %collective-permute-done.7.refs_1_ = bf16[16,4224]{1,0:T(8,128)(2,1)S(1)} collective-permute-done((bf16[16,4224]{1,0:T(8,128)(2,1)S(1)}, bf16[16,4224]{1,0:T(8,128)(2,1)S(1)}, u32[]{:S(2)}, u32[]{:S(2)}) %collective-permute-start.7) | collective-permute-done | bytes 135200 | tf_op jit(solution)/shard_map/ppermute | solution.py:191
  92.4 0.3 join_b.1
  92.8 6.8 %collective-permute-start.8 = (bf16[16,4224]{1,0:T(8,128)(2,1)S(1)}, bf16[16,4224]{1,0:T(8,128)(2,1)S(1)}, u32[]{:S(2)}, u32[]{:S(2)}) collective-permute-start(bf16[16,4224]{1,0:T(8,128)(2,1)S(1)} %join_b.1), channel_id=1, source_target_pairs={{0,1},{1,2},{2,3},{3,0},{4,7},{5,4},{6,5},{7,6},{8,9},{9,10},{10,1... | collective-permute-start | bytes 405512 | tf_op jit(solution)/shard_map/ppermute | solution.py:191
  99.6 1.7 %attend_own.1.own_ref = bf16[16,8448]{1,0:T(8,128)(2,1)S(1)} custom-call(s32[2]{0:T(128)S(1)} %pad_add_fusion.info_ref.refs_0_, s32[1,1]{1,0:T(1,128)S(6)} %copy.7.res_id_ref.refs_1_, s32[1,1]{1,0:T(1,128)S(6)} %copy.8.recv_id_ref.refs_2_, s32[1]{0:T(128)S(6)} %copy.9.length_ref.refs_3_, bf16[16,8192]{1,0:T(8,128)(2,1)S(1)} %bitcast.6, ...), custom_call_target="tpu_custom_call" | custom-call | flops 268435456 | bytes 2097152 | tf_op jit(solution)/shard_map/attend_own/pallas_call | solution.py:112
  101.3 0.3 join_a.1
  101.7 6.2 %collective-permute-start.6 = (bf16[16,4224]{1,0:T(8,128)(2,1)S(1)}, bf16[16,4224]{1,0:T(8,128)(2,1)S(1)}, u32[]{:S(2)}, u32[]{:S(2)}) collective-permute-start(bf16[16,4224]{1,0:T(8,128)(2,1)S(1)} %join_a.1), channel_id=1, source_target_pairs={{0,1},{1,2},{2,3},{3,0},{4,7},{5,4},{6,5},{7,6},{8,9},{9,10},{10,1... | collective-permute-start | bytes 405512 | tf_op jit(solution)/shard_map/ppermute | solution.py:191
  107.9 4.6 %collective-permute-done.6.summed_a_ref = bf16[16,4224]{1,0:T(8,128)(2,1)S(1)} collective-permute-done((bf16[16,4224]{1,0:T(8,128)(2,1)S(1)}, bf16[16,4224]{1,0:T(8,128)(2,1)S(1)}, u32[]{:S(2)}, u32[]{:S(2)}) %collective-permute-start.6) | collective-permute-done | bytes 135200 | tf_op jit(solution)/shard_map/ppermute | solution.py:191
  112.5 1.5 %join_home.1 = bf16[16,8192]{1,0:T(8,128)(2,1)} custom-call(bf16[16,8448]{1,0:T(8,128)(2,1)S(1)} %attend_own.1.own_ref, bf16[16,8448]{1,0:T(8,128)(2,1)S(1)} %collective-permute-done.4.direct_ref, bf16[16,4224]{1,0:T(8,128)(2,1)S(1)} %collective-permute-done.6.summed_a_ref, bf16[16,4224]{1,0:T(8,128)(2,1)S(1)} %collective-permute-done.8.summed_b_ref), custom_call_target="tpu_custom_call" | custom-call | flops 524288 | bytes 540672 | tf_op jit(solution)/shard_map/join_home/pallas_call | solution.py:161
  (8 shorter events, 0.0 us)
Async XLA Ops:
  0.0 48.6 %collective-permute-start.3 = (bf16[2,1,256,1024]{3,2,1,0:T(8,128)(2,1)}, bf16[2,1,256,1024]{3,2,1,0:T(8,128)(2,1)S(1)}, u32[]{:S(2)}, u32[]{:S(2)}) collective-permute-start(bf16[2,1,256,1024]{3,2,1,0:T(8,128)(2,1)} %param.8), channel_id=1, source_target_pairs={{0,256},{4,260},{8,264},{12,268},{16,272},{20,276},{24,280},{28,28... | collective-permute-start | bytes 3145736 | tf_op jit(solution)/shard_map/ppermute | solution.py:30
  4.9 17.6 %collective-permute-start = (bf16[16,8192]{1,0:T(8,128)(2,1)}, bf16[16,8192]{1,0:T(8,128)(2,1)S(1)}, u32[]{:S(2)}, u32[]{:S(2)}) collective-permute-start(bf16[16,8192]{1,0:T(8,128)(2,1)} %bitcast.4), channel_id=1, source_target_pairs={{0,1},{1,2},{2,3},{3,0},{4,7},{5,4},{6,5},{7,6},{8,9},{9,10},{10,1... | collective-permute-start | bytes 786440 | tf_op jit(solution)/shard_map/ppermute | solution.py:191
  14.0 39.4 %collective-permute-start.2 = (bf16[16,8192]{1,0:T(8,128)(2,1)}, bf16[16,8192]{1,0:T(8,128)(2,1)S(1)}, u32[]{:S(2)}, u32[]{:S(2)}) collective-permute-start(bf16[16,8192]{1,0:T(8,128)(2,1)} %bitcast.5), channel_id=1, source_target_pairs={{0,3},{1,0},{2,1},{3,2},{4,5},{5,6},{6,7},{7,4},{8,11},{9,8},{10,9... | collective-permute-start | bytes 786440 | tf_op jit(solution)/shard_map/ppermute | solution.py:191
  22.5 55.6 %collective-permute-start.1 = (bf16[16,8192]{1,0:T(8,128)(2,1)S(1)}, bf16[16,8192]{1,0:T(8,128)(2,1)S(1)}, u32[]{:S(2)}, u32[]{:S(2)}) collective-permute-start(bf16[16,8192]{1,0:T(8,128)(2,1)S(1)} %collective-permute-done.refs_4_), channel_id=1, source_target_pairs={{0,1},{1,2},{2,3},{3,0},{4,7},{5,4},{6,5},{7,6},{8,9},{9,10},{10,1... | collective-permute-start | bytes 786440 | tf_op jit(solution)/shard_map/ppermute | solution.py:191
  48.6 1.2 %copy-start = (bf16[2,1,256,1024]{3,2,1,0:T(8,128)(2,1)S(1)}, bf16[2,1,256,1024]{3,2,1,0:T(8,128)(2,1)}, u32[]{:S(2)}) copy-start(bf16[2,1,256,1024]{3,2,1,0:T(8,128)(2,1)} %res_ref.3) | copy-start | bytes 3145732
  51.5 48.1 %collective-permute-start.4 = (bf16[16,8448]{1,0:T(8,128)(2,1)S(1)}, bf16[16,8448]{1,0:T(8,128)(2,1)S(1)}, u32[]{:S(2)}, u32[]{:S(2)}) collective-permute-start(bf16[16,8448]{1,0:T(8,128)(2,1)S(1)} %attend_before.1), channel_id=1, source_target_pairs={{0,3},{1,0},{2,1},{3,2},{4,5},{5,6},{6,7},{7,4},{8,11},{9,8},{10,9... | collective-permute-start | bytes 811016 | tf_op jit(solution)/shard_map/ppermute | solution.py:191
  78.2 21.5 %copy-start.1 = (bf16[2,1,256,1024]{3,2,1,0:T(8,128)(2,1)S(1)}, bf16[2,1,256,1024]{3,2,1,0:T(8,128)(2,1)}, u32[]{:S(2)}) copy-start(bf16[2,1,256,1024]{3,2,1,0:T(8,128)(2,1)} %res_ref.3) | copy-start | bytes 3145732
  79.8 19.8 %copy-start.2 = (bf16[1,16,8192]{2,1,0:T(8,128)(2,1)S(1)}, bf16[1,16,8192]{2,1,0:T(8,128)(2,1)}, u32[]{:S(2)}) copy-start(bf16[1,16,8192]{2,1,0:T(8,128)(2,1)} %param.6) | copy-start | bytes 786436
  79.8 12.6 %collective-permute-start.7 = (bf16[16,4224]{1,0:T(8,128)(2,1)S(1)}, bf16[16,4224]{1,0:T(8,128)(2,1)S(1)}, u32[]{:S(2)}, u32[]{:S(2)}) collective-permute-start(bf16[16,4224]{1,0:T(8,128)(2,1)S(1)} %get-tuple-element.26), channel_id=1, source_target_pairs={{0,1},{1,2},{2,3},{3,0},{4,7},{5,4},{6,5},{7,6},{8,9},{9,10},{10,1... | collective-permute-start | bytes 405512 | tf_op jit(solution)/shard_map/ppermute | solution.py:191
  88.3 13.0 %collective-permute-start.5 = (bf16[16,4224]{1,0:T(8,128)(2,1)S(1)}, bf16[16,4224]{1,0:T(8,128)(2,1)S(1)}, u32[]{:S(2)}, u32[]{:S(2)}) collective-permute-start(bf16[16,4224]{1,0:T(8,128)(2,1)S(1)} %get-tuple-element.24), channel_id=1, source_target_pairs={{0,1},{1,2},{2,3},{3,0},{4,7},{5,4},{6,5},{7,6},{8,9},{9,10},{10,1... | collective-permute-start | bytes 405512 | tf_op jit(solution)/shard_map/ppermute | solution.py:191
  92.8 15.1 %collective-permute-start.8 = (bf16[16,4224]{1,0:T(8,128)(2,1)S(1)}, bf16[16,4224]{1,0:T(8,128)(2,1)S(1)}, u32[]{:S(2)}, u32[]{:S(2)}) collective-permute-start(bf16[16,4224]{1,0:T(8,128)(2,1)S(1)} %join_b.1), channel_id=1, source_target_pairs={{0,1},{1,2},{2,3},{3,0},{4,7},{5,4},{6,5},{7,6},{8,9},{9,10},{10,1... | collective-permute-start | bytes 405512 | tf_op jit(solution)/shard_map/ppermute | solution.py:191
  101.7 10.8 %collective-permute-start.6 = (bf16[16,4224]{1,0:T(8,128)(2,1)S(1)}, bf16[16,4224]{1,0:T(8,128)(2,1)S(1)}, u32[]{:S(2)}, u32[]{:S(2)}) collective-permute-start(bf16[16,4224]{1,0:T(8,128)(2,1)S(1)} %join_a.1), channel_id=1, source_target_pairs={{0,1},{1,2},{2,3},{3,0},{4,7},{5,4},{6,5},{7,6},{8,9},{9,10},{10,1... | collective-permute-start | bytes 405512 | tf_op jit(solution)/shard_map/ppermute | solution.py:191

commit v3 on v2

v3 whole, which is shorter than its diff:
```python
import functools
import math

import jax
import jax.numpy as jnp
from jax import lax
from jax.experimental import pallas as pl
from jax.experimental.pallas import tpu as pltpu
from jax.sharding import PartitionSpec as P

HEADS = 64
KV_HEADS = 8
HEAD = 128
BLOCK = 256
QROWS = 64
GROUP = HEADS // KV_HEADS
TILE = 128
PARTS = ((0, KV_HEADS // 2), (KV_HEADS // 2, KV_HEADS))
FAR = -1e30
LOG2E = math.log2(math.e)

VMEM = pl.BlockSpec(memory_space=pltpu.VMEM)
SMEM = pl.BlockSpec(memory_space=pltpu.SMEM)


def shifted(value, axis, steps):
    count = lax.axis_size(axis)
    pairs = [(source, (source + steps) % count) for source in range(count)]
    return lax.ppermute(value, axis, pairs)


def split_three(value):
    high = value.astype(jnp.bfloat16)
    rest = value - high.astype(jnp.float32)
    middle = rest.astype(jnp.bfloat16)
    low = (rest - middle.astype(jnp.float32)).astype(jnp.bfloat16)
    return high, middle, low


def packet_heads(packet):
    return (packet.shape[1] - TILE) // HEAD


def put_stats(out_ref, stats):
    heads = packet_heads(out_ref)
    high, middle, low = (term.astype(jnp.float32) for term in split_three(stats))
    lane = lax.broadcasted_iota(jnp.int32, stats.shape, 1)
    middle = pltpu.roll(middle, heads, 1)
    low = pltpu.roll(low, 2 * heads, 1)
    tile = jnp.where(lane < heads, high, jnp.where(lane < 2 * heads, middle, low))
    out_ref[:, heads * HEAD :] = tile.astype(jnp.bfloat16)


def get_stats(packet_ref):
    heads = packet_heads(packet_ref)
    tile = packet_ref[:, heads * HEAD :].astype(jnp.float32)
    middle = pltpu.roll(tile, TILE - heads, 1)
    low = pltpu.roll(tile, TILE - 2 * heads, 1)
    return tile + middle + low


def sections(ref):
    width = GROUP * HEAD
    return [
        ref.at[:, first * width + part * TILE : last * width + (part + 1) * TILE]
        for part, (first, last) in enumerate(PARTS)
    ]


def attend_body(loop, distance, counts, info_ref, res_id_ref, recv_id_ref, length_ref, res_ref, mig_ref, *refs):
    query_counts, packet_counts, forward, base = counts
    query_refs = refs[: len(query_counts)]
    out_refs = refs[len(query_counts) :]
    packet_refs = sections(out_refs[0]) if out_refs[0].shape[1] > HEADS * HEAD else out_refs
    row_count = query_refs[0].shape[0]
    anchor = lax.rem(info_ref[0] + distance * info_ref[1], loop)
    start = length_ref[0] - QROWS + anchor * row_count
    row = lax.broadcasted_iota(jnp.int32, (row_count, BLOCK), 0)
    token = lax.broadcasted_iota(jnp.int32, (row_count, BLOCK), 1)
    bias = []
    for id_ref in (res_id_ref, recv_id_ref):
        limit = start - id_ref[0, 0] * BLOCK
        bias.append(jnp.where(token <= row + limit, 0.0, FAR).astype(jnp.float32))
    bias = jnp.concatenate(bias, axis=1)
    bias = jnp.concatenate([bias] * GROUP, axis=0)
    ones = jnp.ones((2 * BLOCK, HEAD), jnp.bfloat16)
    lane = lax.broadcasted_iota(jnp.int32, (row_count, TILE), 1)
    if forward:
        at = 0
        for query_ref in query_refs:
            out_refs[-1][:, at : at + query_ref.shape[1]] = query_ref[...]
            at += query_ref.shape[1]
    sources = [(ref, local) for ref, count in zip(query_refs, query_counts, strict=True) for local in range(count)]
    key_head = base
    for out_ref, count in zip(packet_refs, packet_counts):
        stats = jnp.zeros((row_count, TILE), jnp.float32)
        for local in range(count):
            query_ref, place = sources[key_head - base]
            columns = slice(key_head * HEAD, (key_head + 1) * HEAD)
            key_head += 1
            query = jnp.concatenate(
                [
                    query_ref[:, (place * GROUP + j) * HEAD : (place * GROUP + j + 1) * HEAD]
                    for j in range(GROUP)
                ],
                axis=0,
            )
            keys = jnp.concatenate([res_ref[0, 0, :, columns], mig_ref[0, 0, :, columns]], axis=0)
            values = jnp.concatenate([res_ref[1, 0, :, columns], mig_ref[1, 0, :, columns]], axis=0)
            scores = lax.dot_general(
                query, keys, (((1,), (1,)), ((), ())), preferred_element_type=jnp.float32
            )
            scores = scores * (LOG2E / math.sqrt(HEAD)) + bias
            row_max = jnp.max(scores, axis=1, keepdims=True)
            weights = jnp.exp2(scores - row_max).astype(jnp.bfloat16)
            mixed = jnp.dot(
                weights,
                jnp.concatenate([values, ones], axis=1),
                preferred_element_type=jnp.float32,
            )
            totals = mixed[:, HEAD:]
            scaled = (mixed[:, :HEAD] / totals).astype(jnp.bfloat16)
            level = row_max + jnp.log2(totals)
            for j in range(GROUP):
                head = local * GROUP + j
                rows = slice(j * row_count, (j + 1) * row_count)
                out_ref[:, head * HEAD : (head + 1) * HEAD] = scaled[rows]
                stats = jnp.where(lane == head, level[rows], stats)
        put_stats(out_ref, stats)


def call(body, operands, columns, scalars, cost, name):
    row_count = operands[-1].shape[0]
    flops, loaded, transcendentals = cost
    return pl.pallas_call(
        body,
        out_shape=[jax.ShapeDtypeStruct((row_count, width), jnp.bfloat16) for width in columns],
        in_specs=[SMEM] * scalars + [VMEM] * (len(operands) - scalars),
        out_specs=[VMEM] * len(columns),
        compiler_params=pltpu.CompilerParams(vmem_limit_bytes=16 * 1024 * 1024),
        cost_estimate=pl.CostEstimate(
            flops=flops, bytes_accessed=loaded, transcendentals=transcendentals
        ),
        name=name,
    )(*operands)


def attend(loop, scalars, res_cache, mig_cache, queries, distance, name, forward=False, single=False, parts=(0, 1)):
    width = GROUP * HEAD
    query_counts = tuple(part.shape[1] // width for part in queries)
    packet_counts = tuple(PARTS[part][1] - PARTS[part][0] for part in parts)
    columns = [count * width + TILE for count in packet_counts]
    columns = ([sum(columns)] if single else columns) + [KV_HEADS * width] * forward
    pairs = queries[0].shape[0] * sum(query_counts) * GROUP * 2 * BLOCK
    return call(
        functools.partial(attend_body, loop, distance, (query_counts, packet_counts, forward, PARTS[parts[0]][0])),
        (*scalars, res_cache, mig_cache, *queries),
        columns,
        len(scalars),
        (pairs * HEAD * 4, 2 * 1024 * 1024, pairs),
        name,
    )


def join_packets(packets):
    stats = [get_stats(packet) for packet in packets]
    top = functools.reduce(jnp.maximum, stats)
    shares = [jnp.exp2(stat - top) for stat in stats]
    total = functools.reduce(jnp.add, shares)
    shares = [share / total for share in shares]
    heads = []
    for head in range(packet_heads(packets[0])):
        columns = slice(head * HEAD, (head + 1) * HEAD)
        terms = [
            packet[:, columns].astype(jnp.float32) * share[:, head : head + 1]
            for packet, share in zip(packets, shares, strict=True)
        ]
        heads.append(functools.reduce(jnp.add, terms))
    return heads, top + jnp.log2(total)


def put_heads(out_ref, first, heads):
    for head, joined in enumerate(heads, first):
        out_ref[:, head * HEAD : (head + 1) * HEAD] = joined.astype(jnp.bfloat16)


def join_body(*refs):
    count = len(refs) // 2
    ones, others, outs = refs[:count], refs[count : len(refs) - count], refs[len(refs) - count :]
    if len(others) < count:
        others = sections(others[0])
    for one_ref, other_ref, out_ref in zip(ones, others, outs, strict=True):
        heads, stats = join_packets((one_ref, other_ref))
        put_heads(out_ref, 0, heads)
        lane = lax.broadcasted_iota(jnp.int32, stats.shape, 1)
        put_stats(out_ref, jnp.where(lane < len(heads), stats, 0.0))


def join_part_body(own_ref, sum_ref, out_ref):
    put_heads(out_ref, 0, join_packets((own_ref, sum_ref))[0])


def join_home_body(done_ref, own_ref, sum_ref, out_ref):
    out_ref[:, : done_ref.shape[1]] = done_ref[...]
    put_heads(out_ref, done_ref.shape[1] // HEAD, join_packets((own_ref, sum_ref))[0])


def join(body, operands, columns, name):
    size = operands[0].shape[0] * sum(columns)
    return call(body, operands, columns, 0, (4 * size, 6 * size, 0), name)


def join_sums(ones, others, name):
    return join(join_body, (*ones, *others), [one.shape[1] for one in ones], name)


def join_home(own, sums):
    (part,) = join(join_part_body, (own[0], sums[0]), [own[0].shape[1] - TILE], "join_part")
    (whole,) = join(join_home_body, (part, own[1], sums[1]), [HEADS * HEAD], "join_home")
    return whole


def onward(value):
    sessions, loop = lax.axis_size("sess"), lax.axis_size("blk")
    pairs = [
        (s * loop + b, s * loop + (b + (1 if s % 2 == 0 else -1)) % loop)
        for s in range(sessions)
        for b in range(loop)
    ]
    return lax.ppermute(value, ("sess", "blk"), pairs)


def per_device(queries, res_cache, mig_cache, res_ids, recv_ids, lengths):
    loop = lax.axis_size("blk")
    way = 1 - 2 * lax.rem(lax.axis_index("sess"), 2)
    info = jnp.stack([lax.axis_index("blk") + loop, way]).astype(jnp.int32)
    scalars = (info, res_ids, recv_ids, lengths)
    mine = queries[0]
    mine = tuple(
        mine[:, first * GROUP * HEAD : last * GROUP * HEAD] for first, last in PARTS
    )
    arrived = shifted(mig_cache, "sess", lax.axis_size("sess") // 2)
    run = functools.partial(attend, loop, scalars, res_cache, arrived)
    before = tuple(onward(part) for part in mine)
    far_a, far_b = tuple(onward(part) for part in before)
    first_a, first_b = tuple(onward(part) for part in run(before, -1, "attend_before"))
    after_a = onward(far_a)
    part_far = run((far_a, far_b), -2, "attend_far")
    (sum_a,) = join_sums(part_far[:1], (first_a,), "join_far_a")
    second_a = onward(sum_a)
    far_b, sum_a = lax.optimization_barrier((far_b, sum_a))
    after_b = onward(far_b)
    (sum_b,) = join_sums(part_far[1:], (first_b,), "join_far_b")
    second_b = onward(sum_b)
    after_a, sum_b = lax.optimization_barrier((after_a, sum_b))
    (sum_a,) = join_sums(run((after_a,), 1, "attend_after_a", parts=(0,)), (second_a,), "join_after_a")
    third_a = onward(sum_a)
    after_b, sum_a = lax.optimization_barrier((after_b, sum_a))
    (sum_b,) = join_sums(run((after_b,), 1, "attend_after_b", parts=(1,)), (second_b,), "join_after_b")
    third_b = onward(sum_b)
    mine, third_a = lax.optimization_barrier((mine, third_a))
    own = run(mine, 0, "attend_own")
    return join_home(own, (third_a, third_b))[None]


def solution(mesh):
    placed = (
        P("sess", "blk", None),
        P(None, "sess", "blk", None),
        P(None, "sess", "blk", None),
        P("sess", "blk"),
        P("sess", "blk"),
        P("sess"),
    )
    return jax.shard_map(
        per_device, mesh=mesh, in_specs=placed, out_specs=P("sess", "blk", None), check_vma=False
    )
```

time: 114 us -> 100 us (0.88)
  the two profiles are of different devices: /device:TPU:24 before, /device:TPU:88 now
where the time goes in v3:
time: 100 us; the launch traced here: 99.5 us
  starting transfers between devices  66.8 us (67%)
  waiting for transfers between devices  17.8 us (18%)
  Pallas kernels  10.5 us (10%)
  local copies, waits for them, and re-layouts  2.21 us (2%)
  between operations  2.15 us (2%)
    ppermute x12, starting transfers between devices, onward(): return lax.ppermute(value, ('sess', 'blk'), pairs)  61.9 us
    ppermute x12, waiting for transfers between devices, onward(): return lax.ppermute(value, ('sess', 'blk'), pairs)  17.8 us
    pallas_call x11, Pallas kernels, call(): pl.pallas_call(body, out_shape=[jax.ShapeDtypeStruct((row_count, width),...  10.5 us
    ppermute x1, starting transfers between devices, shifted(): return lax.ppermute(value, axis, pairs)  4.92 us
  transfers between devices with their start and end apart: 13, of which 6 were waited for; matrix products, arithmetic and copies ran while one was open for 1% of the time, Pallas kernels for 9%

profile of v3, /device:TPU:88, one launch (start us, length us, event | category | flops | bytes accessed | tf_op | source)
XLA Modules:
  0.0 99.5 jit_solution(2574774264134070232)
XLA Ops:
  0.0 4.9 %collective-permute-start = (bf16[2,1,256,1024]{3,2,1,0:T(8,128)(2,1)}, bf16[2,1,256,1024]{3,2,1,0:T(8,128)(2,1)S(1)}, u32[]{:S(2)}, u32[]{:S(2)}) collective-permute-start(bf16[2,1,256,1024]{3,2,1,0:T(8,128)(2,1)} %param.8), channel_id=1, source_target_pairs={{0,256},{4,260},{8,264},{12,268},{16,272},{20,276},{24,280},{28,28... | collective-permute-start | bytes 3145736 | tf_op jit(solution)/shard_map/ppermute | solution.py:29
  4.9 1.0 fusion
  5.9 9.1 %collective-permute-start.4 = (bf16[16,4096]{1,0:T(8,128)(2,1)S(1)}, bf16[16,4096]{1,0:T(8,128)(2,1)S(1)}, u32[]{:S(2)}, u32[]{:S(2)}) collective-permute-start(bf16[16,4096]{1,0:T(8,128)(2,1)S(1)} %get-tuple-element.23.refs_1_), channel_id=1, source_target_pairs={{0,1},{1,2},{2,3},{3,0},{4,7},{5,4},{6,5},{7,6},{8,9},{9,10},{10,1... | collective-permute-start | bytes 393224 | tf_op jit(solution)/shard_map/ppermute | solution.py:230
  15.0 7.3 %collective-permute-start.1 = (bf16[16,4096]{1,0:T(8,128)(2,1)S(1)}, bf16[16,4096]{1,0:T(8,128)(2,1)S(1)}, u32[]{:S(2)}, u32[]{:S(2)}) collective-permute-start(bf16[16,4096]{1,0:T(8,128)(2,1)S(1)} %get-tuple-element.22.refs_0_), channel_id=1, source_target_pairs={{0,1},{1,2},{2,3},{3,0},{4,7},{5,4},{6,5},{7,6},{8,9},{9,10},{10,1... | collective-permute-start | bytes 393224 | tf_op jit(solution)/shard_map/ppermute | solution.py:230
  24.4 4.3 %collective-permute-start.5 = (bf16[16,4096]{1,0:T(8,128)(2,1)S(1)}, bf16[16,4096]{1,0:T(8,128)(2,1)S(1)}, u32[]{:S(2)}, u32[]{:S(2)}) collective-permute-start(bf16[16,4096]{1,0:T(8,128)(2,1)S(1)} %collective-permute-done.4.refs_1_), channel_id=1, source_target_pairs={{0,1},{1,2},{2,3},{3,0},{4,7},{5,4},{6,5},{7,6},{8,9},{9,10},{10,1... | collective-permute-start | bytes 393224 | tf_op jit(solution)/shard_map/ppermute | solution.py:230
  29.6 7.0 %collective-permute-start.2 = (bf16[16,4096]{1,0:T(8,128)(2,1)S(1)}, bf16[16,4096]{1,0:T(8,128)(2,1)S(1)}, u32[]{:S(2)}, u32[]{:S(2)}) collective-permute-start(bf16[16,4096]{1,0:T(8,128)(2,1)S(1)} %collective-permute-done.1.refs_0_), channel_id=1, source_target_pairs={{0,1},{1,2},{2,3},{3,0},{4,7},{5,4},{6,5},{7,6},{8,9},{9,10},{10,1... | collective-permute-start | bytes 393224 | tf_op jit(solution)/shard_map/ppermute | solution.py:230
  36.6 1.2 %copy-done = bf16[2,1,256,1024]{3,2,1,0:T(8,128)(2,1)S(1)} copy-done((bf16[2,1,256,1024]{3,2,1,0:T(8,128)(2,1)S(1)}, bf16[2,1,256,1024]{3,2,1,0:T(8,128)(2,1)}, u32[]{:S(2)}) %copy-start) | copy-done | bytes 1048600
  37.9 1.7 %attend_before.1 = (bf16[16,4224]{1,0:T(8,128)(2,1)S(1)}, bf16[16,4224]{1,0:T(8,128)(2,1)S(1)}) custom-call(s32[2]{0:T(128)S(1)} %pad_add_fusion.info_ref, s32[1,1]{1,0:T(1,128)S(6)} %copy.7.res_id_ref, s32[1,1]{1,0:T(1,128)S(6)} %copy.8.recv_id_ref, s32[1]{0:T(128)S(6)} %copy.9.length_ref, bf16[2,1,256,1024]{3,2,1,0:T(8,128)(2,1)S(1)} %copy-done, ...), custom_call_target="tpu_custom_call" | custom-call | flops 268435456 | bytes 2097152 | tf_op jit(solution)/shard_map/attend_before/pallas_call | solution.py:135
  39.5 6.8 %collective-permute-start.7 = (bf16[16,4224]{1,0:T(8,128)(2,1)S(1)}, bf16[16,4224]{1,0:T(8,128)(2,1)S(1)}, u32[]{:S(2)}, u32[]{:S(2)}) collective-permute-start(bf16[16,4224]{1,0:T(8,128)(2,1)S(1)} %get-tuple-element.21), channel_id=1, source_target_pairs={{0,1},{1,2},{2,3},{3,0},{4,7},{5,4},{6,5},{7,6},{8,9},{9,10},{10,1... | collective-permute-start | bytes 405512 | tf_op jit(solution)/shard_map/ppermute | solution.py:230
  46.3 4.1 %collective-permute-start.6 = (bf16[16,4224]{1,0:T(8,128)(2,1)S(1)}, bf16[16,4224]{1,0:T(8,128)(2,1)S(1)}, u32[]{:S(2)}, u32[]{:S(2)}) collective-permute-start(bf16[16,4224]{1,0:T(8,128)(2,1)S(1)} %get-tuple-element.18), channel_id=1, source_target_pairs={{0,1},{1,2},{2,3},{3,0},{4,7},{5,4},{6,5},{7,6},{8,9},{9,10},{10,1... | collective-permute-start | bytes 405512 | tf_op jit(solution)/shard_map/ppermute | solution.py:230
  50.5 1.9 %collective-permute-start.3 = (bf16[16,4096]{1,0:T(8,128)(2,1)S(1)}, bf16[16,4096]{1,0:T(8,128)(2,1)S(1)}, u32[]{:S(2)}, u32[]{:S(2)}) collective-permute-start(bf16[16,4096]{1,0:T(8,128)(2,1)S(1)} %collective-permute-done.2.refs_0_), channel_id=1, source_target_pairs={{0,1},{1,2},{2,3},{3,0},{4,7},{5,4},{6,5},{7,6},{8,9},{9,10},{10,1... | collective-permute-start | bytes 393224 | tf_op jit(solution)/shard_map/ppermute | solution.py:230
  52.4 1.7 %attend_far.1 = (bf16[16,4224]{1,0:T(8,128)(2,1)S(1)}, bf16[16,4224]{1,0:T(8,128)(2,1)S(1)}) custom-call(s32[2]{0:T(128)S(1)} %pad_add_fusion.info_ref, s32[1,1]{1,0:T(1,128)S(6)} %copy.7.res_id_ref, s32[1,1]{1,0:T(1,128)S(6)} %copy.8.recv_id_ref, s32[1]{0:T(128)S(6)} %copy.9.length_ref, bf16[2,1,256,1024]{3,2,1,0:T(8,128)(2,1)S(1)} %copy-done, ...), custom_call_target="tpu_custom_call" | custom-call | flops 268435456 | bytes 2097152 | tf_op jit(solution)/shard_map/attend_far/pallas_call | solution.py:135
  54.5 6.8 %collective-permute-start.8 = (bf16[16,4224]{1,0:T(8,128)(2,1)S(1)}, bf16[16,4224]{1,0:T(8,128)(2,1)S(1)}, u32[]{:S(2)}, u32[]{:S(2)}) collective-permute-start(bf16[16,4224]{1,0:T(8,128)(2,1)S(1)} %join_far_a.1), channel_id=1, source_target_pairs={{0,1},{1,2},{2,3},{3,0},{4,7},{5,4},{6,5},{7,6},{8,9},{9,10},{10,1... | collective-permute-start | bytes 405512 | tf_op jit(solution)/shard_map/ppermute | solution.py:230
  61.3 6.7 %collective-permute-start.10 = (bf16[16,4096]{1,0:T(8,128)(2,1)S(1)}, bf16[16,4096]{1,0:T(8,128)(2,1)S(1)}, u32[]{:S(2)}, u32[]{:S(2)}) collective-permute-start(bf16[16,4096]{1,0:T(8,128)(2,1)S(1)} %collective-permute-done.5.refs_1_), channel_id=1, source_target_pairs={{0,1},{1,2},{2,3},{3,0},{4,7},{5,4},{6,5},{7,6},{8,9},{9,10},{10,1... | collective-permute-start | bytes 393224 | tf_op jit(solution)/shard_map/ppermute | solution.py:230
  68.4 4.0 %collective-permute-start.11 = (bf16[16,4224]{1,0:T(8,128)(2,1)S(1)}, bf16[16,4224]{1,0:T(8,128)(2,1)S(1)}, u32[]{:S(2)}, u32[]{:S(2)}) collective-permute-start(bf16[16,4224]{1,0:T(8,128)(2,1)S(1)} %join_far_b.1), channel_id=1, source_target_pairs={{0,1},{1,2},{2,3},{3,0},{4,7},{5,4},{6,5},{7,6},{8,9},{9,10},{10,1... | collective-permute-start | bytes 405512 | tf_op jit(solution)/shard_map/ppermute | solution.py:230
  72.5 1.3 %attend_after_a.1.refs_0_ = bf16[16,4224]{1,0:T(8,128)(2,1)S(1)} custom-call(s32[2]{0:T(128)S(1)} %pad_add_fusion.info_ref, s32[1,1]{1,0:T(1,128)S(6)} %copy.7.res_id_ref, s32[1,1]{1,0:T(1,128)S(6)} %copy.8.recv_id_ref, s32[1]{0:T(128)S(6)} %copy.9.length_ref, bf16[2,1,256,1024]{3,2,1,0:T(8,128)(2,1)S(1)} %copy-done.1, ...), custom_call_target="tpu_custom_call" | custom-call | flops 134217728 | bytes 2097152 | tf_op jit(solution)/shard_map/attend_after_a/pallas_call | solution.py:135
  74.2 1.9 %collective-permute-start.9 = (bf16[16,4224]{1,0:T(8,128)(2,1)S(1)}, bf16[16,4224]{1,0:T(8,128)(2,1)S(1)}, u32[]{:S(2)}, u32[]{:S(2)}) collective-permute-start(bf16[16,4224]{1,0:T(8,128)(2,1)S(1)} %join_after_a.1), channel_id=1, source_target_pairs={{0,1},{1,2},{2,3},{3,0},{4,7},{5,4},{6,5},{7,6},{8,9},{9,10},{10,1... | collective-permute-start | bytes 405512 | tf_op jit(solution)/shard_map/ppermute | solution.py:230
  76.1 6.4 %collective-permute-done.10.refs_0_ = bf16[16,4096]{1,0:T(8,128)(2,1)S(1)} collective-permute-done((bf16[16,4096]{1,0:T(8,128)(2,1)S(1)}, bf16[16,4096]{1,0:T(8,128)(2,1)S(1)}, u32[]{:S(2)}, u32[]{:S(2)}) %collective-permute-start.10) | collective-permute-done | bytes 131104 | tf_op jit(solution)/shard_map/ppermute | solution.py:230
  82.5 1.3 %attend_after_b.1.refs_0_ = bf16[16,4224]{1,0:T(8,128)(2,1)S(1)} custom-call(s32[2]{0:T(128)S(1)} %pad_add_fusion.info_ref, s32[1,1]{1,0:T(1,128)S(6)} %copy.7.res_id_ref, s32[1,1]{1,0:T(1,128)S(6)} %copy.8.recv_id_ref, s32[1]{0:T(128)S(6)} %copy.9.length_ref, bf16[2,1,256,1024]{3,2,1,0:T(8,128)(2,1)S(1)} %copy-done.1, ...), custom_call_target="tpu_custom_call" | custom-call | flops 134217728 | bytes 2097152 | tf_op jit(solution)/shard_map/attend_after_b/pallas_call | solution.py:135
  83.8 3.2 %collective-permute-done.11.refs_1_ = bf16[16,4224]{1,0:T(8,128)(2,1)S(1)} collective-permute-done((bf16[16,4224]{1,0:T(8,128)(2,1)S(1)}, bf16[16,4224]{1,0:T(8,128)(2,1)S(1)}, u32[]{:S(2)}, u32[]{:S(2)}) %collective-permute-start.11) | collective-permute-done | bytes 135200 | tf_op jit(solution)/shard_map/ppermute | solution.py:230
  87.3 1.9 %collective-permute-start.12 = (bf16[16,4224]{1,0:T(8,128)(2,1)S(1)}, bf16[16,4224]{1,0:T(8,128)(2,1)S(1)}, u32[]{:S(2)}, u32[]{:S(2)}) collective-permute-start(bf16[16,4224]{1,0:T(8,128)(2,1)S(1)} %join_after_b.1), channel_id=1, source_target_pairs={{0,1},{1,2},{2,3},{3,0},{4,7},{5,4},{6,5},{7,6},{8,9},{9,10},{10,1... | collective-permute-start | bytes 405512 | tf_op jit(solution)/shard_map/ppermute | solution.py:230
  89.9 1.7 %attend_own.1 = (bf16[16,4224]{1,0:T(8,128)(2,1)S(1)}, bf16[16,4224]{1,0:T(8,128)(2,1)S(1)}) custom-call(s32[2]{0:T(128)S(1)} %pad_add_fusion.info_ref, s32[1,1]{1,0:T(1,128)S(6)} %copy.7.res_id_ref, s32[1,1]{1,0:T(1,128)S(6)} %copy.8.recv_id_ref, s32[1]{0:T(128)S(6)} %copy.9.length_ref, bf16[2,1,256,1024]{3,2,1,0:T(8,128)(2,1)S(1)} %copy-done.1, ...), custom_call_target="tpu_custom_call" | custom-call | flops 268435456 | bytes 2097152 | tf_op jit(solution)/shard_map/attend_own/pallas_call | solution.py:135
  91.9 6.6 %collective-permute-done.12.sum_ref = bf16[16,4224]{1,0:T(8,128)(2,1)S(1)} collective-permute-done((bf16[16,4224]{1,0:T(8,128)(2,1)S(1)}, bf16[16,4224]{1,0:T(8,128)(2,1)S(1)}, u32[]{:S(2)}, u32[]{:S(2)}) %collective-permute-start.12) | collective-permute-done | bytes 135200 | tf_op jit(solution)/shard_map/ppermute | solution.py:230
  98.5 1.0 %join_home.1 = bf16[16,8192]{1,0:T(8,128)(2,1)} custom-call(bf16[16,4096]{1,0:T(8,128)(2,1)S(1)} %join_part.1.done_ref, bf16[16,4224]{1,0:T(8,128)(2,1)S(1)} %get-tuple-element.26.own_ref, bf16[16,4224]{1,0:T(8,128)(2,1)S(1)} %collective-permute-done.12.sum_ref), custom_call_target="tpu_custom_call" | custom-call | flops 524288 | bytes 786432 | tf_op jit(solution)/shard_map/join_home/pallas_call | solution.py:135
  (19 shorter events, 3.4 us)
Async XLA Ops:
  0.0 36.6 %collective-permute-start = (bf16[2,1,256,1024]{3,2,1,0:T(8,128)(2,1)}, bf16[2,1,256,1024]{3,2,1,0:T(8,128)(2,1)S(1)}, u32[]{:S(2)}, u32[]{:S(2)}) collective-permute-start(bf16[2,1,256,1024]{3,2,1,0:T(8,128)(2,1)} %param.8), channel_id=1, source_target_pairs={{0,256},{4,260},{8,264},{12,268},{16,272},{20,276},{24,280},{28,28... | collective-permute-start | bytes 3145736 | tf_op jit(solution)/shard_map/ppermute | solution.py:29
  5.9 18.4 %collective-permute-start.4 = (bf16[16,4096]{1,0:T(8,128)(2,1)S(1)}, bf16[16,4096]{1,0:T(8,128)(2,1)S(1)}, u32[]{:S(2)}, u32[]{:S(2)}) collective-permute-start(bf16[16,4096]{1,0:T(8,128)(2,1)S(1)} %get-tuple-element.23.refs_1_), channel_id=1, source_target_pairs={{0,1},{1,2},{2,3},{3,0},{4,7},{5,4},{6,5},{7,6},{8,9},{9,10},{10,1... | collective-permute-start | bytes 393224 | tf_op jit(solution)/shard_map/ppermute | solution.py:230
  15.0 14.6 %collective-permute-start.1 = (bf16[16,4096]{1,0:T(8,128)(2,1)S(1)}, bf16[16,4096]{1,0:T(8,128)(2,1)S(1)}, u32[]{:S(2)}, u32[]{:S(2)}) collective-permute-start(bf16[16,4096]{1,0:T(8,128)(2,1)S(1)} %get-tuple-element.22.refs_0_), channel_id=1, source_target_pairs={{0,1},{1,2},{2,3},{3,0},{4,7},{5,4},{6,5},{7,6},{8,9},{9,10},{10,1... | collective-permute-start | bytes 393224 | tf_op jit(solution)/shard_map/ppermute | solution.py:230
  24.4 28.1 %collective-permute-start.5 = (bf16[16,4096]{1,0:T(8,128)(2,1)S(1)}, bf16[16,4096]{1,0:T(8,128)(2,1)S(1)}, u32[]{:S(2)}, u32[]{:S(2)}) collective-permute-start(bf16[16,4096]{1,0:T(8,128)(2,1)S(1)} %collective-permute-done.4.refs_1_), channel_id=1, source_target_pairs={{0,1},{1,2},{2,3},{3,0},{4,7},{5,4},{6,5},{7,6},{8,9},{9,10},{10,1... | collective-permute-start | bytes 393224 | tf_op jit(solution)/shard_map/ppermute | solution.py:230
  29.6 20.9 %collective-permute-start.2 = (bf16[16,4096]{1,0:T(8,128)(2,1)S(1)}, bf16[16,4096]{1,0:T(8,128)(2,1)S(1)}, u32[]{:S(2)}, u32[]{:S(2)}) collective-permute-start(bf16[16,4096]{1,0:T(8,128)(2,1)S(1)} %collective-permute-done.1.refs_0_), channel_id=1, source_target_pairs={{0,1},{1,2},{2,3},{3,0},{4,7},{5,4},{6,5},{7,6},{8,9},{9,10},{10,1... | collective-permute-start | bytes 393224 | tf_op jit(solution)/shard_map/ppermute | solution.py:230
  36.6 1.2 %copy-start = (bf16[2,1,256,1024]{3,2,1,0:T(8,128)(2,1)S(1)}, bf16[2,1,256,1024]{3,2,1,0:T(8,128)(2,1)}, u32[]{:S(2)}) copy-start(bf16[2,1,256,1024]{3,2,1,0:T(8,128)(2,1)} %res_ref.9) | copy-start | bytes 3145732
  39.5 14.6 %collective-permute-start.7 = (bf16[16,4224]{1,0:T(8,128)(2,1)S(1)}, bf16[16,4224]{1,0:T(8,128)(2,1)S(1)}, u32[]{:S(2)}, u32[]{:S(2)}) collective-permute-start(bf16[16,4224]{1,0:T(8,128)(2,1)S(1)} %get-tuple-element.21), channel_id=1, source_target_pairs={{0,1},{1,2},{2,3},{3,0},{4,7},{5,4},{6,5},{7,6},{8,9},{9,10},{10,1... | collective-permute-start | bytes 405512 | tf_op jit(solution)/shard_map/ppermute | solution.py:230
  46.3 26.1 %copy-start.1 = (bf16[2,1,256,1024]{3,2,1,0:T(8,128)(2,1)S(1)}, bf16[2,1,256,1024]{3,2,1,0:T(8,128)(2,1)}, u32[]{:S(2)}) copy-start(bf16[2,1,256,1024]{3,2,1,0:T(8,128)(2,1)} %res_ref.9) | copy-start | bytes 3145732
  46.3 21.7 %collective-permute-start.6 = (bf16[16,4224]{1,0:T(8,128)(2,1)S(1)}, bf16[16,4224]{1,0:T(8,128)(2,1)S(1)}, u32[]{:S(2)}, u32[]{:S(2)}) collective-permute-start(bf16[16,4224]{1,0:T(8,128)(2,1)S(1)} %get-tuple-element.18), channel_id=1, source_target_pairs={{0,1},{1,2},{2,3},{3,0},{4,7},{5,4},{6,5},{7,6},{8,9},{9,10},{10,1... | collective-permute-start | bytes 405512 | tf_op jit(solution)/shard_map/ppermute | solution.py:230
  50.5 22.0 %collective-permute-start.3 = (bf16[16,4096]{1,0:T(8,128)(2,1)S(1)}, bf16[16,4096]{1,0:T(8,128)(2,1)S(1)}, u32[]{:S(2)}, u32[]{:S(2)}) collective-permute-start(bf16[16,4096]{1,0:T(8,128)(2,1)S(1)} %collective-permute-done.2.refs_0_), channel_id=1, source_target_pairs={{0,1},{1,2},{2,3},{3,0},{4,7},{5,4},{6,5},{7,6},{8,9},{9,10},{10,1... | collective-permute-start | bytes 393224 | tf_op jit(solution)/shard_map/ppermute | solution.py:230
  54.5 19.3 %collective-permute-start.8 = (bf16[16,4224]{1,0:T(8,128)(2,1)S(1)}, bf16[16,4224]{1,0:T(8,128)(2,1)S(1)}, u32[]{:S(2)}, u32[]{:S(2)}) collective-permute-start(bf16[16,4224]{1,0:T(8,128)(2,1)S(1)} %join_far_a.1), channel_id=1, source_target_pairs={{0,1},{1,2},{2,3},{3,0},{4,7},{5,4},{6,5},{7,6},{8,9},{9,10},{10,1... | collective-permute-start | bytes 405512 | tf_op jit(solution)/shard_map/ppermute | solution.py:230
  61.3 21.2 %collective-permute-start.10 = (bf16[16,4096]{1,0:T(8,128)(2,1)S(1)}, bf16[16,4096]{1,0:T(8,128)(2,1)S(1)}, u32[]{:S(2)}, u32[]{:S(2)}) collective-permute-start(bf16[16,4096]{1,0:T(8,128)(2,1)S(1)} %collective-permute-done.5.refs_1_), channel_id=1, source_target_pairs={{0,1},{1,2},{2,3},{3,0},{4,7},{5,4},{6,5},{7,6},{8,9},{9,10},{10,1... | collective-permute-start | bytes 393224 | tf_op jit(solution)/shard_map/ppermute | solution.py:230
  68.4 18.5 %collective-permute-start.11 = (bf16[16,4224]{1,0:T(8,128)(2,1)S(1)}, bf16[16,4224]{1,0:T(8,128)(2,1)S(1)}, u32[]{:S(2)}, u32[]{:S(2)}) collective-permute-start(bf16[16,4224]{1,0:T(8,128)(2,1)S(1)} %join_far_b.1), channel_id=1, source_target_pairs={{0,1},{1,2},{2,3},{3,0},{4,7},{5,4},{6,5},{7,6},{8,9},{9,10},{10,1... | collective-permute-start | bytes 405512 | tf_op jit(solution)/shard_map/ppermute | solution.py:230
  74.2 15.7 %collective-permute-start.9 = (bf16[16,4224]{1,0:T(8,128)(2,1)S(1)}, bf16[16,4224]{1,0:T(8,128)(2,1)S(1)}, u32[]{:S(2)}, u32[]{:S(2)}) collective-permute-start(bf16[16,4224]{1,0:T(8,128)(2,1)S(1)} %join_after_a.1), channel_id=1, source_target_pairs={{0,1},{1,2},{2,3},{3,0},{4,7},{5,4},{6,5},{7,6},{8,9},{9,10},{10,1... | collective-permute-start | bytes 405512 | tf_op jit(solution)/shard_map/ppermute | solution.py:230
  87.3 11.2 %collective-permute-start.12 = (bf16[16,4224]{1,0:T(8,128)(2,1)S(1)}, bf16[16,4224]{1,0:T(8,128)(2,1)S(1)}, u32[]{:S(2)}, u32[]{:S(2)}) collective-permute-start(bf16[16,4224]{1,0:T(8,128)(2,1)S(1)} %join_after_b.1), channel_id=1, source_target_pairs={{0,1},{1,2},{2,3},{3,0},{4,7},{5,4},{6,5},{7,6},{8,9},{9,10},{10,1... | collective-permute-start | bytes 405512 | tf_op jit(solution)/shard_map/ppermute | solution.py:230

commit v4 on v3

--- a/solution.py
+++ b/solution.py
@@ -23,10 +23,28 @@
 SMEM = pl.BlockSpec(memory_space=pltpu.SMEM)
 
 
-def shifted(value, axis, steps):
-    count = lax.axis_size(axis)
-    pairs = [(source, (source + steps) % count) for source in range(count)]
-    return lax.ppermute(value, axis, pairs)
+def half_way(value):
+    count = lax.axis_size("sess")
+    return lax.ppermute(value, "sess", [(s, (s + count // 2) % count) for s in range(count)])
+
+
+def load_body(in_ref, out_ref, sem):
+    copy = pltpu.make_async_copy(in_ref, out_ref, sem)
+    copy.start()
+    copy.wait()
+
+
+def load(value):
+    return pl.pallas_call(
+        load_body,
+        out_shape=jax.ShapeDtypeStruct(value.shape, value.dtype),
+        in_specs=[pl.BlockSpec(memory_space=pl.ANY)],
+        out_specs=VMEM,
+        scratch_shapes=[pltpu.SemaphoreType.DMA],
+        compiler_params=pltpu.CompilerParams(vmem_limit_bytes=16 * 1024 * 1024),
+        cost_estimate=pl.CostEstimate(flops=0, bytes_accessed=2 * value.size * 2, transcendentals=0),
+        name="load",
+    )(value)
 
 
 def split_three(value):
@@ -67,13 +85,14 @@
     ]
 
 
-def attend_body(loop, distance, counts, info_ref, res_id_ref, recv_id_ref, length_ref, res_ref, mig_ref, *refs):
+def attend_body(loop, distance, counts, res_id_ref, recv_id_ref, length_ref, res_ref, mig_ref, *refs):
     query_counts, packet_counts, forward, base = counts
     query_refs = refs[: len(query_counts)]
     out_refs = refs[len(query_counts) :]
     packet_refs = sections(out_refs[0]) if out_refs[0].shape[1] > HEADS * HEAD else out_refs
     row_count = query_refs[0].shape[0]
-    anchor = lax.rem(info_ref[0] + distance * info_ref[1], loop)
+    way = 2 * lax.rem(lax.div(lax.axis_index("sess"), 2), 2) - 1
+    anchor = lax.rem(lax.axis_index("blk") + loop + distance * way, loop)
     start = length_ref[0] - QROWS + anchor * row_count
     row = lax.broadcasted_iota(jnp.int32, (row_count, BLOCK), 0)
     token = lax.broadcasted_iota(jnp.int32, (row_count, BLOCK), 1)
@@ -223,7 +242,7 @@
 def onward(value):
     sessions, loop = lax.axis_size("sess"), lax.axis_size("blk")
     pairs = [
-        (s * loop + b, s * loop + (b + (1 if s % 2 == 0 else -1)) % loop)
+        (s * loop + b, s * loop + (b + (-1 if s // 2 % 2 == 0 else 1)) % loop)
         for s in range(sessions)
         for b in range(loop)
     ]
@@ -232,14 +251,13 @@
 
 def per_device(queries, res_cache, mig_cache, res_ids, recv_ids, lengths):
     loop = lax.axis_size("blk")
-    way = 1 - 2 * lax.rem(lax.axis_index("sess"), 2)
-    info = jnp.stack([lax.axis_index("blk") + loop, way]).astype(jnp.int32)
-    scalars = (info, res_ids, recv_ids, lengths)
+    scalars = (res_ids, recv_ids, lengths)
     mine = queries[0]
     mine = tuple(
         mine[:, first * GROUP * HEAD : last * GROUP * HEAD] for first, last in PARTS
     )
-    arrived = shifted(mig_cache, "sess", lax.axis_size("sess") // 2)
+    arrived = half_way(mig_cache)
+    res_cache = load(res_cache)
     run = functools.partial(attend, loop, scalars, res_cache, arrived)
     before = tuple(onward(part) for part in mine)
     far_a, far_b = tuple(onward(part) for part in before)

time: 100 us -> 98.5 us (0.985)
  the two profiles are of different devices: /device:TPU:88 before, /device:TPU:20 now
where the time goes in v4:
time: 98.5 us; the launch traced here: 97.9 us
  starting transfers between devices  67.5 us (69%)
  waiting for transfers between devices  18.1 us (18%)
  Pallas kernels  7.97 us (8%)
  local copies, waits for them, and re-layouts  2.21 us (2%)
  between operations  2.16 us (2%)
    ppermute x12, starting transfers between devices, onward(): return lax.ppermute(value, ('sess', 'blk'), pairs)  65.1 us
    ppermute x12, waiting for transfers between devices, onward(): return lax.ppermute(value, ('sess', 'blk'), pairs)  18.1 us
    pallas_call x11, Pallas kernels, call(): pl.pallas_call(body, out_shape=[jax.ShapeDtypeStruct((row_count, width),...  7.89 us
    ppermute x1, starting transfers between devices, half_way(): lax.ppermute(value, 'sess', [(s, (s + count // 2) % count) for s in range...  2.4 us
  transfers between devices with their start and end apart: 13, of which 5 were waited for; matrix products, arithmetic and copies ran while one was open for 1% of the time, Pallas kernels for 7%

profile of v4, /device:TPU:20, one launch (start us, length us, event | category | flops | bytes accessed | tf_op | source)
XLA Modules:
  0.0 97.9 jit_solution(4380392916423178053)
XLA Ops:
  0.0 2.4 %collective-permute-start = (bf16[2,1,256,1024]{3,2,1,0:T(8,128)(2,1)}, bf16[2,1,256,1024]{3,2,1,0:T(8,128)(2,1)S(1)}, u32[]{:S(2)}, u32[]{:S(2)}) collective-permute-start(bf16[2,1,256,1024]{3,2,1,0:T(8,128)(2,1)} %param.8), channel_id=1, source_target_pairs={{0,256},{4,260},{8,264},{12,268},{16,272},{20,276},{24,280},{28,28... | collective-permute-start | bytes 3145736 | tf_op jit(solution)/shard_map/ppermute | solution.py:28
  2.4 1.0 %fusion = (bf16[16,4096]{1,0:T(8,128)(2,1)S(1)}, bf16[16,4096]{1,0:T(8,128)(2,1)S(1)}) fusion(bf16[16,8192]{1,0:T(8,128)(2,1)} %bitcast.2), kind=kLoop, calls=%fused_computation | loop fusion | bytes 524288 | tf_op jit(solution)/shard_map/slice | solution.py:257
  3.4 12.7 %collective-permute-start.4 = (bf16[16,4096]{1,0:T(8,128)(2,1)S(1)}, bf16[16,4096]{1,0:T(8,128)(2,1)S(1)}, u32[]{:S(2)}, u32[]{:S(2)}) collective-permute-start(bf16[16,4096]{1,0:T(8,128)(2,1)S(1)} %get-tuple-element.23.refs_1_), channel_id=1, source_target_pairs={{0,3},{1,0},{2,1},{3,2},{4,7},{5,4},{6,5},{7,6},{8,9},{9,10},{10,1... | collective-permute-start | bytes 393224 | tf_op jit(solution)/shard_map/ppermute | solution.py:249
  16.1 5.5 %collective-permute-start.1 = (bf16[16,4096]{1,0:T(8,128)(2,1)S(1)}, bf16[16,4096]{1,0:T(8,128)(2,1)S(1)}, u32[]{:S(2)}, u32[]{:S(2)}) collective-permute-start(bf16[16,4096]{1,0:T(8,128)(2,1)S(1)} %get-tuple-element.22.refs_0_), channel_id=1, source_target_pairs={{0,3},{1,0},{2,1},{3,2},{4,7},{5,4},{6,5},{7,6},{8,9},{9,10},{10,1... | collective-permute-start | bytes 393224 | tf_op jit(solution)/shard_map/ppermute | solution.py:249
  23.6 1.2 %copy-done = bf16[2,1,256,1024]{3,2,1,0:T(8,128)(2,1)S(1)} copy-done((bf16[2,1,256,1024]{3,2,1,0:T(8,128)(2,1)S(1)}, bf16[2,1,256,1024]{3,2,1,0:T(8,128)(2,1)}, u32[]{:S(2)}) %copy-start) | copy-done | bytes 1048600
  24.9 5.3 %collective-permute-start.5 = (bf16[16,4096]{1,0:T(8,128)(2,1)S(1)}, bf16[16,4096]{1,0:T(8,128)(2,1)S(1)}, u32[]{:S(2)}, u32[]{:S(2)}) collective-permute-start(bf16[16,4096]{1,0:T(8,128)(2,1)S(1)} %collective-permute-done.4.refs_1_), channel_id=1, source_target_pairs={{0,3},{1,0},{2,1},{3,2},{4,7},{5,4},{6,5},{7,6},{8,9},{9,10},{10,1... | collective-permute-start | bytes 393224 | tf_op jit(solution)/shard_map/ppermute | solution.py:249
  30.2 7.1 %collective-permute-start.2 = (bf16[16,4096]{1,0:T(8,128)(2,1)S(1)}, bf16[16,4096]{1,0:T(8,128)(2,1)S(1)}, u32[]{:S(2)}, u32[]{:S(2)}) collective-permute-start(bf16[16,4096]{1,0:T(8,128)(2,1)S(1)} %collective-permute-done.1.refs_0_), channel_id=1, source_target_pairs={{0,3},{1,0},{2,1},{3,2},{4,7},{5,4},{6,5},{7,6},{8,9},{9,10},{10,1... | collective-permute-start | bytes 393224 | tf_op jit(solution)/shard_map/ppermute | solution.py:249
  37.3 1.2 %attend_before.1 = (bf16[16,4224]{1,0:T(8,128)(2,1)S(1)}, bf16[16,4224]{1,0:T(8,128)(2,1)S(1)}) custom-call(s32[1,1]{1,0:T(1,128)S(6)} %copy.7.res_id_ref, s32[1,1]{1,0:T(1,128)S(6)} %copy.8.recv_id_ref, s32[1]{0:T(128)S(6)} %copy.9.length_ref, bf16[2,1,256,1024]{3,2,1,0:T(8,128)(2,1)S(1)} %load.1.res_ref, ...), custom_call_target="tpu_custom_call" | custom-call | flops 268435456 | bytes 2097152 | tf_op jit(solution)/shard_map/attend_before/pallas_call | solution.py:154
  38.5 4.1 %collective-permute-start.7 = (bf16[16,4224]{1,0:T(8,128)(2,1)S(1)}, bf16[16,4224]{1,0:T(8,128)(2,1)S(1)}, u32[]{:S(2)}, u32[]{:S(2)}) collective-permute-start(bf16[16,4224]{1,0:T(8,128)(2,1)S(1)} %get-tuple-element.21), channel_id=1, source_target_pairs={{0,3},{1,0},{2,1},{3,2},{4,7},{5,4},{6,5},{7,6},{8,9},{9,10},{10,1... | collective-permute-start | bytes 405512 | tf_op jit(solution)/shard_map/ppermute | solution.py:249
  42.6 5.2 %collective-permute-start.6 = (bf16[16,4224]{1,0:T(8,128)(2,1)S(1)}, bf16[16,4224]{1,0:T(8,128)(2,1)S(1)}, u32[]{:S(2)}, u32[]{:S(2)}) collective-permute-start(bf16[16,4224]{1,0:T(8,128)(2,1)S(1)} %get-tuple-element.18), channel_id=1, source_target_pairs={{0,3},{1,0},{2,1},{3,2},{4,7},{5,4},{6,5},{7,6},{8,9},{9,10},{10,1... | collective-permute-start | bytes 405512 | tf_op jit(solution)/shard_map/ppermute | solution.py:249
  47.9 3.1 %collective-permute-start.3 = (bf16[16,4096]{1,0:T(8,128)(2,1)S(1)}, bf16[16,4096]{1,0:T(8,128)(2,1)S(1)}, u32[]{:S(2)}, u32[]{:S(2)}) collective-permute-start(bf16[16,4096]{1,0:T(8,128)(2,1)S(1)} %collective-permute-done.2.refs_0_), channel_id=1, source_target_pairs={{0,3},{1,0},{2,1},{3,2},{4,7},{5,4},{6,5},{7,6},{8,9},{9,10},{10,1... | collective-permute-start | bytes 393224 | tf_op jit(solution)/shard_map/ppermute | solution.py:249
  51.0 1.2 %attend_far.1 = (bf16[16,4224]{1,0:T(8,128)(2,1)S(1)}, bf16[16,4224]{1,0:T(8,128)(2,1)S(1)}) custom-call(s32[1,1]{1,0:T(1,128)S(6)} %copy.7.res_id_ref, s32[1,1]{1,0:T(1,128)S(6)} %copy.8.recv_id_ref, s32[1]{0:T(128)S(6)} %copy.9.length_ref, bf16[2,1,256,1024]{3,2,1,0:T(8,128)(2,1)S(1)} %load.1.res_ref, ...), custom_call_target="tpu_custom_call" | custom-call | flops 268435456 | bytes 2097152 | tf_op jit(solution)/shard_map/attend_far/pallas_call | solution.py:154
  52.9 6.7 %collective-permute-start.8 = (bf16[16,4224]{1,0:T(8,128)(2,1)S(1)}, bf16[16,4224]{1,0:T(8,128)(2,1)S(1)}, u32[]{:S(2)}, u32[]{:S(2)}) collective-permute-start(bf16[16,4224]{1,0:T(8,128)(2,1)S(1)} %join_far_a.1), channel_id=1, source_target_pairs={{0,3},{1,0},{2,1},{3,2},{4,7},{5,4},{6,5},{7,6},{8,9},{9,10},{10,1... | collective-permute-start | bytes 405512 | tf_op jit(solution)/shard_map/ppermute | solution.py:249
  59.6 4.1 %collective-permute-start.10 = (bf16[16,4096]{1,0:T(8,128)(2,1)S(1)}, bf16[16,4096]{1,0:T(8,128)(2,1)S(1)}, u32[]{:S(2)}, u32[]{:S(2)}) collective-permute-start(bf16[16,4096]{1,0:T(8,128)(2,1)S(1)} %collective-permute-done.5.refs_1_), channel_id=1, source_target_pairs={{0,3},{1,0},{2,1},{3,2},{4,7},{5,4},{6,5},{7,6},{8,9},{9,10},{10,1... | collective-permute-start | bytes 393224 | tf_op jit(solution)/shard_map/ppermute | solution.py:249
  64.1 5.2 %collective-permute-start.11 = (bf16[16,4224]{1,0:T(8,128)(2,1)S(1)}, bf16[16,4224]{1,0:T(8,128)(2,1)S(1)}, u32[]{:S(2)}, u32[]{:S(2)}) collective-permute-start(bf16[16,4224]{1,0:T(8,128)(2,1)S(1)} %join_far_b.1), channel_id=1, source_target_pairs={{0,3},{1,0},{2,1},{3,2},{4,7},{5,4},{6,5},{7,6},{8,9},{9,10},{10,1... | collective-permute-start | bytes 405512 | tf_op jit(solution)/shard_map/ppermute | solution.py:249
  70.1 1.3 %collective-permute-done.8.refs_1_ = bf16[16,4224]{1,0:T(8,128)(2,1)S(1)} collective-permute-done((bf16[16,4224]{1,0:T(8,128)(2,1)S(1)}, bf16[16,4224]{1,0:T(8,128)(2,1)S(1)}, u32[]{:S(2)}, u32[]{:S(2)}) %collective-permute-start.8) | collective-permute-done | bytes 135200 | tf_op jit(solution)/shard_map/ppermute | solution.py:249
  71.8 4.1 %collective-permute-start.9 = (bf16[16,4224]{1,0:T(8,128)(2,1)S(1)}, bf16[16,4224]{1,0:T(8,128)(2,1)S(1)}, u32[]{:S(2)}, u32[]{:S(2)}) collective-permute-start(bf16[16,4224]{1,0:T(8,128)(2,1)S(1)} %join_after_a.1), channel_id=1, source_target_pairs={{0,3},{1,0},{2,1},{3,2},{4,7},{5,4},{6,5},{7,6},{8,9},{9,10},{10,1... | collective-permute-start | bytes 405512 | tf_op jit(solution)/shard_map/ppermute | solution.py:249
  76.0 2.0 %collective-permute-done.10.refs_0_ = bf16[16,4096]{1,0:T(8,128)(2,1)S(1)} collective-permute-done((bf16[16,4096]{1,0:T(8,128)(2,1)S(1)}, bf16[16,4096]{1,0:T(8,128)(2,1)S(1)}, u32[]{:S(2)}, u32[]{:S(2)}) %collective-permute-start.10) | collective-permute-done | bytes 131104 | tf_op jit(solution)/shard_map/ppermute | solution.py:249
  78.0 0.8 attend_after_b.1.refs_0_
  78.8 7.0 %collective-permute-done.11.refs_1_ = bf16[16,4224]{1,0:T(8,128)(2,1)S(1)} collective-permute-done((bf16[16,4224]{1,0:T(8,128)(2,1)S(1)}, bf16[16,4224]{1,0:T(8,128)(2,1)S(1)}, u32[]{:S(2)}, u32[]{:S(2)}) %collective-permute-start.11) | collective-permute-done | bytes 135200 | tf_op jit(solution)/shard_map/ppermute | solution.py:249
  86.1 1.9 %collective-permute-start.12 = (bf16[16,4224]{1,0:T(8,128)(2,1)S(1)}, bf16[16,4224]{1,0:T(8,128)(2,1)S(1)}, u32[]{:S(2)}, u32[]{:S(2)}) collective-permute-start(bf16[16,4224]{1,0:T(8,128)(2,1)S(1)} %join_after_b.1), channel_id=1, source_target_pairs={{0,3},{1,0},{2,1},{3,2},{4,7},{5,4},{6,5},{7,6},{8,9},{9,10},{10,1... | collective-permute-start | bytes 405512 | tf_op jit(solution)/shard_map/ppermute | solution.py:249
  88.0 1.2 %attend_own.1 = (bf16[16,4224]{1,0:T(8,128)(2,1)S(1)}, bf16[16,4224]{1,0:T(8,128)(2,1)S(1)}) custom-call(s32[1,1]{1,0:T(1,128)S(6)} %copy.7.res_id_ref, s32[1,1]{1,0:T(1,128)S(6)} %copy.8.recv_id_ref, s32[1]{0:T(128)S(6)} %copy.9.length_ref, bf16[2,1,256,1024]{3,2,1,0:T(8,128)(2,1)S(1)} %load.1.res_ref, ...), custom_call_target="tpu_custom_call" | custom-call | flops 268435456 | bytes 2097152 | tf_op jit(solution)/shard_map/attend_own/pallas_call | solution.py:154
  89.6 7.3 %collective-permute-done.12.sum_ref = bf16[16,4224]{1,0:T(8,128)(2,1)S(1)} collective-permute-done((bf16[16,4224]{1,0:T(8,128)(2,1)S(1)}, bf16[16,4224]{1,0:T(8,128)(2,1)S(1)}, u32[]{:S(2)}, u32[]{:S(2)}) %collective-permute-start.12) | collective-permute-done | bytes 135200 | tf_op jit(solution)/shard_map/ppermute | solution.py:249
  96.9 1.0 %join_home.1 = bf16[16,8192]{1,0:T(8,128)(2,1)} custom-call(bf16[16,4096]{1,0:T(8,128)(2,1)S(1)} %join_part.1.done_ref, bf16[16,4224]{1,0:T(8,128)(2,1)S(1)} %get-tuple-element.26.own_ref, bf16[16,4224]{1,0:T(8,128)(2,1)S(1)} %collective-permute-done.12.sum_ref), custom_call_target="tpu_custom_call" | custom-call | flops 524288 | bytes 786432 | tf_op jit(solution)/shard_map/join_home/pallas_call | solution.py:154
  (17 shorter events, 3.0 us)
Async XLA Ops:
  0.0 37.3 %collective-permute-start = (bf16[2,1,256,1024]{3,2,1,0:T(8,128)(2,1)}, bf16[2,1,256,1024]{3,2,1,0:T(8,128)(2,1)S(1)}, u32[]{:S(2)}, u32[]{:S(2)}) collective-permute-start(bf16[2,1,256,1024]{3,2,1,0:T(8,128)(2,1)} %param.8), channel_id=1, source_target_pairs={{0,256},{4,260},{8,264},{12,268},{16,272},{20,276},{24,280},{28,28... | collective-permute-start | bytes 3145736 | tf_op jit(solution)/shard_map/ppermute | solution.py:28
  3.4 21.5 %collective-permute-start.4 = (bf16[16,4096]{1,0:T(8,128)(2,1)S(1)}, bf16[16,4096]{1,0:T(8,128)(2,1)S(1)}, u32[]{:S(2)}, u32[]{:S(2)}) collective-permute-start(bf16[16,4096]{1,0:T(8,128)(2,1)S(1)} %get-tuple-element.23.refs_1_), channel_id=1, source_target_pairs={{0,3},{1,0},{2,1},{3,2},{4,7},{5,4},{6,5},{7,6},{8,9},{9,10},{10,1... | collective-permute-start | bytes 393224 | tf_op jit(solution)/shard_map/ppermute | solution.py:249
  16.1 14.1 %collective-permute-start.1 = (bf16[16,4096]{1,0:T(8,128)(2,1)S(1)}, bf16[16,4096]{1,0:T(8,128)(2,1)S(1)}, u32[]{:S(2)}, u32[]{:S(2)}) collective-permute-start(bf16[16,4096]{1,0:T(8,128)(2,1)S(1)} %get-tuple-element.22.refs_0_), channel_id=1, source_target_pairs={{0,3},{1,0},{2,1},{3,2},{4,7},{5,4},{6,5},{7,6},{8,9},{9,10},{10,1... | collective-permute-start | bytes 393224 | tf_op jit(solution)/shard_map/ppermute | solution.py:249
  23.6 1.2 %copy-start = (bf16[2,1,256,1024]{3,2,1,0:T(8,128)(2,1)S(1)}, bf16[2,1,256,1024]{3,2,1,0:T(8,128)(2,1)}, u32[]{:S(2)}) copy-start(bf16[2,1,256,1024]{3,2,1,0:T(8,128)(2,1)} %in_ref.1) | copy-start | bytes 3145732
  24.9 26.1 %collective-permute-start.5 = (bf16[16,4096]{1,0:T(8,128)(2,1)S(1)}, bf16[16,4096]{1,0:T(8,128)(2,1)S(1)}, u32[]{:S(2)}, u32[]{:S(2)}) collective-permute-start(bf16[16,4096]{1,0:T(8,128)(2,1)S(1)} %collective-permute-done.4.refs_1_), channel_id=1, source_target_pairs={{0,3},{1,0},{2,1},{3,2},{4,7},{5,4},{6,5},{7,6},{8,9},{9,10},{10,1... | collective-permute-start | bytes 393224 | tf_op jit(solution)/shard_map/ppermute | solution.py:249
  30.2 17.7 %collective-permute-start.2 = (bf16[16,4096]{1,0:T(8,128)(2,1)S(1)}, bf16[16,4096]{1,0:T(8,128)(2,1)S(1)}, u32[]{:S(2)}, u32[]{:S(2)}) collective-permute-start(bf16[16,4096]{1,0:T(8,128)(2,1)S(1)} %collective-permute-done.1.refs_0_), channel_id=1, source_target_pairs={{0,3},{1,0},{2,1},{3,2},{4,7},{5,4},{6,5},{7,6},{8,9},{9,10},{10,1... | collective-permute-start | bytes 393224 | tf_op jit(solution)/shard_map/ppermute | solution.py:249
  38.5 14.1 %collective-permute-start.7 = (bf16[16,4224]{1,0:T(8,128)(2,1)S(1)}, bf16[16,4224]{1,0:T(8,128)(2,1)S(1)}, u32[]{:S(2)}, u32[]{:S(2)}) collective-permute-start(bf16[16,4224]{1,0:T(8,128)(2,1)S(1)} %get-tuple-element.21), channel_id=1, source_target_pairs={{0,3},{1,0},{2,1},{3,2},{4,7},{5,4},{6,5},{7,6},{8,9},{9,10},{10,1... | collective-permute-start | bytes 405512 | tf_op jit(solution)/shard_map/ppermute | solution.py:249
  42.6 21.1 %collective-permute-start.6 = (bf16[16,4224]{1,0:T(8,128)(2,1)S(1)}, bf16[16,4224]{1,0:T(8,128)(2,1)S(1)}, u32[]{:S(2)}, u32[]{:S(2)}) collective-permute-start(bf16[16,4224]{1,0:T(8,128)(2,1)S(1)} %get-tuple-element.18), channel_id=1, source_target_pairs={{0,3},{1,0},{2,1},{3,2},{4,7},{5,4},{6,5},{7,6},{8,9},{9,10},{10,1... | collective-permute-start | bytes 405512 | tf_op jit(solution)/shard_map/ppermute | solution.py:249
  47.9 21.5 %collective-permute-start.3 = (bf16[16,4096]{1,0:T(8,128)(2,1)S(1)}, bf16[16,4096]{1,0:T(8,128)(2,1)S(1)}, u32[]{:S(2)}, u32[]{:S(2)}) collective-permute-start(bf16[16,4096]{1,0:T(8,128)(2,1)S(1)} %collective-permute-done.2.refs_0_), channel_id=1, source_target_pairs={{0,3},{1,0},{2,1},{3,2},{4,7},{5,4},{6,5},{7,6},{8,9},{9,10},{10,1... | collective-permute-start | bytes 393224 | tf_op jit(solution)/shard_map/ppermute | solution.py:249
  52.9 18.6 %collective-permute-start.8 = (bf16[16,4224]{1,0:T(8,128)(2,1)S(1)}, bf16[16,4224]{1,0:T(8,128)(2,1)S(1)}, u32[]{:S(2)}, u32[]{:S(2)}) collective-permute-start(bf16[16,4224]{1,0:T(8,128)(2,1)S(1)} %join_far_a.1), channel_id=1, source_target_pairs={{0,3},{1,0},{2,1},{3,2},{4,7},{5,4},{6,5},{7,6},{8,9},{9,10},{10,1... | collective-permute-start | bytes 405512 | tf_op jit(solution)/shard_map/ppermute | solution.py:249
  59.6 18.4 %collective-permute-start.10 = (bf16[16,4096]{1,0:T(8,128)(2,1)S(1)}, bf16[16,4096]{1,0:T(8,128)(2,1)S(1)}, u32[]{:S(2)}, u32[]{:S(2)}) collective-permute-start(bf16[16,4096]{1,0:T(8,128)(2,1)S(1)} %collective-permute-done.5.refs_1_), channel_id=1, source_target_pairs={{0,3},{1,0},{2,1},{3,2},{4,7},{5,4},{6,5},{7,6},{8,9},{9,10},{10,1... | collective-permute-start | bytes 393224 | tf_op jit(solution)/shard_map/ppermute | solution.py:249
  64.1 21.6 %collective-permute-start.11 = (bf16[16,4224]{1,0:T(8,128)(2,1)S(1)}, bf16[16,4224]{1,0:T(8,128)(2,1)S(1)}, u32[]{:S(2)}, u32[]{:S(2)}) collective-permute-start(bf16[16,4224]{1,0:T(8,128)(2,1)S(1)} %join_far_b.1), channel_id=1, source_target_pairs={{0,3},{1,0},{2,1},{3,2},{4,7},{5,4},{6,5},{7,6},{8,9},{9,10},{10,1... | collective-permute-start | bytes 405512 | tf_op jit(solution)/shard_map/ppermute | solution.py:249
  71.8 16.2 %collective-permute-start.9 = (bf16[16,4224]{1,0:T(8,128)(2,1)S(1)}, bf16[16,4224]{1,0:T(8,128)(2,1)S(1)}, u32[]{:S(2)}, u32[]{:S(2)}) collective-permute-start(bf16[16,4224]{1,0:T(8,128)(2,1)S(1)} %join_after_a.1), channel_id=1, source_target_pairs={{0,3},{1,0},{2,1},{3,2},{4,7},{5,4},{6,5},{7,6},{8,9},{9,10},{10,1... | collective-permute-start | bytes 405512 | tf_op jit(solution)/shard_map/ppermute | solution.py:249
  86.1 10.8 %collective-permute-start.12 = (bf16[16,4224]{1,0:T(8,128)(2,1)S(1)}, bf16[16,4224]{1,0:T(8,128)(2,1)S(1)}, u32[]{:S(2)}, u32[]{:S(2)}) collective-permute-start(bf16[16,4224]{1,0:T(8,128)(2,1)S(1)} %join_after_b.1), channel_id=1, source_target_pairs={{0,3},{1,0},{2,1},{3,2},{4,7},{5,4},{6,5},{7,6},{8,9},{9,10},{10,1... | collective-permute-start | bytes 405512 | tf_op jit(solution)/shard_map/ppermute | solution.py:249

commit v5 on v4

--- a/solution.py
+++ b/solution.py
@@ -42,7 +42,7 @@
         out_specs=VMEM,
         scratch_shapes=[pltpu.SemaphoreType.DMA],
         compiler_params=pltpu.CompilerParams(vmem_limit_bytes=16 * 1024 * 1024),
-        cost_estimate=pl.CostEstimate(flops=0, bytes_accessed=2 * value.size * 2, transcendentals=0),
+        cost_estimate=pl.CostEstimate(flops=10**11, bytes_accessed=2 * value.size * 2, transcendentals=0),
         name="load",
     )(value)
 
@@ -91,7 +91,7 @@
     out_refs = refs[len(query_counts) :]
     packet_refs = sections(out_refs[0]) if out_refs[0].shape[1] > HEADS * HEAD else out_refs
     row_count = query_refs[0].shape[0]
-    way = 2 * lax.rem(lax.div(lax.axis_index("sess"), 2), 2) - 1
+    way = 1 - 2 * lax.rem(lax.div(lax.axis_index("sess"), 2), 2)
     anchor = lax.rem(lax.axis_index("blk") + loop + distance * way, loop)
     start = length_ref[0] - QROWS + anchor * row_count
     row = lax.broadcasted_iota(jnp.int32, (row_count, BLOCK), 0)
@@ -215,13 +215,14 @@
         put_stats(out_ref, jnp.where(lane < len(heads), stats, 0.0))
 
 
-def join_part_body(own_ref, sum_ref, out_ref):
-    put_heads(out_ref, 0, join_packets((own_ref, sum_ref))[0])
-
-
-def join_home_body(done_ref, own_ref, sum_ref, out_ref):
+def join_part_body(*refs):
+    put_heads(refs[-1], 0, join_packets(refs[:-1])[0])
+
+
+def join_home_body(done_ref, *refs):
+    out_ref = refs[-1]
     out_ref[:, : done_ref.shape[1]] = done_ref[...]
-    put_heads(out_ref, done_ref.shape[1] // HEAD, join_packets((own_ref, sum_ref))[0])
+    put_heads(out_ref, done_ref.shape[1] // HEAD, join_packets(refs[:-1])[0])
 
 
 def join(body, operands, columns, name):
@@ -233,16 +234,16 @@
     return join(join_body, (*ones, *others), [one.shape[1] for one in ones], name)
 
 
-def join_home(own, sums):
-    (part,) = join(join_part_body, (own[0], sums[0]), [own[0].shape[1] - TILE], "join_part")
-    (whole,) = join(join_home_body, (part, own[1], sums[1]), [HEADS * HEAD], "join_home")
+def join_home(one, other):
+    (part,) = join(join_part_body, one, [one[0].shape[1] - TILE], "join_part")
+    (whole,) = join(join_home_body, (part, *other), [HEADS * HEAD], "join_home")
     return whole
 
 
-def onward(value):
+def onward(value, steps=1):
     sessions, loop = lax.axis_size("sess"), lax.axis_size("blk")
     pairs = [
-        (s * loop + b, s * loop + (b + (-1 if s // 2 % 2 == 0 else 1)) % loop)
+        (s * loop + b, s * loop + (b + (steps if s // 2 % 2 == 0 else -steps)) % loop)
         for s in range(sessions)
         for b in range(loop)
     ]
@@ -253,32 +254,32 @@
     loop = lax.axis_size("blk")
     scalars = (res_ids, recv_ids, lengths)
     mine = queries[0]
+    whole = mine
     mine = tuple(
         mine[:, first * GROUP * HEAD : last * GROUP * HEAD] for first, last in PARTS
     )
     arrived = half_way(mig_cache)
     res_cache = load(res_cache)
+    before = tuple(onward(part) for part in mine)
+    far = tuple(onward(part) for part in before)
+    whole, res_cache = lax.optimization_barrier((whole, res_cache))
+    after = onward(whole, -1)
     run = functools.partial(attend, loop, scalars, res_cache, arrived)
-    before = tuple(onward(part) for part in mine)
-    far_a, far_b = tuple(onward(part) for part in before)
-    first_a, first_b = tuple(onward(part) for part in run(before, -1, "attend_before"))
-    after_a = onward(far_a)
-    part_far = run((far_a, far_b), -2, "attend_far")
-    (sum_a,) = join_sums(part_far[:1], (first_a,), "join_far_a")
+    part_far = run(far, 2, "attend_far")
+    via_a, via_b = tuple(onward(part) for part in part_far)
+    *before, part_first = lax.optimization_barrier((*before, part_far[0]))
+    part_before = run(before, -1, "attend_before")
+    direct_a, direct_b = tuple(onward(part, -1) for part in part_before)
+    after, part_last = lax.optimization_barrier((after, part_before[0]))
+    part_after = run((after,), 1, "attend_after")
+    (sum_a,) = join_sums(part_after[:1], (via_a,), "join_after_a")
     second_a = onward(sum_a)
-    far_b, sum_a = lax.optimization_barrier((far_b, sum_a))
-    after_b = onward(far_b)
-    (sum_b,) = join_sums(part_far[1:], (first_b,), "join_far_b")
+    via_b, sum_a = lax.optimization_barrier((via_b, sum_a))
+    (sum_b,) = join_sums(part_after[1:], (via_b,), "join_after_b")
     second_b = onward(sum_b)
-    after_a, sum_b = lax.optimization_barrier((after_a, sum_b))
-    (sum_a,) = join_sums(run((after_a,), 1, "attend_after_a", parts=(0,)), (second_a,), "join_after_a")
-    third_a = onward(sum_a)
-    after_b, sum_a = lax.optimization_barrier((after_b, sum_a))
-    (sum_b,) = join_sums(run((after_b,), 1, "attend_after_b", parts=(1,)), (second_b,), "join_after_b")
-    third_b = onward(sum_b)
-    mine, third_a = lax.optimization_barrier((mine, third_a))
+    mine, second_a = lax.optimization_barrier((mine, second_a))
     own = run(mine, 0, "attend_own")
-    return join_home(own, (third_a, third_b))[None]
+    return join_home((own[0], direct_a, second_a), (own[1], direct_b, second_b))[None]
 
 
 def solution(mesh):

time: 98.5 us -> 95.6 us (0.971)
  the two profiles are of different devices: /device:TPU:20 before, /device:TPU:24 now
where the time goes in v5:
time: 95.6 us; the launch traced here: 94.2 us
  starting transfers between devices  63.2 us (66%)
  waiting for transfers between devices  19.6 us (21%)
  Pallas kernels  7.05 us (7%)
  local copies, waits for them, and re-layouts  2.25 us (2%)
  between operations  2.12 us (2%)
    ppermute x11, starting transfers between devices, onward(): return lax.ppermute(value, ('sess', 'blk'), pairs)  58.2 us
    ppermute x11, waiting for transfers between devices, onward(): return lax.ppermute(value, ('sess', 'blk'), pairs)  15.3 us
    pallas_call x8, Pallas kernels, call(): pl.pallas_call(body, out_shape=[jax.ShapeDtypeStruct((row_count, width),...  6.97 us
    ppermute x1, starting transfers between devices, half_way(): lax.ppermute(value, 'sess', [(s, (s + count // 2) % count) for s in range...  4.93 us
    ppermute x1, waiting for transfers between devices, half_way(): lax.ppermute(value, 'sess', [(s, (s + count // 2) % count) for s in range...  4.27 us
  transfers between devices with their start and end apart: 12, of which 5 were waited for; matrix products, arithmetic and copies ran while one was open for 0% of the time, Pallas kernels for 6%

profile of v5, /device:TPU:24, one launch (start us, length us, event | category | flops | bytes accessed | tf_op | source)
XLA Modules:
  0.0 94.2 jit_solution(9451157901849282757)
XLA Ops:
  0.0 1.0 %fusion = (bf16[16,4096]{1,0:T(8,128)(2,1)S(1)}, bf16[16,4096]{1,0:T(8,128)(2,1)S(1)}) fusion(bf16[16,8192]{1,0:T(8,128)(2,1)} %bitcast.2), kind=kLoop, calls=%fused_computation | loop fusion | bytes 524288 | tf_op jit(solution)/shard_map/slice | solution.py:259
  1.0 9.1 %collective-permute-start.3 = (bf16[16,4096]{1,0:T(8,128)(2,1)S(1)}, bf16[16,4096]{1,0:T(8,128)(2,1)S(1)}, u32[]{:S(2)}, u32[]{:S(2)}) collective-permute-start(bf16[16,4096]{1,0:T(8,128)(2,1)S(1)} %get-tuple-element.31.refs_1_), channel_id=1, source_target_pairs={{0,1},{1,2},{2,3},{3,0},{4,5},{5,6},{6,7},{7,4},{8,11},{9,8},{10,9... | collective-permute-start | bytes 393224 | tf_op jit(solution)/shard_map/ppermute | solution.py:250
  10.1 9.1 %collective-permute-start.2 = (bf16[16,4096]{1,0:T(8,128)(2,1)S(1)}, bf16[16,4096]{1,0:T(8,128)(2,1)S(1)}, u32[]{:S(2)}, u32[]{:S(2)}) collective-permute-start(bf16[16,4096]{1,0:T(8,128)(2,1)S(1)} %get-tuple-element.30.refs_0_), channel_id=1, source_target_pairs={{0,1},{1,2},{2,3},{3,0},{4,5},{5,6},{6,7},{7,4},{8,11},{9,8},{10,9... | collective-permute-start | bytes 393224 | tf_op jit(solution)/shard_map/ppermute | solution.py:250
  19.2 4.9 %collective-permute-start = (bf16[2,1,256,1024]{3,2,1,0:T(8,128)(2,1)}, bf16[2,1,256,1024]{3,2,1,0:T(8,128)(2,1)S(1)}, u32[]{:S(2)}, u32[]{:S(2)}) collective-permute-start(bf16[2,1,256,1024]{3,2,1,0:T(8,128)(2,1)} %param.8), channel_id=1, source_target_pairs={{0,256},{4,260},{8,264},{12,268},{16,272},{20,276},{24,280},{28,28... | collective-permute-start | bytes 3145736 | tf_op jit(solution)/shard_map/ppermute | solution.py:28
  24.2 4.3 %collective-permute-start.5 = (bf16[16,4096]{1,0:T(8,128)(2,1)S(1)}, bf16[16,4096]{1,0:T(8,128)(2,1)S(1)}, u32[]{:S(2)}, u32[]{:S(2)}) collective-permute-start(bf16[16,4096]{1,0:T(8,128)(2,1)S(1)} %collective-permute-done.3.refs_1_), channel_id=1, source_target_pairs={{0,1},{1,2},{2,3},{3,0},{4,5},{5,6},{6,7},{7,4},{8,11},{9,8},{10,9... | collective-permute-start | bytes 393224 | tf_op jit(solution)/shard_map/ppermute | solution.py:250
  28.5 6.6 %collective-permute-start.4 = (bf16[16,4096]{1,0:T(8,128)(2,1)S(1)}, bf16[16,4096]{1,0:T(8,128)(2,1)S(1)}, u32[]{:S(2)}, u32[]{:S(2)}) collective-permute-start(bf16[16,4096]{1,0:T(8,128)(2,1)S(1)} %collective-permute-done.2.refs_0_), channel_id=1, source_target_pairs={{0,1},{1,2},{2,3},{3,0},{4,5},{5,6},{6,7},{7,4},{8,11},{9,8},{10,9... | collective-permute-start | bytes 393224 | tf_op jit(solution)/shard_map/ppermute | solution.py:250
  35.1 1.2 %copy-done = bf16[2,1,256,1024]{3,2,1,0:T(8,128)(2,1)S(1)} copy-done((bf16[2,1,256,1024]{3,2,1,0:T(8,128)(2,1)S(1)}, bf16[2,1,256,1024]{3,2,1,0:T(8,128)(2,1)}, u32[]{:S(2)}) %copy-start) | copy-done | bytes 1048600
  36.4 3.2 %collective-permute-start.1 = (bf16[16,8192]{1,0:T(8,128)(2,1)S(1)}, bf16[16,8192]{1,0:T(8,128)(2,1)S(1)}, u32[]{:S(2)}, u32[]{:S(2)}) collective-permute-start(bf16[16,8192]{1,0:T(8,128)(2,1)S(1)} %bitcast.3), channel_id=1, source_target_pairs={{0,3},{1,0},{2,1},{3,2},{4,7},{5,4},{6,5},{7,6},{8,9},{9,10},{10,1... | collective-permute-start | bytes 786440 | tf_op jit(solution)/shard_map/ppermute | solution.py:250
  41.6 1.4 %collective-permute-done.4.refs_0_ = bf16[16,4096]{1,0:T(8,128)(2,1)S(1)} collective-permute-done((bf16[16,4096]{1,0:T(8,128)(2,1)S(1)}, bf16[16,4096]{1,0:T(8,128)(2,1)S(1)}, u32[]{:S(2)}, u32[]{:S(2)}) %collective-permute-start.4) | collective-permute-done | bytes 131104 | tf_op jit(solution)/shard_map/ppermute | solution.py:250
  42.9 4.3 %collective-permute-done.mig_ref = bf16[2,1,256,1024]{3,2,1,0:T(8,128)(2,1)S(1)} collective-permute-done((bf16[2,1,256,1024]{3,2,1,0:T(8,128)(2,1)}, bf16[2,1,256,1024]{3,2,1,0:T(8,128)(2,1)S(1)}, u32[]{:S(2)}, u32[]{:S(2)}) %collective-permute-start) | collective-permute-done | bytes 1048608 | tf_op jit(solution)/shard_map/ppermute | solution.py:28
  47.2 1.2 %attend_far.1 = (bf16[16,4224]{1,0:T(8,128)(2,1)S(1)}, bf16[16,4224]{1,0:T(8,128)(2,1)S(1)}) custom-call(s32[1,1]{1,0:T(1,128)S(6)} %copy.7.res_id_ref, s32[1,1]{1,0:T(1,128)S(6)} %copy.8.recv_id_ref, s32[1]{0:T(128)S(6)} %copy.9.length_ref, bf16[2,1,256,1024]{3,2,1,0:T(8,128)(2,1)S(1)} %load.1.res_ref, ...), custom_call_target="tpu_custom_call" | custom-call | flops 268435456 | bytes 2097152 | tf_op jit(solution)/shard_map/attend_far/pallas_call | solution.py:154
  48.4 4.3 %collective-permute-start.6 = (bf16[16,4224]{1,0:T(8,128)(2,1)S(1)}, bf16[16,4224]{1,0:T(8,128)(2,1)S(1)}, u32[]{:S(2)}, u32[]{:S(2)}) collective-permute-start(bf16[16,4224]{1,0:T(8,128)(2,1)S(1)} %get-tuple-element.24), channel_id=1, source_target_pairs={{0,1},{1,2},{2,3},{3,0},{4,5},{5,6},{6,7},{7,4},{8,11},{9,8},{10,9... | collective-permute-start | bytes 405512 | tf_op jit(solution)/shard_map/ppermute | solution.py:250
  52.7 2.2 %collective-permute-start.10 = (bf16[16,4224]{1,0:T(8,128)(2,1)S(1)}, bf16[16,4224]{1,0:T(8,128)(2,1)S(1)}, u32[]{:S(2)}, u32[]{:S(2)}) collective-permute-start(bf16[16,4224]{1,0:T(8,128)(2,1)S(1)} %get-tuple-element.37), channel_id=1, source_target_pairs={{0,1},{1,2},{2,3},{3,0},{4,5},{5,6},{6,7},{7,4},{8,11},{9,8},{10,9... | collective-permute-start | bytes 405512 | tf_op jit(solution)/shard_map/ppermute | solution.py:250
  54.9 1.2 %attend_before.1 = (bf16[16,4224]{1,0:T(8,128)(2,1)S(1)}, bf16[16,4224]{1,0:T(8,128)(2,1)S(1)}) custom-call(s32[1,1]{1,0:T(1,128)S(6)} %copy.7.res_id_ref, s32[1,1]{1,0:T(1,128)S(6)} %copy.8.recv_id_ref, s32[1]{0:T(128)S(6)} %copy.9.length_ref, bf16[2,1,256,1024]{3,2,1,0:T(8,128)(2,1)S(1)} %load.1.res_ref, ...), custom_call_target="tpu_custom_call" | custom-call | flops 268435456 | bytes 2097152 | tf_op jit(solution)/shard_map/attend_before/pallas_call | solution.py:154
  56.1 1.2 %attend_after.1 = (bf16[16,4224]{1,0:T(8,128)(2,1)S(1)}, bf16[16,4224]{1,0:T(8,128)(2,1)S(1)}) custom-call(s32[1,1]{1,0:T(1,128)S(6)} %copy.7.res_id_ref, s32[1,1]{1,0:T(1,128)S(6)} %copy.8.recv_id_ref, s32[1]{0:T(128)S(6)} %copy.9.length_ref, bf16[2,1,256,1024]{3,2,1,0:T(8,128)(2,1)S(1)} %load.1.res_ref, ...), custom_call_target="tpu_custom_call" | custom-call | flops 268435456 | bytes 2097152 | tf_op jit(solution)/shard_map/attend_after/pallas_call | solution.py:154
  57.2 4.5 %collective-permute-done.6.refs_1_ = bf16[16,4224]{1,0:T(8,128)(2,1)S(1)} collective-permute-done((bf16[16,4224]{1,0:T(8,128)(2,1)S(1)}, bf16[16,4224]{1,0:T(8,128)(2,1)S(1)}, u32[]{:S(2)}, u32[]{:S(2)}) %collective-permute-start.6) | collective-permute-done | bytes 135200 | tf_op jit(solution)/shard_map/ppermute | solution.py:250
  62.1 5.4 %collective-permute-start.7 = (bf16[16,4224]{1,0:T(8,128)(2,1)S(1)}, bf16[16,4224]{1,0:T(8,128)(2,1)S(1)}, u32[]{:S(2)}, u32[]{:S(2)}) collective-permute-start(bf16[16,4224]{1,0:T(8,128)(2,1)S(1)} %join_after_a.1), channel_id=1, source_target_pairs={{0,1},{1,2},{2,3},{3,0},{4,5},{5,6},{6,7},{7,4},{8,11},{9,8},{10,9... | collective-permute-start | bytes 405512 | tf_op jit(solution)/shard_map/ppermute | solution.py:250
  67.5 4.3 %collective-permute-start.8 = (bf16[16,4224]{1,0:T(8,128)(2,1)S(1)}, bf16[16,4224]{1,0:T(8,128)(2,1)S(1)}, u32[]{:S(2)}, u32[]{:S(2)}) collective-permute-start(bf16[16,4224]{1,0:T(8,128)(2,1)S(1)} %get-tuple-element.27), channel_id=1, source_target_pairs={{0,3},{1,0},{2,1},{3,2},{4,7},{5,4},{6,5},{7,6},{8,9},{9,10},{10,1... | collective-permute-start | bytes 405512 | tf_op jit(solution)/shard_map/ppermute | solution.py:250
  71.9 3.1 %collective-permute-start.9 = (bf16[16,4224]{1,0:T(8,128)(2,1)S(1)}, bf16[16,4224]{1,0:T(8,128)(2,1)S(1)}, u32[]{:S(2)}, u32[]{:S(2)}) collective-permute-start(bf16[16,4224]{1,0:T(8,128)(2,1)S(1)} %get-tuple-element.35), channel_id=1, source_target_pairs={{0,3},{1,0},{2,1},{3,2},{4,7},{5,4},{6,5},{7,6},{8,9},{9,10},{10,1... | collective-permute-start | bytes 405512 | tf_op jit(solution)/shard_map/ppermute | solution.py:250
  75.3 6.7 %collective-permute-start.11 = (bf16[16,4224]{1,0:T(8,128)(2,1)S(1)}, bf16[16,4224]{1,0:T(8,128)(2,1)S(1)}, u32[]{:S(2)}, u32[]{:S(2)}) collective-permute-start(bf16[16,4224]{1,0:T(8,128)(2,1)S(1)} %join_after_b.1), channel_id=1, source_target_pairs={{0,1},{1,2},{2,3},{3,0},{4,5},{5,6},{6,7},{7,4},{8,11},{9,8},{10,9... | collective-permute-start | bytes 405512 | tf_op jit(solution)/shard_map/ppermute | solution.py:250
  82.0 1.2 %attend_own.1 = (bf16[16,4224]{1,0:T(8,128)(2,1)S(1)}, bf16[16,4224]{1,0:T(8,128)(2,1)S(1)}) custom-call(s32[1,1]{1,0:T(1,128)S(6)} %copy.7.res_id_ref, s32[1,1]{1,0:T(1,128)S(6)} %copy.8.recv_id_ref, s32[1]{0:T(128)S(6)} %copy.9.length_ref, bf16[2,1,256,1024]{3,2,1,0:T(8,128)(2,1)S(1)} %load.1.res_ref, ...), custom_call_target="tpu_custom_call" | custom-call | flops 268435456 | bytes 2097152 | tf_op jit(solution)/shard_map/attend_own/pallas_call | solution.py:154
  83.6 1.4 %collective-permute-done.9.refs_1_ = bf16[16,4224]{1,0:T(8,128)(2,1)S(1)} collective-permute-done((bf16[16,4224]{1,0:T(8,128)(2,1)S(1)}, bf16[16,4224]{1,0:T(8,128)(2,1)S(1)}, u32[]{:S(2)}, u32[]{:S(2)}) %collective-permute-start.9) | collective-permute-done | bytes 135200 | tf_op jit(solution)/shard_map/ppermute | solution.py:250
  85.0 8.0 %collective-permute-done.11.refs_2_ = bf16[16,4224]{1,0:T(8,128)(2,1)S(1)} collective-permute-done((bf16[16,4224]{1,0:T(8,128)(2,1)S(1)}, bf16[16,4224]{1,0:T(8,128)(2,1)S(1)}, u32[]{:S(2)}, u32[]{:S(2)}) %collective-permute-start.11) | collective-permute-done | bytes 135200 | tf_op jit(solution)/shard_map/ppermute | solution.py:250
  93.0 1.1 %join_home.1 = bf16[16,8192]{1,0:T(8,128)(2,1)} custom-call(bf16[16,4096]{1,0:T(8,128)(2,1)S(1)} %join_part.1.done_ref, bf16[16,4224]{1,0:T(8,128)(2,1)S(1)} %get-tuple-element.34.refs_0_, bf16[16,4224]{1,0:T(8,128)(2,1)S(1)} %collective-permute-done.9.refs_1_, bf16[16,4224]{1,0:T(8,128)(2,1)S(1)} %collective-permute-done.11.refs_2_), custom_call_target="tpu_custom_call" | custom-call | flops 524288 | bytes 786432 | tf_op jit(solution)/shard_map/join_home/pallas_call | solution.py:154
  (14 shorter events, 1.2 us)
Async XLA Ops:
  0.0 36.4 %copy-start.1 = (bf16[1,16,8192]{2,1,0:T(8,128)(2,1)S(1)}, bf16[1,16,8192]{2,1,0:T(8,128)(2,1)}, u32[]{:S(2)}) copy-start(bf16[1,16,8192]{2,1,0:T(8,128)(2,1)} %param.6) | copy-start | bytes 786436
  1.0 23.2 %collective-permute-start.3 = (bf16[16,4096]{1,0:T(8,128)(2,1)S(1)}, bf16[16,4096]{1,0:T(8,128)(2,1)S(1)}, u32[]{:S(2)}, u32[]{:S(2)}) collective-permute-start(bf16[16,4096]{1,0:T(8,128)(2,1)S(1)} %get-tuple-element.31.refs_1_), channel_id=1, source_target_pairs={{0,1},{1,2},{2,3},{3,0},{4,5},{5,6},{6,7},{7,4},{8,11},{9,8},{10,9... | collective-permute-start | bytes 393224 | tf_op jit(solution)/shard_map/ppermute | solution.py:250
  10.1 18.4 %collective-permute-start.2 = (bf16[16,4096]{1,0:T(8,128)(2,1)S(1)}, bf16[16,4096]{1,0:T(8,128)(2,1)S(1)}, u32[]{:S(2)}, u32[]{:S(2)}) collective-permute-start(bf16[16,4096]{1,0:T(8,128)(2,1)S(1)} %get-tuple-element.30.refs_0_), channel_id=1, source_target_pairs={{0,1},{1,2},{2,3},{3,0},{4,5},{5,6},{6,7},{7,4},{8,11},{9,8},{10,9... | collective-permute-start | bytes 393224 | tf_op jit(solution)/shard_map/ppermute | solution.py:250
  19.2 27.9 %collective-permute-start = (bf16[2,1,256,1024]{3,2,1,0:T(8,128)(2,1)}, bf16[2,1,256,1024]{3,2,1,0:T(8,128)(2,1)S(1)}, u32[]{:S(2)}, u32[]{:S(2)}) collective-permute-start(bf16[2,1,256,1024]{3,2,1,0:T(8,128)(2,1)} %param.8), channel_id=1, source_target_pairs={{0,256},{4,260},{8,264},{12,268},{16,272},{20,276},{24,280},{28,28... | collective-permute-start | bytes 3145736 | tf_op jit(solution)/shard_map/ppermute | solution.py:28
  24.2 17.3 %collective-permute-start.5 = (bf16[16,4096]{1,0:T(8,128)(2,1)S(1)}, bf16[16,4096]{1,0:T(8,128)(2,1)S(1)}, u32[]{:S(2)}, u32[]{:S(2)}) collective-permute-start(bf16[16,4096]{1,0:T(8,128)(2,1)S(1)} %collective-permute-done.3.refs_1_), channel_id=1, source_target_pairs={{0,1},{1,2},{2,3},{3,0},{4,5},{5,6},{6,7},{7,4},{8,11},{9,8},{10,9... | collective-permute-start | bytes 393224 | tf_op jit(solution)/shard_map/ppermute | solution.py:250
  28.5 14.4 %collective-permute-start.4 = (bf16[16,4096]{1,0:T(8,128)(2,1)S(1)}, bf16[16,4096]{1,0:T(8,128)(2,1)S(1)}, u32[]{:S(2)}, u32[]{:S(2)}) collective-permute-start(bf16[16,4096]{1,0:T(8,128)(2,1)S(1)} %collective-permute-done.2.refs_0_), channel_id=1, source_target_pairs={{0,1},{1,2},{2,3},{3,0},{4,5},{5,6},{6,7},{7,4},{8,11},{9,8},{10,9... | collective-permute-start | bytes 393224 | tf_op jit(solution)/shard_map/ppermute | solution.py:250
  35.1 1.2 %copy-start = (bf16[2,1,256,1024]{3,2,1,0:T(8,128)(2,1)S(1)}, bf16[2,1,256,1024]{3,2,1,0:T(8,128)(2,1)}, u32[]{:S(2)}) copy-start(bf16[2,1,256,1024]{3,2,1,0:T(8,128)(2,1)} %in_ref.1) | copy-start | bytes 3145732
  36.4 19.6 %collective-permute-start.1 = (bf16[16,8192]{1,0:T(8,128)(2,1)S(1)}, bf16[16,8192]{1,0:T(8,128)(2,1)S(1)}, u32[]{:S(2)}, u32[]{:S(2)}) collective-permute-start(bf16[16,8192]{1,0:T(8,128)(2,1)S(1)} %bitcast.3), channel_id=1, source_target_pairs={{0,3},{1,0},{2,1},{3,2},{4,7},{5,4},{6,5},{7,6},{8,9},{9,10},{10,1... | collective-permute-start | bytes 786440 | tf_op jit(solution)/shard_map/ppermute | solution.py:250
  48.4 13.4 %collective-permute-start.6 = (bf16[16,4224]{1,0:T(8,128)(2,1)S(1)}, bf16[16,4224]{1,0:T(8,128)(2,1)S(1)}, u32[]{:S(2)}, u32[]{:S(2)}) collective-permute-start(bf16[16,4224]{1,0:T(8,128)(2,1)S(1)} %get-tuple-element.24), channel_id=1, source_target_pairs={{0,1},{1,2},{2,3},{3,0},{4,5},{5,6},{6,7},{7,4},{8,11},{9,8},{10,9... | collective-permute-start | bytes 405512 | tf_op jit(solution)/shard_map/ppermute | solution.py:250
  52.7 22.3 %collective-permute-start.10 = (bf16[16,4224]{1,0:T(8,128)(2,1)S(1)}, bf16[16,4224]{1,0:T(8,128)(2,1)S(1)}, u32[]{:S(2)}, u32[]{:S(2)}) collective-permute-start(bf16[16,4224]{1,0:T(8,128)(2,1)S(1)} %get-tuple-element.37), channel_id=1, source_target_pairs={{0,1},{1,2},{2,3},{3,0},{4,5},{5,6},{6,7},{7,4},{8,11},{9,8},{10,9... | collective-permute-start | bytes 405512 | tf_op jit(solution)/shard_map/ppermute | solution.py:250
  62.1 19.9 %collective-permute-start.7 = (bf16[16,4224]{1,0:T(8,128)(2,1)S(1)}, bf16[16,4224]{1,0:T(8,128)(2,1)S(1)}, u32[]{:S(2)}, u32[]{:S(2)}) collective-permute-start(bf16[16,4224]{1,0:T(8,128)(2,1)S(1)} %join_after_a.1), channel_id=1, source_target_pairs={{0,1},{1,2},{2,3},{3,0},{4,5},{5,6},{6,7},{7,4},{8,11},{9,8},{10,9... | collective-permute-start | bytes 405512 | tf_op jit(solution)/shard_map/ppermute | solution.py:250
  67.5 15.7 %collective-permute-start.8 = (bf16[16,4224]{1,0:T(8,128)(2,1)S(1)}, bf16[16,4224]{1,0:T(8,128)(2,1)S(1)}, u32[]{:S(2)}, u32[]{:S(2)}) collective-permute-start(bf16[16,4224]{1,0:T(8,128)(2,1)S(1)} %get-tuple-element.27), channel_id=1, source_target_pairs={{0,3},{1,0},{2,1},{3,2},{4,7},{5,4},{6,5},{7,6},{8,9},{9,10},{10,1... | collective-permute-start | bytes 405512 | tf_op jit(solution)/shard_map/ppermute | solution.py:250
  71.9 13.2 %collective-permute-start.9 = (bf16[16,4224]{1,0:T(8,128)(2,1)S(1)}, bf16[16,4224]{1,0:T(8,128)(2,1)S(1)}, u32[]{:S(2)}, u32[]{:S(2)}) collective-permute-start(bf16[16,4224]{1,0:T(8,128)(2,1)S(1)} %get-tuple-element.35), channel_id=1, source_target_pairs={{0,3},{1,0},{2,1},{3,2},{4,7},{5,4},{6,5},{7,6},{8,9},{9,10},{10,1... | collective-permute-start | bytes 405512 | tf_op jit(solution)/shard_map/ppermute | solution.py:250
  75.3 17.7 %collective-permute-start.11 = (bf16[16,4224]{1,0:T(8,128)(2,1)S(1)}, bf16[16,4224]{1,0:T(8,128)(2,1)S(1)}, u32[]{:S(2)}, u32[]{:S(2)}) collective-permute-start(bf16[16,4224]{1,0:T(8,128)(2,1)S(1)} %join_after_b.1), channel_id=1, source_target_pairs={{0,1},{1,2},{2,3},{3,0},{4,5},{5,6},{6,7},{7,4},{8,11},{9,8},{10,9... | collective-permute-start | bytes 405512 | tf_op jit(solution)/shard_map/ppermute | solution.py:250

commit v6 on v5

--- a/solution.py
+++ b/solution.py
@@ -279,7 +279,8 @@
     second_b = onward(sum_b)
     mine, second_a = lax.optimization_barrier((mine, second_a))
     own = run(mine, 0, "attend_own")
-    return join_home((own[0], direct_a, second_a), (own[1], direct_b, second_b))[None]
+    near = [join_sums(own[i : i + 1], (direct,), "join_near")[0] for i, direct in enumerate((direct_a, direct_b))]
+    return join_home((near[0], second_a), (near[1], second_b))[None]
 
 
 def solution(mesh):

time: 95.6 us -> 95.5 us (level)
    pallas_call x8 -> x10, Pallas kernels: 6.97 us -> 7.51 us  [call(): pl.pallas_call(body, out_shape=[jax.ShapeDtypeStruct((row_count, width),...]
  transfers between devices with their start and end apart: 12 -> 12, of which waited for: 5 -> 5; matrix products, arithmetic and copies ran while one was open for 0% -> 0% of each run, Pallas kernels for 6% -> 7%
where the time goes in v6:
time: 95.5 us; the launch traced here: 94.1 us
  starting transfers between devices  63.2 us (66%)
  waiting for transfers between devices  18.9 us (20%)
  Pallas kernels  7.59 us (8%)
  local copies, waits for them, and re-layouts  2.25 us (2%)
  between operations  2.13 us (2%)
    ppermute x11, starting transfers between devices, onward(): return lax.ppermute(value, ('sess', 'blk'), pairs)  58.2 us
    ppermute x11, waiting for transfers between devices, onward(): return lax.ppermute(value, ('sess', 'blk'), pairs)  14.7 us
    pallas_call x10, Pallas kernels, call(): pl.pallas_call(body, out_shape=[jax.ShapeDtypeStruct((row_count, width),...  7.51 us
    ppermute x1, starting transfers between devices, half_way(): lax.ppermute(value, 'sess', [(s, (s + count // 2) % count) for s in range...  4.93 us
    ppermute x1, waiting for transfers between devices, half_way(): lax.ppermute(value, 'sess', [(s, (s + count // 2) % count) for s in range...  4.27 us
  transfers between devices with their start and end apart: 12, of which 5 were waited for; matrix products, arithmetic and copies ran while one was open for 0% of the time, Pallas kernels for 7%

profile of v6, /device:TPU:24, one launch (start us, length us, event | category | flops | bytes accessed | tf_op | source)
XLA Modules:
  0.0 94.1 jit_solution(569073772336834786)
XLA Ops:
  0.0 1.0 %fusion = (bf16[16,4096]{1,0:T(8,128)(2,1)S(1)}, bf16[16,4096]{1,0:T(8,128)(2,1)S(1)}) fusion(bf16[16,8192]{1,0:T(8,128)(2,1)} %bitcast.2), kind=kLoop, calls=%fused_computation | loop fusion | bytes 524288 | tf_op jit(solution)/shard_map/slice | solution.py:259
  1.0 9.1 %collective-permute-start.3 = (bf16[16,4096]{1,0:T(8,128)(2,1)S(1)}, bf16[16,4096]{1,0:T(8,128)(2,1)S(1)}, u32[]{:S(2)}, u32[]{:S(2)}) collective-permute-start(bf16[16,4096]{1,0:T(8,128)(2,1)S(1)} %get-tuple-element.31.refs_1_), channel_id=1, source_target_pairs={{0,1},{1,2},{2,3},{3,0},{4,5},{5,6},{6,7},{7,4},{8,11},{9,8},{10,9... | collective-permute-start | bytes 393224 | tf_op jit(solution)/shard_map/ppermute | solution.py:250
  10.1 9.1 %collective-permute-start.2 = (bf16[16,4096]{1,0:T(8,128)(2,1)S(1)}, bf16[16,4096]{1,0:T(8,128)(2,1)S(1)}, u32[]{:S(2)}, u32[]{:S(2)}) collective-permute-start(bf16[16,4096]{1,0:T(8,128)(2,1)S(1)} %get-tuple-element.30.refs_0_), channel_id=1, source_target_pairs={{0,1},{1,2},{2,3},{3,0},{4,5},{5,6},{6,7},{7,4},{8,11},{9,8},{10,9... | collective-permute-start | bytes 393224 | tf_op jit(solution)/shard_map/ppermute | solution.py:250
  19.2 4.9 %collective-permute-start = (bf16[2,1,256,1024]{3,2,1,0:T(8,128)(2,1)}, bf16[2,1,256,1024]{3,2,1,0:T(8,128)(2,1)S(1)}, u32[]{:S(2)}, u32[]{:S(2)}) collective-permute-start(bf16[2,1,256,1024]{3,2,1,0:T(8,128)(2,1)} %param.8), channel_id=1, source_target_pairs={{0,256},{4,260},{8,264},{12,268},{16,272},{20,276},{24,280},{28,28... | collective-permute-start | bytes 3145736 | tf_op jit(solution)/shard_map/ppermute | solution.py:28
  24.2 4.3 %collective-permute-start.5 = (bf16[16,4096]{1,0:T(8,128)(2,1)S(1)}, bf16[16,4096]{1,0:T(8,128)(2,1)S(1)}, u32[]{:S(2)}, u32[]{:S(2)}) collective-permute-start(bf16[16,4096]{1,0:T(8,128)(2,1)S(1)} %collective-permute-done.3.refs_1_), channel_id=1, source_target_pairs={{0,1},{1,2},{2,3},{3,0},{4,5},{5,6},{6,7},{7,4},{8,11},{9,8},{10,9... | collective-permute-start | bytes 393224 | tf_op jit(solution)/shard_map/ppermute | solution.py:250
  28.5 6.6 %collective-permute-start.4 = (bf16[16,4096]{1,0:T(8,128)(2,1)S(1)}, bf16[16,4096]{1,0:T(8,128)(2,1)S(1)}, u32[]{:S(2)}, u32[]{:S(2)}) collective-permute-start(bf16[16,4096]{1,0:T(8,128)(2,1)S(1)} %collective-permute-done.2.refs_0_), channel_id=1, source_target_pairs={{0,1},{1,2},{2,3},{3,0},{4,5},{5,6},{6,7},{7,4},{8,11},{9,8},{10,9... | collective-permute-start | bytes 393224 | tf_op jit(solution)/shard_map/ppermute | solution.py:250
  35.1 1.2 %copy-done = bf16[2,1,256,1024]{3,2,1,0:T(8,128)(2,1)S(1)} copy-done((bf16[2,1,256,1024]{3,2,1,0:T(8,128)(2,1)S(1)}, bf16[2,1,256,1024]{3,2,1,0:T(8,128)(2,1)}, u32[]{:S(2)}) %copy-start) | copy-done | bytes 1048600
  36.4 3.2 %collective-permute-start.1 = (bf16[16,8192]{1,0:T(8,128)(2,1)S(1)}, bf16[16,8192]{1,0:T(8,128)(2,1)S(1)}, u32[]{:S(2)}, u32[]{:S(2)}) collective-permute-start(bf16[16,8192]{1,0:T(8,128)(2,1)S(1)} %bitcast.3), channel_id=1, source_target_pairs={{0,3},{1,0},{2,1},{3,2},{4,7},{5,4},{6,5},{7,6},{8,9},{9,10},{10,1... | collective-permute-start | bytes 786440 | tf_op jit(solution)/shard_map/ppermute | solution.py:250
  41.6 1.4 %collective-permute-done.4.refs_0_ = bf16[16,4096]{1,0:T(8,128)(2,1)S(1)} collective-permute-done((bf16[16,4096]{1,0:T(8,128)(2,1)S(1)}, bf16[16,4096]{1,0:T(8,128)(2,1)S(1)}, u32[]{:S(2)}, u32[]{:S(2)}) %collective-permute-start.4) | collective-permute-done | bytes 131104 | tf_op jit(solution)/shard_map/ppermute | solution.py:250
  42.9 4.3 %collective-permute-done.mig_ref = bf16[2,1,256,1024]{3,2,1,0:T(8,128)(2,1)S(1)} collective-permute-done((bf16[2,1,256,1024]{3,2,1,0:T(8,128)(2,1)}, bf16[2,1,256,1024]{3,2,1,0:T(8,128)(2,1)S(1)}, u32[]{:S(2)}, u32[]{:S(2)}) %collective-permute-start) | collective-permute-done | bytes 1048608 | tf_op jit(solution)/shard_map/ppermute | solution.py:28
  47.2 1.2 %attend_far.1 = (bf16[16,4224]{1,0:T(8,128)(2,1)S(1)}, bf16[16,4224]{1,0:T(8,128)(2,1)S(1)}) custom-call(s32[1,1]{1,0:T(1,128)S(6)} %copy.7.res_id_ref, s32[1,1]{1,0:T(1,128)S(6)} %copy.8.recv_id_ref, s32[1]{0:T(128)S(6)} %copy.9.length_ref, bf16[2,1,256,1024]{3,2,1,0:T(8,128)(2,1)S(1)} %load.1.res_ref, ...), custom_call_target="tpu_custom_call" | custom-call | flops 268435456 | bytes 2097152 | tf_op jit(solution)/shard_map/attend_far/pallas_call | solution.py:154
  48.4 4.3 %collective-permute-start.6 = (bf16[16,4224]{1,0:T(8,128)(2,1)S(1)}, bf16[16,4224]{1,0:T(8,128)(2,1)S(1)}, u32[]{:S(2)}, u32[]{:S(2)}) collective-permute-start(bf16[16,4224]{1,0:T(8,128)(2,1)S(1)} %get-tuple-element.24), channel_id=1, source_target_pairs={{0,1},{1,2},{2,3},{3,0},{4,5},{5,6},{6,7},{7,4},{8,11},{9,8},{10,9... | collective-permute-start | bytes 405512 | tf_op jit(solution)/shard_map/ppermute | solution.py:250
  52.7 2.2 %collective-permute-start.10 = (bf16[16,4224]{1,0:T(8,128)(2,1)S(1)}, bf16[16,4224]{1,0:T(8,128)(2,1)S(1)}, u32[]{:S(2)}, u32[]{:S(2)}) collective-permute-start(bf16[16,4224]{1,0:T(8,128)(2,1)S(1)} %get-tuple-element.37), channel_id=1, source_target_pairs={{0,1},{1,2},{2,3},{3,0},{4,5},{5,6},{6,7},{7,4},{8,11},{9,8},{10,9... | collective-permute-start | bytes 405512 | tf_op jit(solution)/shard_map/ppermute | solution.py:250
  54.9 1.2 %attend_before.1 = (bf16[16,4224]{1,0:T(8,128)(2,1)S(1)}, bf16[16,4224]{1,0:T(8,128)(2,1)S(1)}) custom-call(s32[1,1]{1,0:T(1,128)S(6)} %copy.7.res_id_ref, s32[1,1]{1,0:T(1,128)S(6)} %copy.8.recv_id_ref, s32[1]{0:T(128)S(6)} %copy.9.length_ref, bf16[2,1,256,1024]{3,2,1,0:T(8,128)(2,1)S(1)} %load.1.res_ref, ...), custom_call_target="tpu_custom_call" | custom-call | flops 268435456 | bytes 2097152 | tf_op jit(solution)/shard_map/attend_before/pallas_call | solution.py:154
  56.1 1.2 %attend_after.1 = (bf16[16,4224]{1,0:T(8,128)(2,1)S(1)}, bf16[16,4224]{1,0:T(8,128)(2,1)S(1)}) custom-call(s32[1,1]{1,0:T(1,128)S(6)} %copy.7.res_id_ref, s32[1,1]{1,0:T(1,128)S(6)} %copy.8.recv_id_ref, s32[1]{0:T(128)S(6)} %copy.9.length_ref, bf16[2,1,256,1024]{3,2,1,0:T(8,128)(2,1)S(1)} %load.1.res_ref, ...), custom_call_target="tpu_custom_call" | custom-call | flops 268435456 | bytes 2097152 | tf_op jit(solution)/shard_map/attend_after/pallas_call | solution.py:154
  57.2 4.5 %collective-permute-done.6.refs_1_ = bf16[16,4224]{1,0:T(8,128)(2,1)S(1)} collective-permute-done((bf16[16,4224]{1,0:T(8,128)(2,1)S(1)}, bf16[16,4224]{1,0:T(8,128)(2,1)S(1)}, u32[]{:S(2)}, u32[]{:S(2)}) %collective-permute-start.6) | collective-permute-done | bytes 135200 | tf_op jit(solution)/shard_map/ppermute | solution.py:250
  62.1 5.4 %collective-permute-start.7 = (bf16[16,4224]{1,0:T(8,128)(2,1)S(1)}, bf16[16,4224]{1,0:T(8,128)(2,1)S(1)}, u32[]{:S(2)}, u32[]{:S(2)}) collective-permute-start(bf16[16,4224]{1,0:T(8,128)(2,1)S(1)} %join_after_a.1), channel_id=1, source_target_pairs={{0,1},{1,2},{2,3},{3,0},{4,5},{5,6},{6,7},{7,4},{8,11},{9,8},{10,9... | collective-permute-start | bytes 405512 | tf_op jit(solution)/shard_map/ppermute | solution.py:250
  67.5 4.3 %collective-permute-start.8 = (bf16[16,4224]{1,0:T(8,128)(2,1)S(1)}, bf16[16,4224]{1,0:T(8,128)(2,1)S(1)}, u32[]{:S(2)}, u32[]{:S(2)}) collective-permute-start(bf16[16,4224]{1,0:T(8,128)(2,1)S(1)} %get-tuple-element.27), channel_id=1, source_target_pairs={{0,3},{1,0},{2,1},{3,2},{4,7},{5,4},{6,5},{7,6},{8,9},{9,10},{10,1... | collective-permute-start | bytes 405512 | tf_op jit(solution)/shard_map/ppermute | solution.py:250
  71.9 3.1 %collective-permute-start.9 = (bf16[16,4224]{1,0:T(8,128)(2,1)S(1)}, bf16[16,4224]{1,0:T(8,128)(2,1)S(1)}, u32[]{:S(2)}, u32[]{:S(2)}) collective-permute-start(bf16[16,4224]{1,0:T(8,128)(2,1)S(1)} %get-tuple-element.35), channel_id=1, source_target_pairs={{0,3},{1,0},{2,1},{3,2},{4,7},{5,4},{6,5},{7,6},{8,9},{9,10},{10,1... | collective-permute-start | bytes 405512 | tf_op jit(solution)/shard_map/ppermute | solution.py:250
  75.3 6.7 %collective-permute-start.11 = (bf16[16,4224]{1,0:T(8,128)(2,1)S(1)}, bf16[16,4224]{1,0:T(8,128)(2,1)S(1)}, u32[]{:S(2)}, u32[]{:S(2)}) collective-permute-start(bf16[16,4224]{1,0:T(8,128)(2,1)S(1)} %join_after_b.1), channel_id=1, source_target_pairs={{0,1},{1,2},{2,3},{3,0},{4,5},{5,6},{6,7},{7,4},{8,11},{9,8},{10,9... | collective-permute-start | bytes 405512 | tf_op jit(solution)/shard_map/ppermute | solution.py:250
  82.0 1.2 %attend_own.1 = (bf16[16,4224]{1,0:T(8,128)(2,1)S(1)}, bf16[16,4224]{1,0:T(8,128)(2,1)S(1)}) custom-call(s32[1,1]{1,0:T(1,128)S(6)} %copy.7.res_id_ref, s32[1,1]{1,0:T(1,128)S(6)} %copy.8.recv_id_ref, s32[1]{0:T(128)S(6)} %copy.9.length_ref, bf16[2,1,256,1024]{3,2,1,0:T(8,128)(2,1)S(1)} %load.1.res_ref, ...), custom_call_target="tpu_custom_call" | custom-call | flops 268435456 | bytes 2097152 | tf_op jit(solution)/shard_map/attend_own/pallas_call | solution.py:154
  83.9 1.2 %collective-permute-done.9.refs_1_ = bf16[16,4224]{1,0:T(8,128)(2,1)S(1)} collective-permute-done((bf16[16,4224]{1,0:T(8,128)(2,1)S(1)}, bf16[16,4224]{1,0:T(8,128)(2,1)S(1)}, u32[]{:S(2)}, u32[]{:S(2)}) %collective-permute-start.9) | collective-permute-done | bytes 135200 | tf_op jit(solution)/shard_map/ppermute | solution.py:250
  85.4 7.6 %collective-permute-done.11.refs_1_ = bf16[16,4224]{1,0:T(8,128)(2,1)S(1)} collective-permute-done((bf16[16,4224]{1,0:T(8,128)(2,1)S(1)}, bf16[16,4224]{1,0:T(8,128)(2,1)S(1)}, u32[]{:S(2)}, u32[]{:S(2)}) %collective-permute-start.11) | collective-permute-done | bytes 135200 | tf_op jit(solution)/shard_map/ppermute | solution.py:250
  93.0 1.0 %join_home.1 = bf16[16,8192]{1,0:T(8,128)(2,1)} custom-call(bf16[16,4096]{1,0:T(8,128)(2,1)S(1)} %join_part.1.done_ref, bf16[16,4224]{1,0:T(8,128)(2,1)S(1)} %join_near.3.refs_0_, bf16[16,4224]{1,0:T(8,128)(2,1)S(1)} %collective-permute-done.11.refs_1_), custom_call_target="tpu_custom_call" | custom-call | flops 524288 | bytes 786432 | tf_op jit(solution)/shard_map/join_home/pallas_call | solution.py:154
  (16 shorter events, 1.8 us)
Async XLA Ops:
  0.0 36.4 %copy-start.1 = (bf16[1,16,8192]{2,1,0:T(8,128)(2,1)S(1)}, bf16[1,16,8192]{2,1,0:T(8,128)(2,1)}, u32[]{:S(2)}) copy-start(bf16[1,16,8192]{2,1,0:T(8,128)(2,1)} %param.6) | copy-start | bytes 786436
  1.0 23.2 %collective-permute-start.3 = (bf16[16,4096]{1,0:T(8,128)(2,1)S(1)}, bf16[16,4096]{1,0:T(8,128)(2,1)S(1)}, u32[]{:S(2)}, u32[]{:S(2)}) collective-permute-start(bf16[16,4096]{1,0:T(8,128)(2,1)S(1)} %get-tuple-element.31.refs_1_), channel_id=1, source_target_pairs={{0,1},{1,2},{2,3},{3,0},{4,5},{5,6},{6,7},{7,4},{8,11},{9,8},{10,9... | collective-permute-start | bytes 393224 | tf_op jit(solution)/shard_map/ppermute | solution.py:250
  10.1 18.4 %collective-permute-start.2 = (bf16[16,4096]{1,0:T(8,128)(2,1)S(1)}, bf16[16,4096]{1,0:T(8,128)(2,1)S(1)}, u32[]{:S(2)}, u32[]{:S(2)}) collective-permute-start(bf16[16,4096]{1,0:T(8,128)(2,1)S(1)} %get-tuple-element.30.refs_0_), channel_id=1, source_target_pairs={{0,1},{1,2},{2,3},{3,0},{4,5},{5,6},{6,7},{7,4},{8,11},{9,8},{10,9... | collective-permute-start | bytes 393224 | tf_op jit(solution)/shard_map/ppermute | solution.py:250
  19.2 27.9 %collective-permute-start = (bf16[2,1,256,1024]{3,2,1,0:T(8,128)(2,1)}, bf16[2,1,256,1024]{3,2,1,0:T(8,128)(2,1)S(1)}, u32[]{:S(2)}, u32[]{:S(2)}) collective-permute-start(bf16[2,1,256,1024]{3,2,1,0:T(8,128)(2,1)} %param.8), channel_id=1, source_target_pairs={{0,256},{4,260},{8,264},{12,268},{16,272},{20,276},{24,280},{28,28... | collective-permute-start | bytes 3145736 | tf_op jit(solution)/shard_map/ppermute | solution.py:28
  24.2 17.3 %collective-permute-start.5 = (bf16[16,4096]{1,0:T(8,128)(2,1)S(1)}, bf16[16,4096]{1,0:T(8,128)(2,1)S(1)}, u32[]{:S(2)}, u32[]{:S(2)}) collective-permute-start(bf16[16,4096]{1,0:T(8,128)(2,1)S(1)} %collective-permute-done.3.refs_1_), channel_id=1, source_target_pairs={{0,1},{1,2},{2,3},{3,0},{4,5},{5,6},{6,7},{7,4},{8,11},{9,8},{10,9... | collective-permute-start | bytes 393224 | tf_op jit(solution)/shard_map/ppermute | solution.py:250
  28.5 14.4 %collective-permute-start.4 = (bf16[16,4096]{1,0:T(8,128)(2,1)S(1)}, bf16[16,4096]{1,0:T(8,128)(2,1)S(1)}, u32[]{:S(2)}, u32[]{:S(2)}) collective-permute-start(bf16[16,4096]{1,0:T(8,128)(2,1)S(1)} %collective-permute-done.2.refs_0_), channel_id=1, source_target_pairs={{0,1},{1,2},{2,3},{3,0},{4,5},{5,6},{6,7},{7,4},{8,11},{9,8},{10,9... | collective-permute-start | bytes 393224 | tf_op jit(solution)/shard_map/ppermute | solution.py:250
  35.1 1.2 %copy-start = (bf16[2,1,256,1024]{3,2,1,0:T(8,128)(2,1)S(1)}, bf16[2,1,256,1024]{3,2,1,0:T(8,128)(2,1)}, u32[]{:S(2)}) copy-start(bf16[2,1,256,1024]{3,2,1,0:T(8,128)(2,1)} %in_ref.1) | copy-start | bytes 3145732
  36.4 19.6 %collective-permute-start.1 = (bf16[16,8192]{1,0:T(8,128)(2,1)S(1)}, bf16[16,8192]{1,0:T(8,128)(2,1)S(1)}, u32[]{:S(2)}, u32[]{:S(2)}) collective-permute-start(bf16[16,8192]{1,0:T(8,128)(2,1)S(1)} %bitcast.3), channel_id=1, source_target_pairs={{0,3},{1,0},{2,1},{3,2},{4,7},{5,4},{6,5},{7,6},{8,9},{9,10},{10,1... | collective-permute-start | bytes 786440 | tf_op jit(solution)/shard_map/ppermute | solution.py:250
  48.4 13.4 %collective-permute-start.6 = (bf16[16,4224]{1,0:T(8,128)(2,1)S(1)}, bf16[16,4224]{1,0:T(8,128)(2,1)S(1)}, u32[]{:S(2)}, u32[]{:S(2)}) collective-permute-start(bf16[16,4224]{1,0:T(8,128)(2,1)S(1)} %get-tuple-element.24), channel_id=1, source_target_pairs={{0,1},{1,2},{2,3},{3,0},{4,5},{5,6},{6,7},{7,4},{8,11},{9,8},{10,9... | collective-permute-start | bytes 405512 | tf_op jit(solution)/shard_map/ppermute | solution.py:250
  52.7 22.3 %collective-permute-start.10 = (bf16[16,4224]{1,0:T(8,128)(2,1)S(1)}, bf16[16,4224]{1,0:T(8,128)(2,1)S(1)}, u32[]{:S(2)}, u32[]{:S(2)}) collective-permute-start(bf16[16,4224]{1,0:T(8,128)(2,1)S(1)} %get-tuple-element.37), channel_id=1, source_target_pairs={{0,1},{1,2},{2,3},{3,0},{4,5},{5,6},{6,7},{7,4},{8,11},{9,8},{10,9... | collective-permute-start | bytes 405512 | tf_op jit(solution)/shard_map/ppermute | solution.py:250
  62.1 19.9 %collective-permute-start.7 = (bf16[16,4224]{1,0:T(8,128)(2,1)S(1)}, bf16[16,4224]{1,0:T(8,128)(2,1)S(1)}, u32[]{:S(2)}, u32[]{:S(2)}) collective-permute-start(bf16[16,4224]{1,0:T(8,128)(2,1)S(1)} %join_after_a.1), channel_id=1, source_target_pairs={{0,1},{1,2},{2,3},{3,0},{4,5},{5,6},{6,7},{7,4},{8,11},{9,8},{10,9... | collective-permute-start | bytes 405512 | tf_op jit(solution)/shard_map/ppermute | solution.py:250
  67.5 15.7 %collective-permute-start.8 = (bf16[16,4224]{1,0:T(8,128)(2,1)S(1)}, bf16[16,4224]{1,0:T(8,128)(2,1)S(1)}, u32[]{:S(2)}, u32[]{:S(2)}) collective-permute-start(bf16[16,4224]{1,0:T(8,128)(2,1)S(1)} %get-tuple-element.27), channel_id=1, source_target_pairs={{0,3},{1,0},{2,1},{3,2},{4,7},{5,4},{6,5},{7,6},{8,9},{9,10},{10,1... | collective-permute-start | bytes 405512 | tf_op jit(solution)/shard_map/ppermute | solution.py:250
  71.9 13.2 %collective-permute-start.9 = (bf16[16,4224]{1,0:T(8,128)(2,1)S(1)}, bf16[16,4224]{1,0:T(8,128)(2,1)S(1)}, u32[]{:S(2)}, u32[]{:S(2)}) collective-permute-start(bf16[16,4224]{1,0:T(8,128)(2,1)S(1)} %get-tuple-element.35), channel_id=1, source_target_pairs={{0,3},{1,0},{2,1},{3,2},{4,7},{5,4},{6,5},{7,6},{8,9},{9,10},{10,1... | collective-permute-start | bytes 405512 | tf_op jit(solution)/shard_map/ppermute | solution.py:250
  75.3 17.7 %collective-permute-start.11 = (bf16[16,4224]{1,0:T(8,128)(2,1)S(1)}, bf16[16,4224]{1,0:T(8,128)(2,1)S(1)}, u32[]{:S(2)}, u32[]{:S(2)}) collective-permute-start(bf16[16,4224]{1,0:T(8,128)(2,1)S(1)} %join_after_b.1), channel_id=1, source_target_pairs={{0,1},{1,2},{2,3},{3,0},{4,5},{5,6},{6,7},{7,4},{8,11},{9,8},{10,9... | collective-permute-start | bytes 405512 | tf_op jit(solution)/shard_map/ppermute | solution.py:250
